TPU v7x, 32 devices: a whole 2x2x4 slice. The times are simulated.
32 devices in a mesh: seq: 16 (over z, x, core), head: 2 (over y).
Axes of the slice: x: 2, y: 2, z: 4, core: 2. Of those that a mesh axis runs over, the one named last changes fastest.
Arguments:
- tokens: bfloat16 [2, 1024, 1536], P(None, 'seq'), may hold values from -6 to 6
- w_query: bfloat16 [1536, 1536], P('seq', 'head'), may hold values from -0.15625 to 0.15625
- w_key: bfloat16 [1536, 1536], P('seq', 'head'), may hold values from -0.15625 to 0.15625
- w_value: bfloat16 [1536, 1536], P('seq', 'head'), may hold values from -0.15625 to 0.15625
- w_house: bfloat16 [1536, 1536], P('seq', 'head'), may hold values from -0.15625 to 0.15625
- w_beta: bfloat16 [1536, 12], P('seq', 'head'), may hold values from -0.15625 to 0.15625
- beta_bias: float32 [12], P('head'), may hold values from -4 to 4
- w_out: bfloat16 [1536, 1536], P('head', 'seq'), may hold values from -0.625 to 0.625
- w_gate: bfloat16 [1536, 4096], P('seq', 'head'), may hold values from -0.15625 to 0.15625
- w_up: bfloat16 [1536, 4096], P('seq', 'head'), may hold values from -0.15625 to 0.15625
- w_down: bfloat16 [4096, 1536], P('head', 'seq'), may hold values from -0.09375 to 0.09375
- gain_attn: float32 [1536], replicated, may hold values from 0.5 to 1.5
- gain_mlp: float32 [1536], replicated, may hold values from 0.5 to 1.5
- segment_ids: int32 [2, 1024], P(None, 'seq'), may hold values from 0 to 3, as said below
- out_grad: bfloat16 [2, 1024, 1536], P(None, 'seq'), may hold values from -6 to 6
Outputs:
- block_out: bfloat16 [2, 1024, 1536], P(None, 'seq')
- tokens_grad: float32 [2, 1024, 1536], P(None, 'seq')
- query_grad: float32 [1536, 1536], P('seq', 'head')
- key_grad: float32 [1536, 1536], P('seq', 'head')
- value_grad: float32 [1536, 1536], P('seq', 'head')
- house_grad: float32 [1536, 1536], P('seq', 'head')
- beta_grad: float32 [1536, 12], P('seq', 'head')
- bias_grad: float32 [12], P('head')
- out_weight_grad: float32 [1536, 1536], P('head', 'seq')
- gate_grad: float32 [1536, 4096], P('seq', 'head')
- up_grad: float32 [1536, 4096], P('seq', 'head')
- down_grad: float32 [4096, 1536], P('head', 'seq')
- attn_gain_grad: float32 [1536], replicated
- mlp_gain_grad: float32 [1536], replicated
Inputs may be any that keep to these rules, and one draw needn't show every extreme that they name: `segment_ids`: along each micro-batch the ids start at 0 and rise by one at each new sequence; the first rise lies within the first 64 positions and the last within the last 64; one micro-batch, drawn from the seed, holds three sequences, the others four.
All inputs are finite; a program needn't handle non-finite values.
Results may differ from a plain program's by a relative error of at most 0.012.
The roundings to bfloat16 on the way count: a program that leaves them out, or rounds other values in their place, can miss the bound.
Values may be sent and summed in bfloat16 or wider, within the bound.
No kernel may reach another device: no remote copies, remote signals or barrier semaphores. Data moves between devices by JAX's collectives and lax.ppermute only.
A program may use at most 192 MiB of HBM per device.

v0:
```python
import jax
import jax.numpy as jnp
from jax import lax
from jax.sharding import PartitionSpec as P

highest = lax.Precision.HIGHEST
epsilon = 1e-06
masked_score = -1e30


def passed_along(value, axis, steps):
    count = lax.axis_size(axis)
    leading, last = (max(0, -steps), min(count, count - steps))
    return lax.ppermute(value, axis, [(source, source + steps) for source in range(leading, last)])


def normalize(values):
    return values * lax.rsqrt(jnp.mean(values * values, axis=-1, keepdims=True) + epsilon)


def norm_back(cotangent, normed, values):
    scaled = lax.rsqrt(jnp.mean(values * values, axis=-1, keepdims=True) + epsilon)
    return scaled * (cotangent - normed * jnp.mean(cotangent * normed, axis=-1, keepdims=True))


def block_factors(house_raw, beta_logit):
    mirror = house_raw * lax.rsqrt(jnp.sum(house_raw * house_raw, axis=-1, keepdims=True) + epsilon)
    strength = 2.0 * jax.nn.sigmoid(beta_logit)
    length = mirror.shape[-2]
    inner_dots = jnp.einsum("...td,...sd->...ts", mirror, mirror, precision=highest)
    strict_lower = jnp.tril(jnp.ones((length, length), jnp.float32), -1)
    system = jnp.eye(length, dtype=jnp.float32) + strength[..., :, None] * inner_dots * strict_lower
    diagonal = jnp.eye(length, dtype=jnp.float32) * strength[..., None, :]
    triang = jax.scipy.linalg.solve_triangular(system, diagonal, lower=True, unit_diagonal=True)
    return (mirror, triang)


def local_terms(queries, key_vecs, mirror, triang):
    length = queries.shape[-2]
    lower_incl = jnp.tril(jnp.ones((length, length), jnp.float32))
    query_dots = jnp.einsum("...id,...td->...it", queries, mirror, precision=highest) * lower_incl
    key_dots = jnp.einsum("...jd,...td->...jt", key_vecs, mirror, precision=highest) * (
        1.0 - lower_incl
    )
    query_mix = jnp.einsum("...it,...ts->...is", query_dots, triang, precision=highest)
    moved_query = queries - jnp.einsum("...is,...sd->...id", query_mix, mirror, precision=highest)
    key_mix = jnp.einsum("...js,...ts->...jt", key_dots, triang, precision=highest)
    moved_key = key_vecs - jnp.einsum("...jt,...td->...jd", key_mix, mirror, precision=highest)
    logits = jnp.einsum("...id,...jd->...ij", queries, key_vecs, precision=highest)
    logits = logits - jnp.einsum("...is,...js->...ij", query_mix, key_dots, precision=highest)
    return (moved_query, moved_key, logits)


def local_all(queries, key_vecs, house_raw, beta_logit):
    mirror, triang = block_factors(house_raw, beta_logit)
    moved_query, moved_key, logits = local_terms(queries, key_vecs, mirror, triang)
    return (moved_query, moved_key, logits, mirror, triang)


def transform(keys_in, mirror, triang):
    key_dots = jnp.einsum("...jd,...sd->...js", keys_in, mirror, precision=highest)
    key_mix = jnp.einsum("...js,...ts->...jt", key_dots, triang, precision=highest)
    return keys_in - jnp.einsum("...jt,...td->...jd", key_mix, mirror, precision=highest)


def absorb(running, moved_query, keys_in, values_in, labels_in, labels, score_scale):
    old_max, old_sum, old_out = running
    logits = jnp.einsum("mhid,mhjd->mhij", moved_query, keys_in, precision=highest) * score_scale
    allowed = labels[:, None, :, None] == labels_in[:, None, None, :]
    logits = jnp.where(allowed, logits, masked_score)
    new_max = jnp.maximum(old_max, jnp.max(logits, axis=-1))
    factor = jnp.exp(old_max - new_max)
    weights = jnp.exp(logits - new_max[..., None])
    new_sum = old_sum * factor + jnp.sum(weights, axis=-1)
    new_out = old_out * factor[..., None] + jnp.einsum(
        "mhij,mhjd->mhid", weights, values_in, precision=highest
    )
    return (new_max, new_sum, new_out)


def block_grads(logits, allowed, log_total, attn_grad, row_delta, values_in, score_scale):
    attn_probs = jnp.where(allowed, jnp.exp(logits * score_scale - log_total[..., None]), 0.0)
    value_part = jnp.einsum("mhij,mhid->mhjd", attn_probs, attn_grad, precision=highest)
    prob_grad = jnp.einsum("mhid,mhjd->mhij", attn_grad, values_in, precision=highest)
    score_grad = attn_probs * (prob_grad - row_delta[..., None]) * score_scale
    return (score_grad, value_part)


def split_heads(row_values, batches, positions, head_count):
    return row_values.reshape(batches, positions, head_count, -1).transpose(0, 2, 1, 3)


def join_heads(blocks):
    batches, head_count, positions, head_dim = blocks.shape
    return blocks.transpose(0, 2, 1, 3).reshape(batches * positions, head_count * head_dim)


def local(
    tokens,
    w_query,
    w_key,
    w_value,
    w_house,
    w_beta,
    beta_bias,
    w_out,
    w_gate,
    w_up,
    w_down,
    gain_attn,
    gain_mlp,
    segment_ids,
    out_grad,
):
    batches, positions, model_width = tokens.shape
    row_count = batches * positions
    seq_devices = lax.axis_size("seq")
    gathered = (
        lax.all_gather(w_query, "seq", axis=0, tiled=True),
        lax.all_gather(w_key, "seq", axis=0, tiled=True),
        lax.all_gather(w_value, "seq", axis=0, tiled=True),
        lax.all_gather(w_house, "seq", axis=0, tiled=True),
        lax.all_gather(w_beta, "seq", axis=0, tiled=True),
        lax.all_gather(w_out, "seq", axis=1, tiled=True),
        lax.all_gather(w_gate, "seq", axis=0, tiled=True),
        lax.all_gather(w_up, "seq", axis=0, tiled=True),
        lax.all_gather(w_down, "seq", axis=1, tiled=True),
    )
    (
        query_full,
        key_full,
        value_full,
        house_full,
        beta_full,
        out_full,
        gate_full,
        up_full,
        down_full,
    ) = gathered
    head_count = beta_full.shape[1]
    head_dim = query_full.shape[1] // head_count
    score_scale = head_dim ** (-0.5)
    inputs = tokens.astype(jnp.float32).reshape(row_count, model_width)
    normed_one = normalize(inputs)
    attn_in = (normed_one * gain_attn).astype(jnp.bfloat16)

    def project_heads(weight):
        return split_heads(
            jnp.dot(attn_in, weight, preferred_element_type=jnp.float32),
            batches,
            positions,
            head_count,
        )

    queries = project_heads(query_full)
    key_vecs = project_heads(key_full)
    value_vecs = project_heads(value_full)
    house_raw = project_heads(house_full)
    beta_logit = (
        (jnp.dot(attn_in, beta_full, preferred_element_type=jnp.float32) + beta_bias)
        .reshape(batches, positions, head_count)
        .transpose(0, 2, 1)
    )
    labels = (segment_ids + 1).astype(jnp.float32)
    moved_query, moved_key, logits, mirror, triang = local_all(
        queries, key_vecs, house_raw, beta_logit
    )
    causal = jnp.tril(jnp.ones((positions, positions), jnp.bool_))
    own_allowed = (causal[None] & (labels[:, :, None] == labels[:, None, :]))[:, None]
    own_logits = jnp.where(own_allowed, logits * score_scale, masked_score)
    start_max = jnp.max(own_logits, axis=-1)
    own_weights = jnp.exp(own_logits - start_max[..., None])
    running = (
        start_max,
        jnp.sum(own_weights, axis=-1),
        jnp.einsum("mhij,mhjd->mhid", own_weights, value_vecs, precision=highest),
    )
    distances = jnp.arange(1, seq_devices, dtype=jnp.int32)

    def forward_turn(carried, distance):
        state, keys_out, values_out, labels_out = carried
        keys_in, values_in, labels_in = passed_along((keys_out, values_out, labels_out), "seq", 1)
        state = absorb(state, moved_query, keys_in, values_in, labels_in, labels, score_scale)
        return (
            (state, transform(keys_in, mirror, triang), values_in, labels_in),
            (keys_in, values_in, labels_in),
        )

    final_state, kept = lax.scan(forward_turn, (running, moved_key, value_vecs, labels), distances)
    running = final_state[0]
    kept_keys, kept_values, kept_labels = kept
    final_max, final_sum, final_out = running
    attended = final_out / final_sum[..., None]
    log_total = final_max + jnp.log(final_sum)
    attended_low = join_heads(attended).astype(jnp.bfloat16)
    attn_branch = lax.psum(
        jnp.dot(attended_low, out_full, preferred_element_type=jnp.float32), "head"
    )
    middle = inputs + attn_branch
    normed_two = normalize(middle)
    mlp_in = (normed_two * gain_mlp).astype(jnp.bfloat16)
    gate_proj = jnp.dot(mlp_in, gate_full, preferred_element_type=jnp.float32)
    up_proj = jnp.dot(mlp_in, up_full, preferred_element_type=jnp.float32)
    hidden = (jax.nn.silu(gate_proj) * up_proj).astype(jnp.bfloat16)
    mlp_branch = lax.psum(
        jnp.dot(hidden, down_full, preferred_element_type=jnp.float32).astype(jnp.bfloat16), "head"
    ).astype(jnp.float32)
    block_out = (middle + mlp_branch).astype(jnp.bfloat16).reshape(batches, positions, model_width)
    branch_grad = out_grad.reshape(row_count, model_width)
    down_grad = jnp.dot(hidden.T, branch_grad, preferred_element_type=jnp.float32)
    hidden_grad = jnp.dot(branch_grad, down_full.T, preferred_element_type=jnp.float32)
    sigmoid_gate = jax.nn.sigmoid(gate_proj)
    gate_rows = (
        hidden_grad * up_proj * sigmoid_gate * (1.0 + gate_proj * (1.0 - sigmoid_gate))
    ).astype(jnp.bfloat16)
    up_rows = (hidden_grad * jax.nn.silu(gate_proj)).astype(jnp.bfloat16)
    gate_grad = jnp.dot(mlp_in.T, gate_rows, preferred_element_type=jnp.float32)
    up_grad = jnp.dot(mlp_in.T, up_rows, preferred_element_type=jnp.float32)
    mlp_in_part = jnp.dot(gate_rows, gate_full.T, preferred_element_type=jnp.float32) + jnp.dot(
        up_rows, up_full.T, preferred_element_type=jnp.float32
    )
    mlp_in_grad = lax.psum(mlp_in_part, "head")
    mlp_gain_part = jnp.sum(mlp_in_grad * normed_two, axis=0)
    middle_grad = out_grad.astype(jnp.float32).reshape(row_count, model_width) + norm_back(
        mlp_in_grad * gain_mlp, normed_two, middle
    )
    branch_low = middle_grad.astype(jnp.bfloat16)
    out_weight_grad = jnp.dot(attended_low.T, branch_low, preferred_element_type=jnp.float32)
    attn_grad = split_heads(
        jnp.dot(branch_low, out_full.T, preferred_element_type=jnp.float32),
        batches,
        positions,
        head_count,
    )
    row_delta = jnp.sum(attn_grad * attended, axis=-1)
    own_grad, own_values = block_grads(
        logits, own_allowed, log_total, attn_grad, row_delta, value_vecs, score_scale
    )

    def cross_grads(keys_in, values_in, labels_in, key_grad_in):
        cross_logits = jnp.einsum("mhid,mhjd->mhij", moved_query, keys_in, precision=highest)
        allowed = labels[:, None, :, None] == labels_in[:, None, None, :]
        score_grad, value_part = block_grads(
            cross_logits, allowed, log_total, attn_grad, row_delta, values_in, score_scale
        )
        query_part = jnp.einsum("mhij,mhjd->mhid", score_grad, keys_in, precision=highest)
        key_part = jnp.einsum("mhij,mhid->mhjd", score_grad, moved_query, precision=highest)
        pullback = jax.vjp(transform, keys_in, mirror, triang)[1]
        back_key, mirror_part, triang_part = pullback(key_grad_in)
        return (query_part, key_part + back_key, value_part, mirror_part, triang_part)

    turns = jnp.arange(seq_devices - 1, dtype=jnp.int32)

    def backward_turn(carried, turn_index):
        key_grad_in, value_grad_in, query_acc, mirror_acc, triang_acc = carried
        slot_index = seq_devices - 2 - turn_index
        keys_in = lax.dynamic_index_in_dim(kept_keys, slot_index, 0, keepdims=False)
        values_in = lax.dynamic_index_in_dim(kept_values, slot_index, 0, keepdims=False)
        labels_in = lax.dynamic_index_in_dim(kept_labels, slot_index, 0, keepdims=False)
        query_part, key_grad_out, value_part, mirror_part, triang_part = cross_grads(
            keys_in, values_in, labels_in, key_grad_in
        )
        passed = passed_along((key_grad_out, value_part + value_grad_in), "seq", -1)
        return (
            (
                passed[0],
                passed[1],
                query_acc + query_part,
                mirror_acc + mirror_part,
                triang_acc + triang_part,
            ),
            None,
        )

    start_state = (
        jnp.zeros_like(moved_key),
        jnp.zeros_like(value_vecs),
        jnp.zeros_like(moved_query),
        jnp.zeros_like(mirror),
        jnp.zeros_like(triang),
    )
    final_grads = lax.scan(backward_turn, start_state, turns)[0]
    own_key_grad, carried_values, query_acc, mirror_acc, triang_acc = final_grads
    value_total = own_values + carried_values
    local_pull = jax.vjp(local_all, queries, key_vecs, house_raw, beta_logit)[1]
    query_back, key_back, house_back, logit_back = local_pull(
        (query_acc, own_key_grad, own_grad, mirror_acc, triang_acc)
    )
    query_rows = join_heads(query_back).astype(jnp.bfloat16)
    key_rows = join_heads(key_back).astype(jnp.bfloat16)
    value_rows = join_heads(value_total).astype(jnp.bfloat16)
    house_rows = join_heads(house_back).astype(jnp.bfloat16)
    logit_rows = logit_back.transpose(0, 2, 1).reshape(row_count, head_count).astype(jnp.bfloat16)
    query_grad = jnp.dot(attn_in.T, query_rows, preferred_element_type=jnp.float32)
    key_grad = jnp.dot(attn_in.T, key_rows, preferred_element_type=jnp.float32)
    value_grad = jnp.dot(attn_in.T, value_rows, preferred_element_type=jnp.float32)
    house_grad = jnp.dot(attn_in.T, house_rows, preferred_element_type=jnp.float32)
    beta_grad = jnp.dot(attn_in.T, logit_rows, preferred_element_type=jnp.float32)
    bias_part = jnp.sum(logit_rows.astype(jnp.float32), axis=0)
    attn_in_part = jnp.dot(query_rows, query_full.T, preferred_element_type=jnp.float32)
    attn_in_part = attn_in_part + jnp.dot(key_rows, key_full.T, preferred_element_type=jnp.float32)
    attn_in_part = attn_in_part + jnp.dot(
        value_rows, value_full.T, preferred_element_type=jnp.float32
    )
    attn_in_part = attn_in_part + jnp.dot(
        house_rows, house_full.T, preferred_element_type=jnp.float32
    )
    attn_in_part = attn_in_part + jnp.dot(
        logit_rows, beta_full.T, preferred_element_type=jnp.float32
    )
    attn_in_grad = lax.psum(attn_in_part.astype(jnp.bfloat16), "head").astype(jnp.float32)
    attn_gain_part = jnp.sum(attn_in_grad * normed_one, axis=0)
    tokens_grad = (middle_grad + norm_back(attn_in_grad * gain_attn, normed_one, inputs)).reshape(
        batches, positions, model_width
    )
    scattered = (
        lax.psum_scatter(query_grad, "seq", scatter_dimension=0, tiled=True),
        lax.psum_scatter(key_grad, "seq", scatter_dimension=0, tiled=True),
        lax.psum_scatter(value_grad, "seq", scatter_dimension=0, tiled=True),
        lax.psum_scatter(house_grad, "seq", scatter_dimension=0, tiled=True),
        lax.psum_scatter(beta_grad, "seq", scatter_dimension=0, tiled=True),
        lax.psum_scatter(out_weight_grad, "seq", scatter_dimension=1, tiled=True),
        lax.psum_scatter(gate_grad, "seq", scatter_dimension=0, tiled=True),
        lax.psum_scatter(up_grad, "seq", scatter_dimension=0, tiled=True),
        lax.psum_scatter(down_grad, "seq", scatter_dimension=1, tiled=True),
    )
    small_sums = lax.psum((attn_gain_part, mlp_gain_part, bias_part), "seq")
    return (
        block_out,
        tokens_grad,
        scattered[0],
        scattered[1],
        scattered[2],
        scattered[3],
        scattered[4],
        small_sums[2],
        scattered[5],
        scattered[6],
        scattered[7],
        scattered[8],
        small_sums[0],
        small_sums[1],
    )


def solution(mesh):
    placed = (
        P(None, "seq", None),
        P("seq", "head"),
        P("seq", "head"),
        P("seq", "head"),
        P("seq", "head"),
        P("seq", "head"),
        P("head"),
        P("head", "seq"),
        P("seq", "head"),
        P("seq", "head"),
        P("head", "seq"),
        P(),
        P(),
        P(None, "seq"),
        P(None, "seq", None),
    )
    return jax.shard_map(
        local,
        mesh=mesh,
        in_specs=placed,
        out_specs=(
            P(None, "seq", None),
            P(None, "seq", None),
            P("seq", "head"),
            P("seq", "head"),
            P("seq", "head"),
            P("seq", "head"),
            P("seq", "head"),
            P("head"),
            P("head", "seq"),
            P("seq", "head"),
            P("seq", "head"),
            P("head", "seq"),
            P(),
            P(),
        ),
        check_vma=False,
    )
```

profile of v0, /device:TPU:21, one launch (start us, length us, event | category | flops | bytes accessed | tf_op | source)
XLA Modules:
  0.0 2217.6 jit_solution(284317868854431845)
XLA Ops:
  16.6 16.8 all-gather
  34.5 18.2 all-gather.10.cloned.1.call-done
  57.1 39.1 %all-gather.12.cloned.1.call-done = bf16[1536,768]{1,0:T(8,128)(2,1)} async-done(((bf16[96,768]{1,0:T(8,128)(2,1)}), bf16[1536,768]{1,0:T(8,128)(2,1)}) %all-gather.12.cloned.1.call-update) | async-done | bytes 2359312 | tf_op jit(solution)/shard_map/all_gather | solution.py:120
  105.7 33.9 %all-gather.14.cloned.1.call-done = bf16[1536,768]{1,0:T(8,128)(2,1)} async-done(((bf16[96,768]{1,0:T(8,128)(2,1)}), bf16[1536,768]{1,0:T(8,128)(2,1)}) %all-gather.14.cloned.1.call-update) | async-done | bytes 2359312 | tf_op jit(solution)/shard_map/all_gather | solution.py:122
  150.0 59.0 %custom-call.10 = f32[2,6,1,64,64]{3,4,2,1,0:T(8,128)S(1)} custom-call(f32[2,6,1,64,64]{4,3,2,1,0:T(8,128)S(1)} %add_bitcast_fusion), custom_call_target="InvertDiagBlocksLowerTriangular" | custom-call | tf_op jit(solution)/shard_map/jit(_solve_triangular)/vmap(vmap())/triangular_solve/custom-call.1 | solution.py:34
  226.2 305.2 %while.47 = (s32[]{:T(128)}, f32[2,6,64]{2,1,0:T(8,128)S(1)}, f32[2,6,64]{2,1,0:T(8,128)}, f32[2,6,64,128]{3,2,1,0:T(8,128)S(1)}, f32[2,6,64,128]{3,2,1,0:T(8,12...) while((s32[]{:T(128)}, f32[2,6,64]{2,1,0:T(8,128)S(1)}, ...), condition=%wide.region_7.9_spmd, body=%wide.region_4.8_spmd.sunk | while | flops 340436480 | bytes 11098393 | solution.py:189
  372.6 5.1 collective-permute-start.2
  413.2 5.1 collective-permute-start.2
  538.5 31.1 %all-reduce.6.cloned.1.call-done = f32[128,1536]{1,0:T(8,128)} async-done(((f32[128,1536]{1,0:T(8,128)}), f32[128,1536]{1,0:T(8,128)}) %all-reduce.6.cloned.1.call-update) | async-done | bytes 786448 | tf_op jit(solution)/shard_map/psum | solution.py:196
  572.3 62.5 %all-gather.20.cloned.1.call-done = bf16[1536,2048]{1,0:T(8,128)(2,1)} async-done(((bf16[96,2048]{1,0:T(8,128)(2,1)}), bf16[1536,2048]{1,0:T(8,128)(2,1)}) %all-gather.20.cloned.1.call-update) | async-done | bytes 6291472 | tf_op jit(solution)/shard_map/all_gather | solution.py:125
  639.6 58.3 %all-gather.22.cloned.1.call-done = bf16[1536,2048]{1,0:T(8,128)(2,1)} async-done(((bf16[96,2048]{1,0:T(8,128)(2,1)}), bf16[1536,2048]{1,0:T(8,128)(2,1)}) %all-gather.22.cloned.1.call-update) | async-done | bytes 6291472 | tf_op jit(solution)/shard_map/all_gather | solution.py:126
  702.6 58.3 %all-gather.24.cloned.1.call-done = bf16[2048,1536]{0,1:T(8,128)(2,1)} async-done(((bf16[2048,96]{0,1:T(8,128)(2,1)}), bf16[2048,1536]{0,1:T(8,128)(2,1)}) %all-gather.24.cloned.1.call-update) | async-done | bytes 6291472 | tf_op jit(solution)/shard_map/all_gather | solution.py:127
  760.9 5.8 multiply_convert_fusion
  767.5 5.7 fusion.149
  776.3 9.9 reduce-scatter.28.cloned.1.call-start
  786.9 6.0 convolution_convert_fusion
  792.8 15.7 all-reduce.8.cloned.1.call-done
  829.3 437.2 %while.48 = (s32[]{:T(128)}, f32[2,6,64,128]{3,2,1,0:T(8,128)S(1)}, f32[2,6,64,128]{3,2,1,0:T(8,128)}, f32[2,6,64,128]{3,2,1,0:T(8,128)}, f32[2,6,64,128]{3,2,1,...) while((s32[]{:T(128)}, f32[2,6,64,128]{3,2,1,0:T(8,128)S(1)}, ...), condition=%wide.region_15.17_spmd.clone, body=%wide.region_14.16_spmd.clone.sunk | while | flops 869605376 | bytes 18314600 | solution.py:282
  1321.4 6.4 fusion.151
  1328.9 6.4 fusion.152
  1336.5 6.4 fusion.153
  1343.0 15.2 reduce-scatter.28.cloned.1.call-done
  1359.7 36.9 %all-reduce.10.cloned.1.call-done = (bf16[128,1536]{1,0:T(8,128)(2,1)}, bf16[128,1536]{1,0:T(8,128)(2,1)}) async-done(((bf16[128,1536]{1,0:T(8,128)(2,1)}, bf16[128,1536]{1,0:T(8,128)(2,1)}), (bf16[128,1536]{1,0:T(8,128)(2,1)}, bf16[128,1536]{1,0:T(8,128)(2,1)})) %all-reduce.10.cloned.1.call-update) | async-done | bytes 786448 | tf_op jit(solution)/shard_map/psum | solution.py:205
  1398.0 48.3 %all-reduce = (f32[6]{0:T(128)}, f32[1536]{0:T(1024)}, f32[1536]{0:T(1024)}) all-reduce(f32[6]{0:T(128)S(1)} %copy-done.83, f32[1536]{0:T(1024)S(1)} %get-tuple-element.407, f32[1536]{0:T(1024)S(1)} %copy-done.78), channel_id=1, replica_groups=mesh['seq'=16,'head'=2] {'seq'}, use_global_device_ids=true, to_apply=%region_27.30 | all-reduce | flops 3078 | bytes 24624 | tf_op jit(solution)/shard_map/psum | solution.py:327
  1450.3 25.2 %reduce-scatter.12.cloned.1.call-done = f32[96,768]{1,0:T(8,128)} async-done(((f32[1536,768]{1,0:T(8,128)}), f32[96,768]{1,0:T(8,128)}) %reduce-scatter.12.cloned.1.call-update) | async-done | bytes 294928 | tf_op jit(solution)/shard_map/reduce_scatter | solution.py:317
  1475.5 79.4 %reduce-scatter.14.cloned.1.call-done = f32[96,768]{1,0:T(8,128)} async-done(((f32[1536,768]{1,0:T(8,128)}), f32[96,768]{1,0:T(8,128)}) %reduce-scatter.14.cloned.1.call-update) | async-done | bytes 294928 | tf_op jit(solution)/shard_map/reduce_scatter | solution.py:318
  1554.9 78.8 %reduce-scatter.16.cloned.1.call-done = f32[96,768]{1,0:T(8,128)} async-done(((f32[1536,768]{1,0:T(8,128)}), f32[96,768]{1,0:T(8,128)}) %reduce-scatter.16.cloned.1.call-update) | async-done | bytes 294928 | tf_op jit(solution)/shard_map/reduce_scatter | solution.py:319
  1633.7 79.6 %reduce-scatter.18.cloned.1.call-done = f32[96,768]{1,0:T(8,128)} async-done(((f32[1536,768]{1,0:T(8,128)}), f32[96,768]{1,0:T(8,128)}) %reduce-scatter.18.cloned.1.call-update) | async-done | bytes 294928 | tf_op jit(solution)/shard_map/reduce_scatter | solution.py:320
  1713.3 78.9 %reduce-scatter.20.cloned.1.call-done = f32[768,96]{0,1:T(8,128)} async-done(((f32[768,1536]{0,1:T(8,128)}), f32[768,96]{0,1:T(8,128)}) %reduce-scatter.20.cloned.1.call-update) | async-done | bytes 294928 | tf_op jit(solution)/shard_map/reduce_scatter | solution.py:322
  1792.1 140.5 %reduce-scatter.22.cloned.1.call-done = f32[96,2048]{1,0:T(8,128)} async-done(((f32[1536,2048]{1,0:T(8,128)}), f32[96,2048]{1,0:T(8,128)}) %reduce-scatter.22.cloned.1.call-update) | async-done | bytes 786448 | tf_op jit(solution)/shard_map/reduce_scatter | solution.py:323
  1932.6 139.1 %reduce-scatter.24.cloned.1.call-done = f32[96,2048]{1,0:T(8,128)} async-done(((f32[1536,2048]{1,0:T(8,128)}), f32[96,2048]{1,0:T(8,128)}) %reduce-scatter.24.cloned.1.call-update) | async-done | bytes 786448 | tf_op jit(solution)/shard_map/reduce_scatter | solution.py:324
  2071.7 138.8 %reduce-scatter.26.cloned.1.call-done = f32[2048,96]{0,1:T(8,128)} async-done(((f32[2048,1536]{0,1:T(8,128)}), f32[2048,96]{0,1:T(8,128)}) %reduce-scatter.26.cloned.1.call-update) | async-done | bytes 786448 | tf_op jit(solution)/shard_map/reduce_scatter | solution.py:325
  (956 shorter events, 868.3 us)
Async XLA Ops:
  7.2 45.6 %all-gather.10.cloned.1.call-start = ((), (), s32[]{:S(2)}) async-start(), calls=%async_computation.9 | async-start | bytes 2506752 | tf_op jit(solution)/shard_map/all_gather | solution.py:119
  7.9 88.3 %all-gather.12.cloned.1.call-start = ((), (), s32[]{:S(2)}) async-start(), calls=%async_computation.10 | async-start | bytes 2506752 | tf_op jit(solution)/shard_map/all_gather | solution.py:120
  8.7 130.9 %all-gather.14.cloned.1.call-start = ((), (), s32[]{:S(2)}) async-start(), calls=%async_computation.11 | async-start | bytes 2506752 | tf_op jit(solution)/shard_map/all_gather | solution.py:122
  9.4 202.1 %all-gather.16.cloned.1.call-start = ((), (), s32[]{:S(2)}) async-start(), calls=%async_computation.12 | async-start | bytes 2506752 | tf_op jit(solution)/shard_map/all_gather | solution.py:121
  10.0 522.7 %all-gather.18.cloned.1.call-start = ((), (), s32[]{:S(2)}) async-start(), calls=%async_computation.13 | async-start | bytes 2506752 | tf_op jit(solution)/shard_map/all_gather | solution.py:124
  10.6 559.0 %all-reduce.6.cloned.1.call-start = ((), (), s32[]{:S(2)}) async-start(), calls=%async_computation.14 | async-start | bytes 1572864 | tf_op jit(solution)/shard_map/psum | solution.py:196
  536.2 98.7 %all-gather.20.cloned.1.call-start = ((), (), s32[]{:S(2)}) async-start(), calls=%async_computation.15 | async-start | bytes 6684672 | tf_op jit(solution)/shard_map/all_gather | solution.py:125
  536.9 160.9 %all-gather.22.cloned.1.call-start = ((), (), s32[]{:S(2)}) async-start(), calls=%async_computation.16 | async-start | bytes 6684672 | tf_op jit(solution)/shard_map/all_gather | solution.py:126
  537.7 223.2 %all-gather.24.cloned.1.call-start = ((), (), s32[]{:S(2)}) async-start(), calls=%async_computation.17 | async-start | bytes 6684672 | tf_op jit(solution)/shard_map/all_gather | solution.py:127
  538.4 270.1 %all-reduce.8.cloned.1.call-start = ((), (), s32[]{:S(2)}) async-start(), calls=%async_computation.18 | async-start | bytes 1572864 | tf_op jit(solution)/shard_map/psum | solution.py:222
  776.3 581.9 %reduce-scatter.28.cloned.1.call-start = ((), (), s32[]{:S(2)}) async-start(), calls=%async_computation.27 | async-start | bytes 835584
  840.0 17.5 collective-permute-start.3
  869.2 17.9 collective-permute-start.3
  898.8 18.7 collective-permute-start.3
  929.2 17.9 collective-permute-start.3
  958.7 17.6 collective-permute-start.3
  988.0 17.2 collective-permute-start.3
  1016.9 17.2 collective-permute-start.3
  1045.8 17.2 collective-permute-start.3
  1074.6 17.2 collective-permute-start.3
  1103.5 17.2 collective-permute-start.3
  1132.4 17.2 collective-permute-start.3
  1190.2 17.2 collective-permute-start.3
  1298.4 98.2 %all-reduce.10.cloned.1.call-start = ((), (), s32[]{:S(2)}) async-start(), calls=%async_computation.28 | async-start | bytes 1572864 | tf_op jit(solution)/shard_map/psum | solution.py:205
  1306.1 169.4 %reduce-scatter.12.cloned.1.call-start = ((), (), s32[]{:S(2)}) async-start(), calls=%async_computation.19 | async-start | bytes 5013504 | tf_op jit(solution)/shard_map/reduce_scatter | solution.py:317
  1309.1 245.8 %reduce-scatter.14.cloned.1.call-start = ((), (), s32[]{:S(2)}) async-start(), calls=%async_computation.20 | async-start | bytes 5013504 | tf_op jit(solution)/shard_map/reduce_scatter | solution.py:318
  1312.3 321.4 %reduce-scatter.16.cloned.1.call-start = ((), (), s32[]{:S(2)}) async-start(), calls=%async_computation.21 | async-start | bytes 5013504 | tf_op jit(solution)/shard_map/reduce_scatter | solution.py:319
  1315.3 398.0 %reduce-scatter.18.cloned.1.call-start = ((), (), s32[]{:S(2)}) async-start(), calls=%async_computation.22 | async-start | bytes 5013504 | tf_op jit(solution)/shard_map/reduce_scatter | solution.py:320
  1318.3 473.8 %reduce-scatter.20.cloned.1.call-start = ((), (), s32[]{:S(2)}) async-start(), calls=%async_computation.23 | async-start | bytes 5013504 | tf_op jit(solution)/shard_map/reduce_scatter | solution.py:322
  1321.4 611.2 %reduce-scatter.22.cloned.1.call-start = ((), (), s32[]{:S(2)}) async-start(), calls=%async_computation.24 | async-start | bytes 13369344 | tf_op jit(solution)/shard_map/reduce_scatter | solution.py:323
  1327.9 743.8 %reduce-scatter.24.cloned.1.call-start = ((), (), s32[]{:S(2)}) async-start(), calls=%async_computation.25 | async-start | bytes 13369344 | tf_op jit(solution)/shard_map/reduce_scatter | solution.py:324
  1335.3 875.2 %reduce-scatter.26.cloned.1.call-start = ((), (), s32[]{:S(2)}) async-start(), calls=%async_computation.26 | async-start | bytes 13369344 | tf_op jit(solution)/shard_map/reduce_scatter | solution.py:325
  (147 other events, 4337.1 us)
Sparse Core Ops, SparseCore 0:
  10.3 42.4 all-gather.9
  55.0 41.0 all-gather.11
  98.5 41.0 all-gather.13
  141.7 41.8 all-gather.15
  185.8 41.5 all-gather.17
  536.3 33.2 all-reduce.5
  572.1 62.6 all-gather.19
  637.4 60.4 all-gather.21
  700.4 60.4 all-gather.23
  776.4 32.0 all-reduce.7
  1298.5 59.6 reduce-scatter.27
  1361.1 35.4 all-reduce.9
  1401.0 74.4 reduce-scatter.11
  1480.3 74.5 reduce-scatter.13
  1559.2 74.4 reduce-scatter.15
  1638.5 74.7 reduce-scatter.17
  1717.5 74.5 reduce-scatter.19
  1797.2 135.3 reduce-scatter.21
  1937.8 133.8 reduce-scatter.23
  2076.7 133.7 reduce-scatter.25
where the time goes:
time: 2240 us; the launch traced here: 2220 us
  waiting for transfers between devices  1140 us (51%)
  matrix products  497 us (22%)
  starting transfers between devices  207 us (9%)
  local copies, waits for them, and re-layouts  150 us (7%)
  other arithmetic  125 us (6%)
  blocking collectives  65.1 us (3%)
  loops' own time  23 us (1%)
    ppermute x75, starting transfers between devices, passed_along(): lax.ppermute(value, axis, [(source, source + steps) for source in range(l...  196 us
    reduce_scatter x1, waiting for transfers between devices, local(): lax.psum_scatter(gate_grad, 'seq', scatter_dimension=0, tiled=True)  140 us
    reduce_scatter x1, waiting for transfers between devices, local(): lax.psum_scatter(up_grad, 'seq', scatter_dimension=0, tiled=True)  139 us
    reduce_scatter x1, waiting for transfers between devices, local(): lax.psum_scatter(down_grad, 'seq', scatter_dimension=1, tiled=True)  139 us
    dot_general x60, matrix products, transform(): jnp.einsum('...jd,...sd->...js', keys_in, mirror, precision=highest)  96.9 us
    reduce_scatter x1, waiting for transfers between devices, local(): lax.psum_scatter(house_grad, 'seq', scatter_dimension=0, tiled=True)  79.6 us
    reduce_scatter x1, waiting for transfers between devices, local(): lax.psum_scatter(key_grad, 'seq', scatter_dimension=0, tiled=True)  79.4 us
    reduce_scatter x1, waiting for transfers between devices, local(): lax.psum_scatter(out_weight_grad, 'seq', scatter_dimension=1, tiled=True)  78.9 us
  transfers between devices with their start and end apart: 95, of which 18 were waited for; matrix products, arithmetic and copies ran while one was open for 25% of the time, Pallas kernels for 0%

commit v1 on v0

v1 whole, which is shorter than its diff:
```python
import functools

import jax
import jax.numpy as jnp
from jax import lax
from jax.experimental import pallas as pl
from jax.experimental.pallas import tpu as pltpu
from jax.sharding import Mesh
from jax.sharding import PartitionSpec as P

epsilon = 1e-06
masked_score = -1e30
MERGE_LIMIT = 2048
LEAF = 128
NN, NT, TN = ((1,), (0,)), ((1,), (1,)), ((0,), (0,))


def split(a):
    if isinstance(a, tuple):
        return a
    if a.dtype == jnp.bfloat16:
        return (a, None)
    high = a.astype(jnp.bfloat16)
    return (high, (a - high.astype(jnp.float32)).astype(jnp.bfloat16))


def raw_dot(a, b, dims):
    return lax.dot_general(a, b, (dims, ((), ())), preferred_element_type=jnp.float32)


def dot_parts(a, b, dims):
    (ah, al), (bh, bl) = split(a), split(b)
    total = raw_dot(ah, bh, dims)
    if bl is not None:
        total = total + raw_dot(ah, bl, dims)
    if al is not None:
        total = total + raw_dot(al, bh, dims)
    return total


def grid_of(shape, axis):
    return lax.broadcasted_iota(jnp.int32, shape, axis)


def leaf_masks():
    row, col = grid_of((LEAF, LEAF), 0), grid_of((LEAF, LEAF), 1)
    return row, col


def leaf_forward_kernel(leaves, q_ref, k_ref, h_ref, g_ref, x_out, a_out, c_out, u_out, w_out, tm_out, dots_out, own_out, qm_out, km_out, p_out):
    mm = dot_parts
    row, col = leaf_masks()
    eye = (row == col).astype(jnp.float32)
    span = range(leaves)
    at = [pl.ds(g * LEAF, LEAF) for g in span]
    q = [split(q_ref[i, :]) for i in at]
    k = [split(k_ref[i, :]) for i in at]
    mirror, strength = [], []
    for i in at:
        h = h_ref[i, :]
        mirror.append(split(h * lax.rsqrt(jnp.sum(h * h, axis=-1, keepdims=True) + epsilon)))
        strength.append(2.0 * jax.nn.sigmoid(jnp.broadcast_to(g_ref[i, 0:1], (LEAF, LEAF))))
    dots = [mm(m, m, NT) for m in mirror]
    system = [jnp.where(row > col, d, 0.0) * s for d, s in zip(dots, strength)]
    inverse = [eye - jnp.where((row // 2 == col // 2), n, 0.0) for n in system]
    width = 2
    while width < LEAF:
        picked = (row // (2 * width) == col // (2 * width)) & (row // width != col // width)
        parts = [split(x) for x in inverse]
        off = [split(jnp.where(picked, n, 0.0)) for n in system]
        turned = [mm(x, n, NN) for x, n in zip(parts, off)]
        inverse = [x - mm(t, p, NN) for x, t, p in zip(inverse, turned, parts)]
        width *= 2
    triang = [split(x * s.T) for x, s in zip(inverse, strength)]
    a_part = [split(jnp.where(row >= col, mm(x, m, NT), 0.0)) for x, m in zip(q, mirror)]
    c_part = [split(jnp.where(row < col, mm(x, m, NT), 0.0)) for x, m in zip(k, mirror)]
    own = [mm(x, y, NT) for x, y in zip(q, k)]
    u_part = [split(mm(x, t, NN)) for x, t in zip(a_part, triang)]
    w_part = [split(mm(x, t, NT)) for x, t in zip(c_part, triang)]
    tm_part = [split(mm(t, m, NN)) for t, m in zip(triang, mirror)]
    for g, i in enumerate(at):
        x_out[i, :] = inverse[g]
        dots_out[i, :] = dots[g]
        for ref, value in ((a_out, a_part), (c_out, c_part), (u_out, u_part), (w_out, w_part), (tm_out, tm_part)):
            high, low = value[g]
            ref[i, :] = high.astype(jnp.float32) + low.astype(jnp.float32)
        own_out[i, :] = own[g] - mm(u_part[g], c_part[g], NT)
        qm_out[i, :] = q_ref[i, :] - mm(u_part[g], mirror[g], NN)
        km_out[i, :] = k_ref[i, :] - mm(w_part[g], mirror[g], NN)
        p_out[i, :] = eye - mm(mirror[g], tm_part[g], TN)


def leaf_backward_kernel(leaves, q_ref, k_ref, h_ref, g_ref, x_ref, a_ref, c_ref, u_ref, w_ref, tm_ref, dots_ref, gown_ref, gqm_ref, gkm_ref, gp_ref, dv_ref, out):
    mm = dot_parts
    row, col = leaf_masks()
    ones = jnp.ones((LEAF, LEAF), jnp.bfloat16)
    at = [pl.ds(g * LEAF, LEAF) for g in range(leaves)]
    q = [split(q_ref[i, :]) for i in at]
    k = [split(k_ref[i, :]) for i in at]
    h = [h_ref[i, :] for i in at]
    scaling = [lax.rsqrt(jnp.sum(x * x, axis=-1, keepdims=True) + epsilon) for x in h]
    mirror_full = [x * r for x, r in zip(h, scaling)]
    mirror = [split(x) for x in mirror_full]
    strength = [2.0 * jax.nn.sigmoid(jnp.broadcast_to(g_ref[i, 0:1], (LEAF, LEAF))) for i in at]
    inverse_full = [x_ref[i, :] for i in at]
    inverse = [split(x) for x in inverse_full]
    strength_row = [s.T for s in strength]
    triang = [split(x * s) for x, s in zip(inverse_full, strength_row)]
    a_part = [split(a_ref[i, :]) for i in at]
    c_part = [split(c_ref[i, :]) for i in at]
    u_part = [split(u_ref[i, :]) for i in at]
    w_part = [split(w_ref[i, :]) for i in at]
    tm_part = [split(tm_ref[i, :]) for i in at]
    gown = [split(gown_ref[i, :]) for i in at]
    gqm = [split(gqm_ref[i, :]) for i in at]
    gkm = [split(gkm_ref[i, :]) for i in at]
    gp = [split(gp_ref[i, :]) for i in at]
    span = range(leaves)
    gu = [split(-mm(gqm[g], mirror[g], NT) - mm(gown[g], c_part[g], NN)) for g in span]
    gw = [split(-mm(gkm[g], mirror[g], NT)) for g in span]
    mgp = [split(mm(mirror[g], gp[g], NN)) for g in span]
    ga = [split(jnp.where(row >= col, mm(gu[g], triang[g], NT), 0.0)) for g in span]
    gc = [split(jnp.where(row < col, mm(gw[g], triang[g], NN) - mm(gown[g], u_part[g], TN), 0.0)) for g in span]
    gt = [mm(a_part[g], gu[g], TN) + mm(gw[g], c_part[g], TN) - mm(mgp[g], mirror[g], NT) for g in span]
    gx = [split(gt[g] * strength_row[g]) for g in span]
    xgx = [split(mm(inverse[g], gx[g], TN)) for g in span]
    gn = [jnp.where(row > col, -mm(xgx[g], inverse[g], NT), 0.0) for g in span]
    gdots = [split(strength[g] * gn[g]) for g in span]
    for g, i in enumerate(at):
        gm = (
            -mm(u_part[g], gqm[g], TN)
            - mm(w_part[g], gkm[g], TN)
            + mm(ga[g], q[g], TN)
            + mm(gc[g], k[g], TN)
            + mm(gdots[g], mirror[g], NN)
            + mm(gdots[g], mirror[g], TN)
            - mm(tm_part[g], gp[g], NT)
            - mm(triang[g], mgp[g], TN)
        )
        gq = gqm_ref[i, :] + mm(gown[g], k[g], NN) + mm(ga[g], mirror[g], NN)
        gk = gkm_ref[i, :] + mm(gown[g], q[g], TN) + mm(gc[g], mirror[g], NN)
        gh = scaling[g] * (gm - mirror_full[g] * jnp.sum(gm * mirror_full[g], axis=-1, keepdims=True))
        gs = mm(gn[g] * dots_ref[i, :], ones, NN) + mm(gt[g] * inverse_full[g], ones, TN)
        gl = gs * strength[g] * (1.0 - 0.5 * strength[g])
        out[i, 0:128] = gq.astype(jnp.bfloat16)
        out[i, 128:256] = gk.astype(jnp.bfloat16)
        out[i, 256:384] = dv_ref[i, :].astype(jnp.bfloat16)
        out[i, 384:512] = gh.astype(jnp.bfloat16)
        out[i, 512:640] = jnp.where(col == 0, gl, 0.0).astype(jnp.bfloat16)


def halves(length):
    found, h = [], LEAF
    while h < length:
        found.append(h)
        h *= 2
    return found


def merge_forward(length, scale, own, v, qm, km, p, lab_col, lab_row, attended, lse, levels, m_ref, l_ref, o_ref):
    mm = dot_parts
    row, col = leaf_masks()
    for start in range(0, length, LEAF):
        i = slice(start, start + LEAF)
        allowed = (row >= col) & (lab_col[i, 0:1] == lab_row[:, i])
        scores = jnp.where(allowed, own[i, :] * scale, masked_score)
        top = jnp.max(scores, axis=-1, keepdims=True)
        weights = jnp.exp(scores - top)
        m_ref[i, :] = top
        l_ref[i, :] = jnp.sum(weights, axis=-1, keepdims=True)
        o_ref[i, :] = mm(weights, v[i, :], NN)
    sizes = halves(length)
    for step, h in enumerate(sizes):
        last = step + 1 == len(sizes)
        if not last:
            qm_next, km_next, p_next = levels[step]
        for start in range(0, length, 2 * h):
            a, b = slice(start, start + h), slice(start + h, start + 2 * h)
            pa = slice(start // h * LEAF, start // h * LEAF + LEAF)
            pb = slice(start // h * LEAF + LEAF, start // h * LEAF + 2 * LEAF)
            qm_b, km_a = split(qm[b, :]), split(km[a, :])
            scores = mm(qm_b, km_a, NT) * scale
            scores = jnp.where(lab_col[b, 0:1] == lab_row[:, a], scores, masked_score)
            old = m_ref[b, :]
            top = jnp.maximum(old, jnp.max(scores, axis=-1, keepdims=True))
            factor = jnp.exp(old - top)
            weights = jnp.exp(scores - top)
            m_ref[b, :] = top
            l_ref[b, :] = l_ref[b, :] * factor + jnp.sum(weights, axis=-1, keepdims=True)
            o_ref[b, :] = o_ref[b, :] * factor + mm(weights, v[a, :], NN)
            if not last:
                p_a, p_b = split(p[pa, :]), split(p[pb, :])
                qm_next[a, :] = qm[a, :]
                qm_next[b, :] = mm(qm_b, p_a, NN)
                km_next[b, :] = km[b, :]
                km_next[a, :] = mm(km_a, p_b, NT)
                if p_next is not None:
                    into = start // (2 * h) * LEAF
                    p_next[slice(into, into + LEAF), :] = mm(p_b, p_a, NN)
        if not last:
            qm, km, p = qm_next, km_next, p_next
    total = l_ref[...]
    attended[...] = o_ref[...] / total
    lse[...] = jnp.broadcast_to(m_ref[...] + jnp.log(total), (length, LEAF))


def merge_backward(length, scale, own, v, levels, lab_col, lab_row, attended, lse, dout, gown, gqm, gkm, gp, dv, delta_ref):
    mm = dot_parts
    row, col = leaf_masks()
    delta_ref[...] = jnp.sum(dout[...] * attended[...], axis=-1, keepdims=True)
    for start in range(0, length, LEAF):
        i = slice(start, start + LEAF)
        allowed = (row >= col) & (lab_col[i, 0:1] == lab_row[:, i])
        probs = jnp.where(allowed, jnp.exp(own[i, :] * scale - lse[i, 0:1]), 0.0)
        grad = split(dout[i, :])
        dv[i, :] = mm(probs, grad, TN)
        gown[i, :] = probs * (mm(grad, v[i, :], NT) - delta_ref[i, :]) * scale
    sizes = halves(length)
    for step in reversed(range(len(sizes))):
        h = sizes[step]
        last = step + 1 == len(sizes)
        qm, km, p = levels[step]
        for start in range(0, length, 2 * h):
            a, b = slice(start, start + h), slice(start + h, start + 2 * h)
            pa = slice(start // h * LEAF, start // h * LEAF + LEAF)
            pb = slice(start // h * LEAF + LEAF, start // h * LEAF + 2 * LEAF)
            qm_b, km_a, grad = split(qm[b, :]), split(km[a, :]), split(dout[b, :])
            scores = mm(qm_b, km_a, NT) * scale
            allowed = lab_col[b, 0:1] == lab_row[:, a]
            probs = jnp.where(allowed, jnp.exp(scores - lse[b, 0:1]), 0.0)
            dv[a, :] = dv[a, :] + mm(probs, grad, TN)
            ds = split(probs * (mm(grad, v[a, :], NT) - delta_ref[b, :]) * scale)
            gq_part = mm(ds, km_a, NN)
            gk_part = mm(ds, qm_b, TN)
            if last:
                gqm[a, :] = jnp.zeros((h, LEAF), jnp.float32)
                gkm[b, :] = jnp.zeros((h, LEAF), jnp.float32)
                gqm[b, :] = gq_part
                gkm[a, :] = gk_part
            else:
                p_a, p_b = split(p[pa, :]), split(p[pb, :])
                gq_b, gk_a = split(gqm[b, :]), split(gkm[a, :])
                gp_a, gp_b = mm(qm_b, gq_b, TN), mm(gk_a, km_a, TN)
                if step + 2 < len(sizes):
                    into = start // (2 * h) * LEAF
                    g_up = split(gp[step + 1][slice(into, into + LEAF), :])
                    gp_a, gp_b = gp_a + mm(p_b, g_up, TN), gp_b + mm(g_up, p_a, NT)
                gp[step][pa, :] = gp_a
                gp[step][pb, :] = gp_b
                gqm[b, :] = mm(gq_b, p_a, NT) + gq_part
                gkm[a, :] = mm(gk_a, p_b, NN) + gk_part


def whole_dot(spec, *operands):
    return jnp.einsum(spec, *operands, precision=lax.Precision.HIGHEST)


def pairs(value, size):
    both = value.reshape(-1, 2, size, value.shape[-1])
    return both[:, 0], both[:, 1]


def joined(first, second):
    return jnp.stack([first, second], axis=1).reshape(-1, first.shape[-1])


def long_allowed(label, size, own):
    both = label.reshape(-1, size) if own else label.reshape(-1, 2, size)
    left, right = (both, both) if own else (both[:, 0], both[:, 1])
    same = right[:, :, None] == left[:, None, :]
    return same & jnp.tril(jnp.ones((size, size), jnp.bool_)) if own else same


def long_forward(length, scale, own, v, qm, km, p, label):
    scores = jnp.where(long_allowed(label, LEAF, True), own.reshape(-1, LEAF, LEAF) * scale, masked_score)
    top = jnp.max(scores, axis=-1, keepdims=True)
    weights = jnp.exp(scores - top)
    state = [
        x.reshape(length, -1)
        for x in (top, jnp.sum(weights, axis=-1, keepdims=True), whole_dot("nij,njd->nid", weights, v.reshape(-1, LEAF, LEAF)))
    ]
    levels = []
    for h in halves(length):
        (q_a, q_b), (k_a, k_b), (v_a, _) = pairs(qm, h), pairs(km, h), pairs(v, h)
        scores = whole_dot("nid,njd->nij", q_b, k_a) * scale
        scores = jnp.where(long_allowed(label, h, False), scores, masked_score)
        (m_a, m_b), (l_a, l_b), (o_a, o_b) = (pairs(x, h) for x in state)
        top = jnp.maximum(m_b, jnp.max(scores, axis=-1, keepdims=True))
        factor = jnp.exp(m_b - top)
        weights = jnp.exp(scores - top)
        l_b = l_b * factor + jnp.sum(weights, axis=-1, keepdims=True)
        o_b = o_b * factor + whole_dot("nij,njd->nid", weights, v_a)
        state = [joined(m_a, top), joined(l_a, l_b), joined(o_a, o_b)]
        if 2 * h < length:
            p_a, p_b = pairs(p, LEAF)
            qm = joined(q_a, whole_dot("nid,nde->nie", q_b, p_a))
            km = joined(whole_dot("nid,ned->nie", k_a, p_b), k_b)
            p = whole_dot("nde,nef->ndf", p_b, p_a).reshape(-1, LEAF)
            levels += [qm, km] + ([p] if 4 * h < length else [])
    top, total, out = state
    return [out / total, jnp.broadcast_to(top + jnp.log(total), (length, LEAF))] + levels


def long_backward(length, scale, own, v, levels, label, attended, lse, dout):
    lse = lse[:, :1]
    delta = jnp.sum(dout * attended, axis=-1, keepdims=True)
    blocks = lambda x: x.reshape(length // LEAF, LEAF, -1)
    probs = jnp.exp(blocks(own) * scale - blocks(lse))
    probs = jnp.where(long_allowed(label, LEAF, True), probs, 0.0)
    dv = whole_dot("nij,nid->njd", probs, blocks(dout)).reshape(length, LEAF)
    gown = probs * (whole_dot("nid,njd->nij", blocks(dout), blocks(v)) - blocks(delta)) * scale
    gqm = gkm = gp = None
    for h, (qm, km, p) in reversed(list(zip(halves(length), levels))):
        (_, q_b), (k_a, _), (v_a, _), (_, o_b) = pairs(qm, h), pairs(km, h), pairs(v, h), pairs(dout, h)
        scores = whole_dot("nid,njd->nij", q_b, k_a) * scale - pairs(lse, h)[1]
        probs = jnp.where(long_allowed(label, h, False), jnp.exp(scores), 0.0)
        dv_a, dv_b = pairs(dv, h)
        dv = joined(dv_a + whole_dot("nij,nid->njd", probs, o_b), dv_b)
        ds = probs * (whole_dot("nid,njd->nij", o_b, v_a) - pairs(delta, h)[1]) * scale
        gq_part, gk_part = whole_dot("nij,njd->nid", ds, k_a), whole_dot("nij,nid->njd", ds, q_b)
        if gqm is None:
            gqm, gkm = joined(jnp.zeros_like(gq_part), gq_part), joined(gk_part, jnp.zeros_like(gk_part))
            continue
        (gq_a, gq_b), (gk_a, gk_b), (p_a, p_b) = pairs(gqm, h), pairs(gkm, h), pairs(p, LEAF)
        gp_a, gp_b = whole_dot("nid,nie->nde", q_b, gq_b), whole_dot("nid,nie->nde", gk_a, k_a)
        if gp is not None:
            above = gp.reshape(-1, LEAF, LEAF)
            gp_a = gp_a + whole_dot("nde,ndf->nef", p_b, above)
            gp_b = gp_b + whole_dot("ndf,nef->nde", above, p_a)
        gp = joined(gp_a, gp_b)
        gqm = joined(gq_a, whole_dot("nid,ned->nie", gq_b, p_a) + gq_part)
        gkm = joined(whole_dot("nid,nde->nie", gk_a, p_b) + gk_part, gk_b)
    return [gown.reshape(length, LEAF), gqm, gkm, gp, dv]


def matrix(rows, columns=LEAF, dtype=jnp.float32):
    return jax.ShapeDtypeStruct((rows, columns), dtype)


def cost(flops, moved):
    return pl.CostEstimate(flops=flops, bytes_accessed=moved, transcendentals=0)


def settings():
    return pltpu.CompilerParams(vmem_limit_bytes=56 * 1024 * 1024)


def leaf_group(length):
    leaves = length // LEAF
    return 4 if leaves % 4 == 0 else 1


def leaf_forward(proj):
    length = proj.shape[0]
    leaves = leaf_group(length)
    rows = leaves * LEAF
    column = lambda j: pl.BlockSpec((rows, LEAF), lambda i, j=j: (i, j))
    return pl.pallas_call(
        functools.partial(leaf_forward_kernel, leaves),
        grid=(length // rows,),
        in_specs=[column(0), column(1), column(3), column(4)],
        out_specs=[column(0)] * 11,
        out_shape=[matrix(length)] * 11,
        compiler_params=settings(),
        name="leaf_forward",
    )(proj, proj, proj, proj)


def leaf_backward(proj, saved, grads):
    length = proj.shape[0]
    leaves = leaf_group(length)
    rows = leaves * LEAF
    column = lambda j: pl.BlockSpec((rows, LEAF), lambda i, j=j: (i, j))
    return pl.pallas_call(
        functools.partial(leaf_backward_kernel, leaves),
        grid=(length // rows,),
        in_specs=[column(0), column(1), column(3), column(4)] + [column(0)] * (len(saved) + len(grads)),
        out_specs=pl.BlockSpec((rows, 5 * LEAF), lambda i: (i, 0)),
        out_shape=matrix(length, 5 * LEAF, jnp.bfloat16),
        compiler_params=settings(),
        name="leaf_backward",
    )(proj, proj, proj, proj, *saved, *grads)


def level_shapes(length):
    sizes = halves(length)
    shapes = []
    for step in range(1, len(sizes)):
        shapes += [matrix(length), matrix(length)]
        if step + 1 < len(sizes):
            shapes.append(matrix(length // sizes[step] * LEAF))
    return shapes


def level_groups(length, flat):
    sizes, groups, flat = halves(length), [], list(flat)
    for step in range(1, len(sizes)):
        qm, km = flat.pop(0), flat.pop(0)
        groups.append((qm, km, flat.pop(0) if step + 1 < len(sizes) else None))
    return groups


def whole_spec():
    return pl.BlockSpec(memory_space=pltpu.VMEM)


def value_spec(length):
    return pl.BlockSpec((length, LEAF), lambda i: (0, 2))


def plain_spec(shape):
    return pl.BlockSpec(shape, lambda i: (0, 0))


def merge_forward_kernel(length, scale, own, v, qm, km, p, lab_col, lab_row, attended, lse, *rest):
    flat, (m_ref, l_ref, o_ref) = rest[:-3], rest[-3:]
    merge_forward(
        length, scale, own, v, qm, km, p, lab_col, lab_row, attended, lse, level_groups(length, flat), m_ref, l_ref, o_ref
    )


def run_merge_forward(proj, own, qm, km, p, lab_col, lab_row, scale):
    length = proj.shape[0]
    extra = level_shapes(length)
    if length > MERGE_LIMIT:
        return long_forward(length, scale, own, proj[:, 2 * LEAF : 3 * LEAF], qm, km, p, lab_row)
    outs = [matrix(length), matrix(length)] + extra
    return pl.pallas_call(
        functools.partial(merge_forward_kernel, length, scale),
        grid=(1,),
        in_specs=[plain_spec(own.shape), value_spec(length)] + [plain_spec(x.shape) for x in (qm, km, p, lab_col, lab_row)],
        out_specs=[plain_spec(x.shape) for x in outs],
        out_shape=outs,
        scratch_shapes=[pltpu.VMEM((length, 1), jnp.float32), pltpu.VMEM((length, 1), jnp.float32), pltpu.VMEM((length, LEAF), jnp.float32)],
        compiler_params=settings(),
        name="merge_forward",
    )(own, proj, qm, km, p, lab_col, lab_row)


def merge_backward_kernel(length, scale, own, v, qm, km, p, *rest):
    count = len(level_shapes(length))
    flat, rest = rest[:count], rest[count:]
    lab_col, lab_row, attended, lse, dout, gown, gqm, gkm, gp, dv, delta_ref = rest[:11]
    levels = [(qm, km, p)] + level_groups(length, flat)
    merge_backward(
        length, scale, own, v, levels, lab_col, lab_row, attended, lse, dout, gown, gqm, gkm, [gp] + list(rest[11:]), dv, delta_ref
    )


def gp_shapes(length):
    return [(length // h * LEAF, LEAF) for h in halves(length)[1:]]


def run_merge_backward(proj, own, qm, km, p, flat, lab_col, lab_row, attended, lse, dout, scale):
    length = proj.shape[0]
    if length > MERGE_LIMIT:
        levels = [(qm, km, p)] + level_groups(length, flat)
        return long_backward(length, scale, own, proj[:, 2 * LEAF : 3 * LEAF], levels, lab_row, attended, lse, dout)
    operands = [own, proj, qm, km, p, *flat, lab_col, lab_row, attended, lse, dout]
    specs = [plain_spec(x.shape) for x in operands]
    specs[1] = value_spec(length)
    return pl.pallas_call(
        functools.partial(merge_backward_kernel, length, scale),
        grid=(1,),
        in_specs=specs,
        out_specs=[plain_spec((length, LEAF))] * 5,
        out_shape=[matrix(length)] * 5,
        scratch_shapes=[pltpu.VMEM((length, 1), jnp.float32)] + [pltpu.VMEM(shape, jnp.float32) for shape in gp_shapes(length)],
        compiler_params=settings(),
        name="merge_backward",
    )(*operands)


SEQ = ("outer", "mid", "core")
INNER = ("mid", "core")
GROUP = ("mid", "core", "head")
EXTRA = 16


def normalize(values):
    return values * lax.rsqrt(jnp.mean(values * values, axis=-1, keepdims=True) + epsilon)


def norm_back(cotangent, normed, values):
    scaled = lax.rsqrt(jnp.mean(values * values, axis=-1, keepdims=True) + epsilon)
    return scaled * (cotangent - normed * jnp.mean(cotangent * normed, axis=-1, keepdims=True))


def dot(a, b, dims=NN):
    return lax.dot_general(a, b, (dims, ((), ())), preferred_element_type=jnp.float32)


def other_head(value):
    return lax.ppermute(value, "head", [(0, 1), (1, 0)])


def by_head(own, other, axis=0):
    first = lax.axis_index("head") == 0
    return jnp.concatenate([jnp.where(first, own, other), jnp.where(first, other, own)], axis=axis)


def padded(value, axis, size):
    widths = [(0, 0)] * value.ndim
    widths[axis] = (0, size - value.shape[axis])
    return jnp.pad(value, widths)


def local(
    tokens, w_query, w_key, w_value, w_house, w_beta, beta_bias, w_out, w_gate, w_up, w_down, gain_attn, gain_mlp, segment_ids, out_grad
):
    low = jnp.bfloat16
    batches, positions, width = tokens.shape
    half = lax.axis_index("head")
    rank = lax.axis_index(SEQ)
    count = lax.axis_size(SEQ)
    inner = lax.axis_size(INNER)
    rows, half_heads = w_beta.shape
    heads = 2 * half_heads
    assert batches == lax.axis_size("head") and heads <= count
    length = count * positions
    units = w_gate.shape[1] // inner
    scale = LEAF ** (-0.5)

    own_tokens = lax.dynamic_index_in_dim(tokens, half, 0, False)
    all_tokens = lax.all_gather(own_tokens, SEQ, axis=0, tiled=True)
    labels = lax.dynamic_index_in_dim(segment_ids, half, 0, False).astype(low)
    by_heads = [w.reshape(rows, half_heads, LEAF) for w in (w_query, w_key, w_value, w_house)]
    packed = jnp.concatenate(by_heads, axis=2).transpose(1, 0, 2)
    beta_row = padded(w_beta.T[:, None, :], 2, 4 * LEAF)
    packed = padded(jnp.concatenate([packed, beta_row], axis=1), 1, rows + EXTRA)
    packed = padded(by_head(packed, other_head(packed)), 0, count)
    label_row = padded(labels[None], 1, 4 * LEAF)[None]
    at_row = lax.broadcasted_iota(jnp.int32, (1, rows + EXTRA, 1), 1) == rows + 1
    packed = jnp.where(at_row, label_row, packed)
    packed = lax.all_to_all(packed, SEQ, 0, 0, tiled=True)
    weight = packed[:, :rows].reshape(width, 4 * LEAF)
    beta_column = padded(packed[:, rows, :rows].reshape(width, 1), 1, LEAF)
    weight = jnp.concatenate([weight, beta_column], axis=1)
    label_all = packed[:, rows + 1, :positions].reshape(1, length).astype(jnp.float32)
    label_column = jnp.broadcast_to(label_all.reshape(length, 1), (length, LEAF))
    bias_all = padded(by_head(beta_bias, other_head(beta_bias)), 0, count)
    bias_row = padded(lax.dynamic_slice(bias_all, (rank,), (1,)), 0, LEAF)
    bias_row = jnp.concatenate([jnp.zeros(4 * LEAF, jnp.float32), bias_row])

    all_inputs = all_tokens.astype(jnp.float32)
    attn_in = (normalize(all_inputs) * gain_attn).astype(low)
    proj = dot(attn_in, weight) + bias_row
    *saved, own_logits, query_moved, key_moved, product = leaf_forward(proj)
    attended, log_total, *levels = run_merge_forward(
        proj, own_logits, query_moved, key_moved, product, label_column, label_all, scale
    )
    attended_low = attended.astype(low)

    blocks = [w.reshape(rows, inner, units) for w in (w_gate, w_up, w_down.T)]
    mlp_weight = jnp.concatenate(blocks, axis=2).transpose(1, 0, 2)
    mlp_weight = lax.all_to_all(mlp_weight, INNER, 0, 0, tiled=True).reshape(inner * rows, 3 * units)
    mlp_weight = lax.all_gather(mlp_weight, "outer", axis=0, tiled=True)
    gate_up_weight, down_weight = mlp_weight[:, : 2 * units], mlp_weight[:, 2 * units :]
    out_own = lax.all_gather(w_out.T, SEQ, axis=0, tiled=True)
    out_other = other_head(out_own)
    grad_group = lax.all_gather(out_grad, INNER, axis=0, tiled=True).reshape(-1, width)

    heads_here = lax.all_to_all(attended_low.reshape(count, positions, LEAF), SEQ, 0, 0, tiled=True)
    heads_here = heads_here[:heads].reshape(2, half_heads, positions, LEAF).transpose(0, 2, 1, 3)
    heads_here = heads_here.reshape(2, positions, half_heads * LEAF)
    branch = dot(lax.dynamic_index_in_dim(heads_here, half, 0, False), out_own, NT)
    branch = branch + dot(lax.dynamic_index_in_dim(heads_here, 1 - half, 0, False), out_other, NT)
    inputs = own_tokens.astype(jnp.float32)
    middle = inputs + branch
    normed_two = normalize(middle)
    mlp_in = (normed_two * gain_mlp).astype(low)

    mlp_group = lax.all_gather(mlp_in, GROUP, axis=0, tiled=True)
    gate_up = dot(mlp_group, gate_up_weight)
    gate, up = gate_up[:, :units], gate_up[:, units:]
    sigmoid_gate = jax.nn.sigmoid(gate)
    silu_gate = gate * sigmoid_gate
    hidden = (silu_gate * up).astype(low)
    hidden_grad = dot(grad_group, down_weight)
    gate_rows = (hidden_grad * up * sigmoid_gate * (1.0 + gate * (1.0 - sigmoid_gate))).astype(low)
    up_rows = (hidden_grad * silu_gate).astype(low)
    rows_grad = jnp.concatenate([gate_rows, up_rows], axis=1)
    mlp_in_part = dot(rows_grad, gate_up_weight, NT).astype(low)
    mlp_in_grad = lax.psum_scatter(mlp_in_part, GROUP, scatter_dimension=0, tiled=True).astype(jnp.float32)
    mlp_part = dot(hidden, down_weight, NT).astype(low)
    mlp_branch = lax.psum_scatter(mlp_part, GROUP, scatter_dimension=0, tiled=True).astype(jnp.float32)
    block_out = (middle + mlp_branch).astype(low)[None]
    block_out = by_head(block_out, other_head(block_out))

    mlp_grads = jnp.concatenate([dot(mlp_group, rows_grad, TN), dot(grad_group, hidden, TN)], axis=1).astype(low)
    mlp_grads = lax.psum_scatter(mlp_grads, "outer", scatter_dimension=0, tiled=True)
    mlp_grads = lax.all_to_all(mlp_grads.reshape(inner, rows, 3 * units), INNER, 0, 0, tiled=True).astype(jnp.float32)
    gate_grad, up_grad, down_grad = (
        mlp_grads[:, :, i * units : (i + 1) * units].transpose(1, 0, 2).reshape(rows, inner * units) for i in range(3)
    )
    down_grad = down_grad.T

    mlp_gain_part = jnp.sum(mlp_in_grad * normed_two, axis=0)
    own_grad = lax.dynamic_index_in_dim(out_grad, half, 0, False).astype(jnp.float32)
    middle_grad = own_grad + norm_back(mlp_in_grad * gain_mlp, normed_two, middle)
    branch_low = middle_grad.astype(low)
    attended_grad = by_head(dot(branch_low, out_own).astype(low)[None], dot(branch_low, out_other).astype(low)[None])
    attended_grad = attended_grad.reshape(2, positions, half_heads, LEAF).transpose(0, 2, 1, 3)
    attended_grad = padded(attended_grad.reshape(heads, positions, LEAF), 0, count)
    attended_grad = lax.all_to_all(attended_grad, SEQ, 0, 0, tiled=True).reshape(length, LEAF).astype(jnp.float32)
    branch_all = lax.all_gather(branch_low, SEQ, axis=0, tiled=True)

    merged = run_merge_backward(
        proj, own_logits, query_moved, key_moved, product, levels, label_column, label_all, attended, log_total, attended_grad, scale
    )
    proj_grad = leaf_backward(proj, saved, merged)

    attn_in_part = dot(proj_grad, weight, NT)
    attn_gain_part = jnp.sum(attn_in_part * normalize(all_inputs), axis=0)
    attn_in_grad = lax.psum_scatter(attn_in_part.astype(low), SEQ, scatter_dimension=0, tiled=True).astype(jnp.float32)

    weight_grad = dot(attn_in, proj_grad, TN)
    out_weight = dot(branch_all, attended_low, TN)
    bias_part = jnp.sum(proj_grad[:, 4 * LEAF :].astype(jnp.float32), axis=0)
    span = 5 * LEAF
    main = jnp.concatenate([weight_grad[:, : 4 * LEAF], out_weight], axis=1).reshape(count, rows, span)
    beta_rows = padded(weight_grad[:, 4 * LEAF].reshape(count, 1, rows), 2, span)
    gains = jnp.concatenate([attn_gain_part, mlp_gain_part]).reshape(-1, 4 * LEAF)
    gain_rows = gains.shape[0]
    small = jnp.concatenate([padded(gains, 1, span), padded(bias_part[None], 1, span)], axis=0)
    small = jnp.broadcast_to(padded(small, 0, EXTRA - 1), (count, EXTRA - 1, span))
    packed_grad = jnp.concatenate([main, beta_rows, small], axis=1).astype(low)
    packed_grad = lax.all_to_all(packed_grad, SEQ, 0, 0, tiled=True)
    gain_sums = jnp.sum(packed_grad[:, rows + 1 : rows + 1 + gain_rows].astype(jnp.float32), axis=0)
    gain_sums = lax.reduce_precision(gain_sums, 8, 7)
    by_half = packed_grad[:heads].reshape(2, half_heads, rows + EXTRA, span)
    kept = lax.dynamic_index_in_dim(by_half, half, 0, False)
    sent = lax.dynamic_index_in_dim(by_half, 1 - half, 0, False)
    sent = sent.at[:, rows + 1 : rows + 1 + gain_rows].set(gain_sums.astype(low)[None])
    came = other_head(sent)
    sums = kept.astype(jnp.float32) + came.astype(jnp.float32)
    gain_sums = gain_sums + came[0, rows + 1 : rows + 1 + gain_rows].astype(jnp.float32)
    gain_sums = gain_sums[:, : 4 * LEAF].reshape(2, width)
    grads = [
        sums[:, :rows, i * LEAF : (i + 1) * LEAF].transpose(1, 0, 2).reshape(rows, half_heads * LEAF) for i in range(4)
    ]
    out_weight_grad = sums[:, :rows, 4 * LEAF :].transpose(0, 2, 1).reshape(half_heads * LEAF, rows)
    beta_grad = sums[:, rows, :rows].T
    bias_grad = sums[:, rows + 1 + gain_rows, 0]

    tokens_grad = (middle_grad + norm_back(attn_in_grad * gain_attn, normalize(inputs), inputs))[None]
    tokens_grad = by_head(tokens_grad, other_head(tokens_grad))
    return (
        block_out, tokens_grad, *grads, beta_grad, bias_grad, out_weight_grad, gate_grad, up_grad, down_grad, gain_sums[0], gain_sums[1]
    )


def solution(mesh):
    inner = (2, 2)
    fine = Mesh(mesh.devices.reshape(-1, *inner, mesh.shape["head"]), (*SEQ, "head"))
    split_rows, split_columns, by_position = P(SEQ, "head"), P("head", SEQ), P(None, SEQ, None)
    placed = (
        (by_position,) + (split_rows,) * 5 + (P("head"), split_columns, split_rows, split_rows, split_columns)
        + (P(), P(), P(None, SEQ), by_position)
    )
    returned = (
        (by_position, by_position) + (split_rows,) * 5 + (P("head"), split_columns, split_rows, split_rows, split_columns, P(), P())
    )
    return jax.shard_map(local, mesh=fine, in_specs=placed, out_specs=returned, check_vma=False)
```

time: 2240 us -> 630 us (0.28)
  waiting for transfers between devices: 1140 us -> 397 us
  matrix products: 497 us -> 46.2 us
  starting transfers between devices: 207 us -> 32 us
  local copies, waits for them, and re-layouts: 150 us -> 38.3 us
  other arithmetic: 125 us -> 30.1 us
  blocking collectives: 65.1 us -> 18.5 us
  Pallas kernels: 0 us -> 45.6 us
  loops' own time: 23 us -> 0 us
    reduce_scatter x8 -> x4, waiting for transfers between devices: 760 us -> 212 us  [the longest x1 79.5 us: local(): lax.psum_scatter(mlp_grads, 'outer', scatter_dimension=0, tiled=True)]
    dot_general x328 -> x14, matrix products: 494 us -> 46.2 us  [dot(): lax.dot_general(a, b, (dims, ((), ())), preferred_element_type=jnp.float32)]
    ppermute x75 -> x6, starting transfers between devices: 196 us -> 4.68 us  [other_head(): return lax.ppermute(value, 'head', [(0, 1), (1, 0)])]
    all_gather x8 -> x6, waiting for transfers between devices: 270 us -> 90.4 us  [the longest x1 35.4 us: local(): mlp_weight = lax.all_gather(mlp_weight, 'outer', axis=0, tiled=True)]
    psum x3 -> x0, waiting for transfers between devices: 83.7 us -> none  [the longest x1 36.9 us: local(): lax.psum(jnp.dot(hidden, down_full, preferred_element_type=jnp.float32).a...]
    all_to_all x0 -> x5, waiting for transfers between devices: none -> 75.5 us  [the longest x1 46.1 us: local(): packed = lax.all_to_all(packed, SEQ, 0, 0, tiled=True)]
    another operation x7 -> x0, other arithmetic: 59.3 us -> none  [the longest x5 59.2 us: block_factors(): jax.scipy.linalg.solve_triangular(system, diagonal, lower=True, unit_diag...]
    psum x1 -> x0, blocking collectives: 48.3 us -> none  [local(): small_sums = lax.psum((attn_gain_part, mlp_gain_part, bias_part), 'seq')]
  transfers between devices with their start and end apart: 95 -> 21, of which waited for: 18 -> 16; matrix products, arithmetic and copies ran while one was open for 25% -> 15% of each run, Pallas kernels for 0% -> 7%
where the time goes in v1:
time: 630 us; the launch traced here: 623 us
  waiting for transfers between devices  397 us (63%)
  matrix products  46.2 us (7%)
  Pallas kernels  45.6 us (7%)
  local copies, waits for them, and re-layouts  38.3 us (6%)
  starting transfers between devices  32 us (5%)
  other arithmetic  30.1 us (5%)
  blocking collectives  18.5 us (3%)
  between operations  15.1 us (2%)
    reduce_scatter x1, waiting for transfers between devices, local(): lax.psum_scatter(mlp_grads, 'outer', scatter_dimension=0, tiled=True)  79.5 us
    reduce_scatter x1, waiting for transfers between devices, local(): lax.psum_scatter(attn_in_part.astype(low), SEQ, scatter_dimension=0, tile...  53.9 us
    dot_general x14, matrix products, dot(): lax.dot_general(a, b, (dims, ((), ())), preferred_element_type=jnp.float32)  46.2 us
    all_to_all x1, waiting for transfers between devices, local(): packed = lax.all_to_all(packed, SEQ, 0, 0, tiled=True)  46.1 us
    reduce_scatter x1, waiting for transfers between devices, local(): lax.psum_scatter(mlp_part, GROUP, scatter_dimension=0, tiled=True)  40.5 us
    reduce_scatter x1, waiting for transfers between devices, local(): lax.psum_scatter(mlp_in_part, GROUP, scatter_dimension=0, tiled=True)  38.1 us
    all_gather x1, waiting for transfers between devices, local(): mlp_weight = lax.all_gather(mlp_weight, 'outer', axis=0, tiled=True)  35.4 us
    all_gather x1, waiting for transfers between devices, local(): mlp_group = lax.all_gather(mlp_in, GROUP, axis=0, tiled=True)  29.7 us
  transfers between devices with their start and end apart: 21, of which 16 were waited for; matrix products, arithmetic and copies ran while one was open for 15% of the time, Pallas kernels for 7%

profile of v1, /device:TPU:21, one launch (start us, length us, event | category | flops | bytes accessed | tf_op | source)
XLA Modules:
  0.0 622.6 jit_solution(6073458959486915320)
XLA Ops:
  18.0 4.2 all-to-all-start.2
  22.2 9.1 %collective-permute-done = bf16[6,112,512]{2,1,0:T(8,128)(2,1)} collective-permute-done((bf16[6,112,512]{2,1,0:T(8,128)(2,1)S(1)}, bf16[6,112,512]{2,1,0:T(8,128)(2,1)}, u32[]{:S(2)}, u32[]{:S(2)}) %collective-permute-start) | collective-permute-done | bytes 688160 | tf_op jit(solution)/shard_map/ppermute | solution.py:494
  33.8 3.3 all-to-all-done.2
  42.6 6.3 %all-to-all-start = ((bf16[16,112,512]{2,1,0:T(8,128)(2,1)}), bf16[16,112,512]{2,1,0:T(8,128)(2,1)S(1)}, u32[]{:S(2)}, u32[]{:S(2)}) async-start(bf16[16,112,512]{2,1,0:T(8,128)(2,1)} %copy.87), calls=%async_computation | async-start | bytes 3670016 | tf_op jit(solution)/shard_map/all_to_all | solution.py:535
  54.2 46.1 %all-to-all-done = bf16[16,112,512]{2,1,0:T(8,128)(2,1)S(1)} async-done(((bf16[16,112,512]{2,1,0:T(8,128)(2,1)}), bf16[16,112,512]{2,1,0:T(8,128)(2,1)S(1)}, u32[]{:S(2)}, u32[]{:S(2)}) %all-to-all-start) | async-done | bytes 1835040 | tf_op jit(solution)/shard_map/all_to_all | solution.py:535
  102.8 9.6 %all-gather.18.cloned.1.call-done = bf16[1,1024,1536]{2,1,0:T(8,128)(2,1)} async-done(((bf16[1,64,1536]{2,1,0:T(8,128)(2,1)}), bf16[1,1024,1536]{2,1,0:T(8,128)(2,1)}) %all-gather.18.cloned.1.call-update) | async-done | bytes 3145744 | tf_op jit(solution)/shard_map/all_gather | solution.py:525
  115.3 5.2 convolution_add_fusion.1.q_ref.k_ref.h_ref.g_ref.v
  120.5 11.7 %leaf_forward.1 = (f32[1024,128]{1,0:T(8,128)}, f32[1024,128]{1,0:T(8,128)}, f32[1024,128]{1,0:T(8,128)}, f32[1024,128]{1,0:T(8,128)}, f32[1024,128]{1,0:T(8,128...) custom-call(f32[1024,640]{1,0:T(8,128)} %convolution_add_fusion.1.q_, ...), custom_call_target="tpu_custom_call" | custom-call | tf_op jit(solution)/shard_map/leaf_forward/pallas_call | solution.py:358
  133.2 9.9 %merge_forward.1 = (f32[1024,128]{1,0:T(8,128)}, f32[1024,128]{1,0:T(8,128)}, f32[1024,128]{1,0:T(8,128)}, f32[1024,128]{1,0:T(8,128)}, f32[512,128]{1,0:T(8,128...) custom-call(f32[1024,128]{1,0:T(8,128)} %get-tuple-element.49.own, ...), custom_call_target="tpu_custom_call" | custom-call | tf_op jit(solution)/shard_map/merge_forward/pallas_call | solution.py:428
  144.9 6.2 %all-to-all-start.1 = ((bf16[16,64,128]{2,1,0:T(8,128)(2,1)}), bf16[16,64,128]{2,1,0:T(8,128)(2,1)S(1)}, u32[]{:S(2)}, u32[]{:S(2)}) async-start(bf16[16,64,128]{2,1,0:T(8,128)(2,1)} %bitcast.7), calls=%async_computation.1 | async-start | bytes 524288 | tf_op jit(solution)/shard_map/all_to_all | solution.py:563
  151.2 15.1 %all-to-all-done.1 = bf16[16,64,128]{2,1,0:T(8,128)(2,1)S(1)} async-done(((bf16[16,64,128]{2,1,0:T(8,128)(2,1)}), bf16[16,64,128]{2,1,0:T(8,128)(2,1)S(1)}, u32[]{:S(2)}, u32[]{:S(2)}) %all-to-all-start.1) | async-done | bytes 262176 | tf_op jit(solution)/shard_map/all_to_all | solution.py:563
  171.3 35.4 %all-gather.12.cloned.1.call-done = bf16[1536,1536]{1,0:T(8,128)(2,1)} async-done(((bf16[384,1536]{1,0:T(8,128)(2,1)}), bf16[1536,1536]{1,0:T(8,128)(2,1)}) %all-gather.12.cloned.1.call-update) | async-done | bytes 4718608 | tf_op jit(solution)/shard_map/all_gather | solution.py:557
  206.8 29.7 %all-gather.10.cloned.1.call-done = bf16[512,1536]{1,0:T(8,128)(2,1)} async-done(((bf16[64,1536]{1,0:T(8,128)(2,1)}), bf16[512,1536]{1,0:T(8,128)(2,1)}) %all-gather.10.cloned.1.call-update) | async-done | bytes 1572880 | tf_op jit(solution)/shard_map/all_gather | solution.py:573
  236.4 5.5 fusion.11
  241.9 15.7 %all-gather.14.cloned.1.call-done = bf16[8,64,1536]{2,1,0:T(8,128)(2,1)} async-done(((bf16[2,64,1536]{2,1,0:T(8,128)(2,1)}), bf16[8,64,1536]{2,1,0:T(8,128)(2,1)}) %all-gather.14.cloned.1.call-update) | async-done | bytes 1572880 | tf_op jit(solution)/shard_map/all_gather | solution.py:561
  257.6 4.8 multiply_convert_fusion.1
  263.3 3.0 convolution_convert_fusion.4
  266.4 38.1 %reduce-scatter.9.cloned.1.call-done = bf16[64,1536]{1,0:T(8,128)(2,1)} async-done(((bf16[512,1536]{1,0:T(8,128)(2,1)}), bf16[64,1536]{1,0:T(8,128)(2,1)}) %reduce-scatter.9.cloned.1.call-update) | async-done | bytes 196624 | tf_op jit(solution)/shard_map/reduce_scatter | solution.py:584
  311.7 18.5 %all_to_all.30 = bf16[16,64,128]{2,1,0:T(8,128)(2,1)S(1)} all-to-all(bf16[16,64,128]{2,1,0:T(8,128)(2,1)S(1)} %pad.59), channel_id=1, replica_groups=mesh['outer'=4,'mid'=2,'core'=2,'head'=2] {'outer','mid','core'}, dimensions={0} | all-to-all | bytes 524288 | tf_op jit(solution)/shard_map/all_to_all | solution.py:605
  331.0 12.9 %merge_backward.1 = (f32[1024,128]{1,0:T(8,128)}, f32[1024,128]{1,0:T(8,128)}, f32[1024,128]{1,0:T(8,128)}, f32[1024,128]{1,0:T(8,128)}, f32[1024,128]{1,0:T(8,128)}) custom-call(f32[1024,128]{1,0:T(8,128)} %get-tuple-element.49.own, f32[1024,640]{1,0:T(8,128)} %convolution_add_fusion.1.q_ref.k_ref.h_ref.g_ref.v, f32[1024,128]{1,0:T(8,128)} %get-tuple-element.50.qm, ...), custom_call_target="tpu_custom_call" | custom-call | tf_op jit(solution)/shard_map/merge_backward/pallas_call | solution.py:462
  343.9 11.1 %leaf_backward.1 = bf16[1024,640]{1,0:T(8,128)(2,1)} custom-call(f32[1024,640]{1,0:T(8,128)} %convolution_add_fusion.1.q_ref.k_ref.h_ref.g_ref.v, f32[1024,640]{1,0:T(8,128)} %convolution_add_fusion.1.q_ref.k_ref.h_ref.g_ref.v, f32[1024,640]{1,0:T(8,128)} %convolution_add_fusion.1.q_ref.k_ref.h_ref.g_ref.v, ...), custom_call_target="tpu_custom_call" | custom-call | tf_op jit(solution)/shard_map/leaf_backward/pallas_call | solution.py:374
  355.0 5.6 fusion.3
  361.6 3.6 convolution_convert_fusion.3
  372.4 6.8 %copy.105 = bf16[1536,1536]{1,0:T(8,128)(2,1)} copy(bf16[1536,1536]{0,1:T(8,128)(2,1)} %pad_maximum_fusion) | data formatting | bytes 9437184
  380.5 4.4 convolution_convert_fusion.1
  393.9 5.3 all-to-all-start.4
  399.2 53.9 %reduce-scatter.11.cloned.1.call-done = bf16[64,1536]{1,0:T(8,128)(2,1)} async-done(((bf16[1024,1536]{1,0:T(8,128)(2,1)}), bf16[64,1536]{1,0:T(8,128)(2,1)}) %reduce-scatter.11.cloned.1.call-update) | async-done | bytes 196624 | tf_op jit(solution)/shard_map/reduce_scatter | solution.py:615
  454.2 40.5 %reduce-scatter.7.cloned.1.call-done = bf16[64,1536]{1,0:T(8,128)(2,1)} async-done(((bf16[512,1536]{1,0:T(8,128)(2,1)}), bf16[64,1536]{1,0:T(8,128)(2,1)}) %reduce-scatter.7.cloned.1.call-update) | async-done | bytes 196624 | tf_op jit(solution)/shard_map/reduce_scatter | solution.py:586
  498.3 4.3 collective-permute-done.3
  503.4 79.5 %reduce-scatter.13.cloned.1.call-done = bf16[384,1536]{1,0:T(8,128)(2,1)} async-done(((bf16[1536,1536]{1,0:T(8,128)(2,1)}), bf16[384,1536]{1,0:T(8,128)(2,1)}) %reduce-scatter.13.cloned.1.call-update) | async-done | bytes 1179664 | tf_op jit(solution)/shard_map/reduce_scatter | solution.py:591
  582.9 4.8 all-to-all-start.5
  591.9 11.0 %all-to-all-done.5 = bf16[4,96,1536]{2,1,0:T(8,128)(2,1)} async-done(((bf16[4,96,1536]{2,1,0:T(8,128)(2,1)}), bf16[4,96,1536]{2,1,0:T(8,128)(2,1)}, u32[]{:S(2)}, u32[]{:S(2)}) %all-to-all-start.5) | async-done | bytes 1179680 | tf_op jit(solution)/shard_map/all_to_all | solution.py:592
  (193 shorter events, 86.7 us)
Async XLA Ops:
  7.2 7.2 %copy-start.20 = (bf16[96,6]{0,1:T(8,128)(2,1)S(1)}, bf16[96,6]{0,1:T(8,128)(2,1)}, u32[]{:S(2)}) copy-start(bf16[96,6]{0,1:T(8,128)(2,1)} %param.22) | copy-start | bytes 3460
  7.2 45.8 %all-gather.8.cloned.1.call-start = ((), (), s32[]{:S(2)}) async-start(), calls=%async_computation.10 | async-start | bytes 2506752 | tf_op jit(solution)/shard_map/all_gather | solution.py:559
  7.9 104.5 %all-gather.18.cloned.1.call-start = ((), (), s32[]{:S(2)}) async-start(), calls=%async_computation.18 | async-start | bytes 3342336 | tf_op jit(solution)/shard_map/all_gather | solution.py:525
  14.8 16.5 %collective-permute-start = (bf16[6,112,512]{2,1,0:T(8,128)(2,1)S(1)}, bf16[6,112,512]{2,1,0:T(8,128)(2,1)}, u32[]{:S(2)}, u32[]{:S(2)}) collective-permute-start(bf16[6,112,512]{2,1,0:T(8,128)(2,1)S(1)} %pad.54.clone), channel_id=1, source_target_pairs={{0,1},{1,0},{2,3},{3,2},{4,5},{5,4},{6,7},{7,6},{8,9},{9,8},{10,11... | collective-permute-start | bytes 2064392 | tf_op jit(solution)/shard_map/ppermute | solution.py:494
  18.0 19.2 %all-to-all-start.2 = ((bf16[4,96,1536]{2,1,0:T(8,128)(2,1)}), bf16[4,96,1536]{2,1,0:T(8,128)(2,1)S(1)}, u32[]{:S(2)}, u32[]{:S(2)}) async-start(bf16[4,96,1536]{2,1,0:T(8,128)(2,1)} %copy.90), calls=%async_computation.2 | async-start | bytes 2359296 | tf_op jit(solution)/shard_map/all_to_all | solution.py:556
  22.2 184.6 %all-gather.12.cloned.1.call-start = ((), (), s32[]{:S(2)}) async-start(), calls=%async_computation.12 | async-start | bytes 5898240 | tf_op jit(solution)/shard_map/all_gather | solution.py:557
  42.6 57.8 %all-to-all-start = ((bf16[16,112,512]{2,1,0:T(8,128)(2,1)}), bf16[16,112,512]{2,1,0:T(8,128)(2,1)S(1)}, u32[]{:S(2)}, u32[]{:S(2)}) async-start(bf16[16,112,512]{2,1,0:T(8,128)(2,1)} %copy.87), calls=%async_computation | async-start | bytes 3670016 | tf_op jit(solution)/shard_map/all_to_all | solution.py:535
  48.8 2.8 collective-permute-start.1
  53.0 114.3 %collective-permute-start.2 = (bf16[1536,768]{1,0:T(8,128)(2,1)}, bf16[1536,768]{1,0:T(8,128)(2,1)}, u32[]{:S(2)}, u32[]{:S(2)}) collective-permute-start(bf16[1536,768]{1,0:T(8,128)(2,1)} %all-gather.8.cloned.1.call-done), channel_id=1, source_target_pairs={{0,1},{1,0},{2,3},{3,2},{4,5},{5,4},{6,7},{7,6},{8,9},{9,8},{10,11... | collective-permute-start | bytes 7077896 | tf_op jit(solution)/shard_map/ppermute | solution.py:494
  102.8 17.7 %copy-start.10 = (bf16[16,96,512]{2,1,0:T(8,128)(2,1)}, bf16[16,96,512]{2,1,0:T(8,128)(2,1)S(1)}, u32[]{:S(2)}) copy-start(bf16[16,96,512]{2,1,0:T(8,128)(2,1)S(1)} %slice.132) | copy-start | bytes 4718596
  102.8 12.4 %copy-start.19 = (f32[1536]{0:T(1024)S(1)}, f32[1536]{0:T(1024)}, u32[]{:S(2)}) copy-start(f32[1536]{0:T(1024)} %param.28) | copy-start | bytes 18436
  133.2 33.2 %copy-start = (bf16[1536,768]{1,0:T(8,128)(2,1)S(1)}, bf16[1536,768]{1,0:T(8,128)(2,1)}, u32[]{:S(2)}) copy-start(bf16[1536,768]{1,0:T(8,128)(2,1)} %all-gather.8.cloned.1.call-done) | copy-start | bytes 7077892
  143.1 24.2 %copy-start.3 = (bf16[1,64,1536]{2,1,0:T(8,128)(2,1)S(1)}, bf16[1,64,1536]{2,1,0:T(8,128)(2,1)}, u32[]{:S(2)}) copy-start(bf16[1,64,1536]{2,1,0:T(8,128)(2,1)} %get-tuple-element.75) | copy-start | bytes 589828
  144.9 21.4 %all-to-all-start.1 = ((bf16[16,64,128]{2,1,0:T(8,128)(2,1)}), bf16[16,64,128]{2,1,0:T(8,128)(2,1)S(1)}, u32[]{:S(2)}, u32[]{:S(2)}) async-start(bf16[16,64,128]{2,1,0:T(8,128)(2,1)} %bitcast.7), calls=%async_computation.1 | async-start | bytes 524288 | tf_op jit(solution)/shard_map/all_to_all | solution.py:563
  151.1 85.3 %all-gather.10.cloned.1.call-start = ((), (), s32[]{:S(2)}) async-start(), calls=%async_computation.11 | async-start | bytes 1769472 | tf_op jit(solution)/shard_map/all_gather | solution.py:573
  170.7 86.9 %all-gather.14.cloned.1.call-start = ((), (), s32[]{:S(2)}) async-start(), calls=%async_computation.14 | async-start | bytes 1966080 | tf_op jit(solution)/shard_map/all_gather | solution.py:561
  171.3 133.2 %reduce-scatter.9.cloned.1.call-start = ((), (), s32[]{:S(2)}) async-start(), calls=%async_computation.15 | async-start | bytes 1769472 | tf_op jit(solution)/shard_map/reduce_scatter | solution.py:584
  266.3 39.4 %copy-start.12 = (bf16[2,64,1536]{2,1,0:T(8,128)(2,1)S(1)}, bf16[2,64,1536]{2,1,0:T(8,128)(2,1)}, u32[]{:S(2)}) copy-start(bf16[2,64,1536]{2,1,0:T(8,128)(2,1)} %param.31) | copy-start | bytes 1179652
  266.3 119.1 %all-gather.16.cloned.1.call-start = ((), (), s32[]{:S(2)}) async-start(), calls=%async_computation.17 | async-start | bytes 3342336 | tf_op jit(solution)/shard_map/all_gather | solution.py:606
  307.5 145.5 %reduce-scatter.11.cloned.1.call-start = ((), (), s32[]{:S(2)}) async-start(), calls=%async_computation.16 | async-start | bytes 3342336 | tf_op jit(solution)/shard_map/reduce_scatter | solution.py:615
  343.8 11.2 %copy-start.6 = (bf16[1,1024,1536]{2,1,0:T(8,128)(2,1)S(1)}, bf16[1,1024,1536]{2,1,0:T(8,128)(2,1)}, u32[]{:S(2)}) copy-start(bf16[1,1024,1536]{2,1,0:T(8,128)(2,1)} %all-gather.18.cloned.1.call-done) | copy-start | bytes 9437188
  343.8 11.2 %copy-start.11 = (bf16[16,96,512]{2,1,0:T(8,128)(2,1)S(1)}, bf16[16,96,512]{2,1,0:T(8,128)(2,1)}, u32[]{:S(2)}) copy-start(bf16[16,96,512]{2,1,0:T(8,128)(2,1)} %copy-done.10) | copy-start | bytes 4718596
  343.9 11.2 %copy-start.17 = (bf16[1536,1]{1,0:T(8,128)(2,1)S(1)}, bf16[1536,1]{1,0:T(8,128)(2,1)}, u32[]{:S(2)}) copy-start(bf16[1536,1]{1,0:T(8,128)(2,1)} %reshape_squeeze.10) | copy-start | bytes 9220
  360.6 134.2 %reduce-scatter.7.cloned.1.call-start = ((), (), s32[]{:S(2)}) async-start(), calls=%async_computation.13 | async-start | bytes 1769472 | tf_op jit(solution)/shard_map/reduce_scatter | solution.py:586
  365.2 217.6 %reduce-scatter.13.cloned.1.call-start = ((), (), s32[]{:S(2)}) async-start(), calls=%async_computation.19 | async-start | bytes 5898240 | tf_op jit(solution)/shard_map/reduce_scatter | solution.py:591
  393.9 100.9 %copy-start.9 = (bf16[64,1536]{1,0:T(8,128)(2,1)S(1)}, bf16[64,1536]{1,0:T(8,128)(2,1)}, u32[]{:S(2)}) copy-start(bf16[64,1536]{1,0:T(8,128)(2,1)} %reduce-scatter.9.cloned.1.call-done) | copy-start | bytes 589828
  393.9 100.9 %copy-start.13 = (bf16[2,64,1536]{2,1,0:T(8,128)(2,1)S(1)}, bf16[2,64,1536]{2,1,0:T(8,128)(2,1)}, u32[]{:S(2)}) copy-start(bf16[2,64,1536]{2,1,0:T(8,128)(2,1)} %param.31) | copy-start | bytes 1179652
  393.9 189.0 %all-to-all-start.4 = ((bf16[16,112,640]{2,1,0:T(8,128)(2,1)}), bf16[16,112,640]{2,1,0:T(8,128)(2,1)S(1)}, u32[]{:S(2)}, u32[]{:S(2)}) async-start(bf16[16,112,640]{2,1,0:T(8,128)(2,1)} %fusion.16), calls=%async_computation.7 | async-start | bytes 4587520 | tf_op jit(solution)/shard_map/all_to_all | solution.py:628
  496.8 5.7 collective-permute-start.3
  497.2 92.7 %collective-permute-start.4 = (f32[1,64,1536]{2,1,0:T(8,128)}, f32[1,64,1536]{2,1,0:T(8,128)S(1)}, u32[]{:S(2)}, u32[]{:S(2)}) collective-permute-start(f32[1,64,1536]{2,1,0:T(8,128)} %get-tuple-element.93), channel_id=1, source_target_pairs={{0,1},{1,0},{2,3},{3,2},{4,5},{5,4},{6,7},{7,6},{8,9},{9,8},{10,11... | collective-permute-start | bytes 1179656 | tf_op jit(solution)/shard_map/ppermute | solution.py:494
  582.9 19.9 %all-to-all-start.5 = ((bf16[4,96,1536]{2,1,0:T(8,128)(2,1)}), bf16[4,96,1536]{2,1,0:T(8,128)(2,1)}, u32[]{:S(2)}, u32[]{:S(2)}) async-start(bf16[4,96,1536]{2,1,0:T(8,128)(2,1)} %bitcast.145), calls=%async_computation.8 | async-start | bytes 2359296 | tf_op jit(solution)/shard_map/all_to_all | solution.py:592
  589.5 20.8 %collective-permute-start.5 = (bf16[6,112,640]{2,1,0:T(8,128)(2,1)S(1)}, bf16[6,112,640]{2,1,0:T(8,128)(2,1)S(1)}, u32[]{:S(2)}, u32[]{:S(2)}) collective-permute-start(bf16[6,112,640]{2,1,0:T(8,128)(2,1)S(1)} %scatter.4), channel_id=1, source_target_pairs={{0,1},{1,0},{2,3},{3,2},{4,5},{5,4},{6,7},{7,6},{8,9},{9,8},{10,11... | collective-permute-start | bytes 2580488 | tf_op jit(solution)/shard_map/ppermute | solution.py:494
  (19 other events, 48.5 us)
Sparse Core Ops, SparseCore 0:
  10.3 42.3 all-gather.7
  55.6 56.7 all-gather.17
  114.0 92.6 all-gather.11
  209.1 27.2 all-gather.9
  237.8 19.6 all-gather.13
  266.4 38.0 reduce-scatter.8
  307.6 48.2 all-gather.15
  360.7 92.2 reduce-scatter.10
  456.4 38.3 reduce-scatter.6
  496.9 85.9 reduce-scatter.12

commit v2 on v1

--- a/solution.py
+++ b/solution.py
@@ -362,6 +362,7 @@
         out_specs=[column(0)] * 11,
         out_shape=[matrix(length)] * 11,
         compiler_params=settings(),
+        cost_estimate=cost(1, 1),
         name="leaf_forward",
     )(proj, proj, proj, proj)
 
@@ -378,6 +379,7 @@
         out_specs=pl.BlockSpec((rows, 5 * LEAF), lambda i: (i, 0)),
         out_shape=matrix(length, 5 * LEAF, jnp.bfloat16),
         compiler_params=settings(),
+        cost_estimate=cost(1, 1),
         name="leaf_backward",
     )(proj, proj, proj, proj, *saved, *grads)
 
@@ -433,6 +435,7 @@
         out_shape=outs,
         scratch_shapes=[pltpu.VMEM((length, 1), jnp.float32), pltpu.VMEM((length, 1), jnp.float32), pltpu.VMEM((length, LEAF), jnp.float32)],
         compiler_params=settings(),
+        cost_estimate=cost(1, 1),
         name="merge_forward",
     )(own, proj, qm, km, p, lab_col, lab_row)
 
@@ -467,13 +470,11 @@
         out_shape=[matrix(length)] * 5,
         scratch_shapes=[pltpu.VMEM((length, 1), jnp.float32)] + [pltpu.VMEM(shape, jnp.float32) for shape in gp_shapes(length)],
         compiler_params=settings(),
+        cost_estimate=cost(1, 1),
         name="merge_backward",
     )(*operands)
 
 
-SEQ = ("outer", "mid", "core")
-INNER = ("mid", "core")
-GROUP = ("mid", "core", "head")
 EXTRA = 16
 
 
@@ -490,13 +491,65 @@
     return lax.dot_general(a, b, (dims, ((), ())), preferred_element_type=jnp.float32)
 
 
-def other_head(value):
-    return lax.ppermute(value, "head", [(0, 1), (1, 0)])
-
-
-def by_head(own, other, axis=0):
-    first = lax.axis_index("head") == 0
-    return jnp.concatenate([jnp.where(first, own, other), jnp.where(first, other, own)], axis=axis)
+def after(value, *others):
+    return lax.optimization_barrier((value, *others))[0]
+
+
+def swap(value, axis):
+    return lax.ppermute(value, axis, [(0, 1), (1, 0)])
+
+
+def by_index(own, other, axis, at):
+    first = lax.axis_index(axis) == 0
+    return jnp.stack([jnp.where(first, own, other), jnp.where(first, other, own)], axis=at)
+
+
+def pick(value, at, index):
+    return lax.dynamic_index_in_dim(value, index, at, False)
+
+
+def gather_at(value, at, axis):
+    return by_index(value, swap(value, axis), axis, at)
+
+
+def gathered(value, axes):
+    for at, axis in enumerate(axes):
+        value = gather_at(value, at, axis)
+    return value
+
+
+def exchange_at(value, at, axis):
+    me = lax.axis_index(axis)
+    return by_index(pick(value, at, me), swap(pick(value, at, 1 - me), axis), axis, at)
+
+
+def exchanged(value, axes):
+    for at, axis in enumerate(axes):
+        value = exchange_at(value, at, axis)
+    return value
+
+
+def scattered(value, axes):
+    for at, axis in reversed(list(enumerate(axes))):
+        me = lax.axis_index(axis)
+        total = pick(value, at, me).astype(jnp.float32) + swap(pick(value, at, 1 - me), axis).astype(jnp.float32)
+        value = total if at == 0 else total.astype(value.dtype)
+    return value
+
+
+def scatter_at(value, at, axis):
+    me = lax.axis_index(axis)
+    came = swap(pick(value, at, 1 - me), axis).astype(jnp.float32)
+    return (pick(value, at, me).astype(jnp.float32) + came).astype(value.dtype)
+
+
+def copies(value, axes):
+    return lax.all_to_all(jnp.broadcast_to(value, (lax.axis_size(axes), *value.shape)), axes, 0, 0, tiled=True)
+
+
+def sums(value, axes):
+    value = value.reshape(lax.axis_size(axes), -1, value.shape[-1])
+    return jnp.sum(lax.all_to_all(value, axes, 0, 0, tiled=True).astype(jnp.float32), axis=0)
 
 
 def padded(value, axis, size):
@@ -505,160 +558,303 @@
     return jnp.pad(value, widths)
 
 
+def fence(*values):
+    return lax.optimization_barrier(values)
+
+
+def mlp_kernel(units, cut, act_ref, grad_ref, first_w, second_w, rows_out, hidden_out, part_out):
+    act = act_ref[...]
+    rest = 2 * units - cut
+    first = raw_dot(act, first_w[...], NN)
+    second = raw_dot(act, second_w[:, :rest], NN)
+    gate = first[:, :units]
+    up = jnp.concatenate([first[:, units:], second], axis=1)
+    hidden_grad = raw_dot(grad_ref[...], second_w[:, rest:], NN)
+    sigmoid_gate = jax.nn.sigmoid(gate)
+    silu_gate = gate * sigmoid_gate
+    hidden_out[...] = (silu_gate * up).astype(jnp.bfloat16)
+    rows_out[:, :units] = (hidden_grad * up * sigmoid_gate * (1.0 + gate * (1.0 - sigmoid_gate))).astype(jnp.bfloat16)
+    rows_out[:, units:] = (hidden_grad * silu_gate).astype(jnp.bfloat16)
+    part = raw_dot(rows_out[:, :cut], first_w[...], NT) + raw_dot(rows_out[:, cut:], second_w[:, :rest], NT)
+    part_out[...] = part.astype(jnp.bfloat16)
+
+
+def mlp_of(act, grad, first, second):
+    tokens, width = act.shape
+    units = (first.shape[1] + second.shape[1]) // 3
+    outs = [matrix(tokens, 2 * units, jnp.bfloat16), matrix(tokens, units, jnp.bfloat16), matrix(tokens, width, jnp.bfloat16)]
+    return pl.pallas_call(
+        functools.partial(mlp_kernel, units, first.shape[1]),
+        in_specs=[whole_spec()] * 4,
+        out_specs=[whole_spec()] * 3,
+        out_shape=outs,
+        compiler_params=settings(),
+        cost_estimate=cost(1, 1),
+        name="mlp",
+    )(act, grad, first, second)
+
+
+def mlp_grads_kernel(cuts, act_ref, grad_ref, rows_ref, hidden_ref, first_out, second_out, third_out):
+    both = raw_dot(act_ref[...], rows_ref[...], TN).astype(jnp.bfloat16)
+    down = raw_dot(grad_ref[...], hidden_ref[...], TN).astype(jnp.bfloat16)
+    first_out[...] = both[:, : cuts[0]]
+    second_out[...] = both[:, cuts[0] : cuts[1]]
+    third_out[:, : both.shape[1] - cuts[1]] = both[:, cuts[1] :]
+    third_out[:, both.shape[1] - cuts[1] :] = down
+
+
+def mlp_grads_of(act, grad, rows, hidden):
+    tokens, width = act.shape
+    units = hidden.shape[1]
+    cuts = (3 * units // 4, 15 * units // 8) if units % (8 * LEAF) == 0 else (3 * units // 4, 7 * units // 4)
+    if units % (4 * LEAF):
+        cuts = (units, 2 * units)
+    widths = (cuts[0], cuts[1] - cuts[0], 3 * units - cuts[1])
+    step = 2 * LEAF
+    column = pl.BlockSpec((tokens, step), lambda i: (0, i))
+    return list(pl.pallas_call(
+        functools.partial(mlp_grads_kernel, cuts),
+        grid=(width // step,),
+        in_specs=[column, column, plain_spec(rows.shape), plain_spec(hidden.shape)],
+        out_specs=[pl.BlockSpec((step, w), lambda i: (i, 0)) for w in widths],
+        out_shape=[matrix(width, w, jnp.bfloat16) for w in widths],
+        compiler_params=settings(),
+        cost_estimate=cost(1, 1),
+        name="mlp_grads",
+    )(act, grad, rows, hidden))
+
+
+GRAD_ROWS = 3 * LEAF
+
+
+def pair_grads_kernel(rows, in_ref, grad_ref, weight_ref, gain_ref, out, gain_out):
+    result = raw_dot(in_ref[...], grad_ref[...], TN)
+    beta = result[:, 4 * LEAF :].T[0:1, :]
+    low = result[:, : 4 * LEAF].astype(jnp.bfloat16)
+    bias = jnp.sum(grad_ref[:, 4 * LEAF :].astype(jnp.float32), axis=0, keepdims=True)
+    wide = lambda x: jnp.concatenate([x, jnp.zeros((1, 4 * LEAF - x.shape[1]), jnp.float32)], axis=1)
+    small = jnp.concatenate([wide(beta), wide(bias), jnp.zeros((EXTRA - 2, 4 * LEAF), jnp.float32)], axis=0).astype(jnp.bfloat16)
+    for i in range(GRAD_ROWS // rows):
+        out[i, :rows, :] = low[i * rows : (i + 1) * rows, :]
+        out[i, rows:, :] = small
+    products = jnp.sum(result * weight_ref[...].astype(jnp.float32), axis=1, keepdims=True)
+    gain_out[...] = jnp.broadcast_to(products, (GRAD_ROWS, LEAF)).T[0:1, :] / gain_ref[...]
+
+
+def pair_grads_of(attn_in, proj_grad, weight, gain, rows):
+    length, width = attn_in.shape
+    owners = GRAD_ROWS // rows
+    row = pl.BlockSpec((1, GRAD_ROWS), lambda i: (0, i))
+    return pl.pallas_call(
+        functools.partial(pair_grads_kernel, rows),
+        grid=(width // GRAD_ROWS,),
+        in_specs=[
+            pl.BlockSpec((length, GRAD_ROWS), lambda i: (0, i)),
+            plain_spec(proj_grad.shape),
+            pl.BlockSpec((GRAD_ROWS, weight.shape[1]), lambda i: (i, 0)),
+            row,
+        ],
+        out_specs=[pl.BlockSpec((owners, rows + EXTRA, 4 * LEAF), lambda i: (i, 0, 0)), row],
+        out_shape=[
+            jax.ShapeDtypeStruct((width // rows, rows + EXTRA, 4 * LEAF), jnp.bfloat16),
+            jax.ShapeDtypeStruct((1, width), jnp.float32),
+        ],
+        compiler_params=settings(),
+        cost_estimate=cost(1, 1),
+        name="pair_grads",
+    )(attn_in, proj_grad, weight, gain.reshape(1, width))
+
+
 def local(
-    tokens, w_query, w_key, w_value, w_house, w_beta, beta_bias, w_out, w_gate, w_up, w_down, gain_attn, gain_mlp, segment_ids, out_grad
+    steps, tokens, w_query, w_key, w_value, w_house, w_beta, beta_bias, w_out, w_gate, w_up, w_down, gain_attn, gain_mlp, segment_ids, out_grad
 ):
+    outer_axes, inner_axes = steps[:-2], steps[-2:]
+    group = ("head", *inner_axes)
     low = jnp.bfloat16
     batches, positions, width = tokens.shape
     half = lax.axis_index("head")
-    rank = lax.axis_index(SEQ)
-    count = lax.axis_size(SEQ)
-    inner = lax.axis_size(INNER)
+    rank = lax.axis_index(steps)
+    count = lax.axis_size(steps)
+    inner = lax.axis_size(inner_axes)
     rows, half_heads = w_beta.shape
-    heads = 2 * half_heads
-    assert batches == lax.axis_size("head") and heads <= count
+    assert batches == lax.axis_size("head") == 2 and 2 * half_heads <= count
     length = count * positions
     units = w_gate.shape[1] // inner
+    depth = inner * rows
     scale = LEAF ** (-0.5)
-
-    own_tokens = lax.dynamic_index_in_dim(tokens, half, 0, False)
-    all_tokens = lax.all_gather(own_tokens, SEQ, axis=0, tiled=True)
-    labels = lax.dynamic_index_in_dim(segment_ids, half, 0, False).astype(low)
-    by_heads = [w.reshape(rows, half_heads, LEAF) for w in (w_query, w_key, w_value, w_house)]
-    packed = jnp.concatenate(by_heads, axis=2).transpose(1, 0, 2)
+    by_half = lambda own, other, at=0: by_index(own, other, "head", at)
+
+    def gathered_outer(value):
+        return lax.all_gather(value, outer_axes, axis=0, tiled=True)
+
+    def to_owner(value):
+        return exchanged(value.reshape(2, 2, rows, -1), inner_axes).reshape(inner, rows, -1)
+
+    def outer_sums(value):
+        return lax.psum_scatter(value, outer_axes, scatter_dimension=0, tiled=True)
+
+    micro = lax.axis_index(steps[0])
+    slots = count // 2
+    four = (w_query, w_key, w_value, w_house)
+    packed = jnp.stack(
+        [jnp.concatenate([w[:, i * LEAF : (i + 1) * LEAF] for w in four], axis=1) for i in range(half_heads)]
+    )
     beta_row = padded(w_beta.T[:, None, :], 2, 4 * LEAF)
-    packed = padded(jnp.concatenate([packed, beta_row], axis=1), 1, rows + EXTRA)
-    packed = padded(by_head(packed, other_head(packed)), 0, count)
-    label_row = padded(labels[None], 1, 4 * LEAF)[None]
-    at_row = lax.broadcasted_iota(jnp.int32, (1, rows + EXTRA, 1), 1) == rows + 1
-    packed = jnp.where(at_row, label_row, packed)
-    packed = lax.all_to_all(packed, SEQ, 0, 0, tiled=True)
+    label_row = jnp.broadcast_to(padded(segment_ids.astype(low).reshape(1, 1, -1), 2, 4 * LEAF), (half_heads, 1, 4 * LEAF))
+    packed = padded(padded(jnp.concatenate([packed, beta_row, label_row], axis=1), 1, rows + EXTRA), 0, slots)
+    packed = jnp.broadcast_to(packed[None], (2, *packed.shape)).reshape(count, rows + EXTRA, 4 * LEAF)
+    all_tokens = exchanged(tokens, steps[:1])
+    blocks = [slice(i * units, (i + 1) * units) for i in range(inner)]
+    mlp_own = jnp.stack([jnp.concatenate([w_gate[:, i], w_up[:, i], w_down[i].T], axis=1) for i in blocks])
+    mlp_own = exchanged(mlp_own.reshape(2, 2, rows, 3 * units), inner_axes[:1])
+    out_own = gathered(w_out.T, steps[:1])
+    packed, all_tokens, mlp_own, out_own = fence(packed, all_tokens, mlp_own, out_own)
+
+    packed = lax.all_to_all(packed, steps, 0, 0, tiled=True)
+    all_tokens = lax.all_gather(all_tokens, steps[1:], axis=1, tiled=True).reshape(length, width)
+    all_inputs = all_tokens.astype(jnp.float32)
+    attn_in = (normalize(all_inputs) * gain_attn).astype(low)
+    mlp_own = exchange_at(mlp_own, 1, inner_axes[1]).reshape(depth, 3 * units)
+    for at in range(1, len(outer_axes)):
+        out_own = by_index(out_own, swap(out_own, steps[at]), steps[at], at)
+    packed, attn_in, mlp_own, out_own = fence(packed, attn_in, mlp_own, out_own)
+
     weight = packed[:, :rows].reshape(width, 4 * LEAF)
     beta_column = padded(packed[:, rows, :rows].reshape(width, 1), 1, LEAF)
     weight = jnp.concatenate([weight, beta_column], axis=1)
-    label_all = packed[:, rows + 1, :positions].reshape(1, length).astype(jnp.float32)
+    label_all = pick(packed[:, rows + 1, : 2 * positions].reshape(count, 2, positions), 1, micro)
+    label_all = label_all.reshape(1, length).astype(jnp.float32)
     label_column = jnp.broadcast_to(label_all.reshape(length, 1), (length, LEAF))
-    bias_all = padded(by_head(beta_bias, other_head(beta_bias)), 0, count)
-    bias_row = padded(lax.dynamic_slice(bias_all, (rank,), (1,)), 0, LEAF)
+    bias_row = padded(lax.dynamic_slice(padded(beta_bias, 0, slots), (rank % slots,), (1,)), 0, LEAF)
     bias_row = jnp.concatenate([jnp.zeros(4 * LEAF, jnp.float32), bias_row])
-
-    all_inputs = all_tokens.astype(jnp.float32)
-    attn_in = (normalize(all_inputs) * gain_attn).astype(low)
+    cut = 5 * units // 4
+    first_weight = gathered_outer(mlp_own[:, :cut])
     proj = dot(attn_in, weight) + bias_row
+    proj, out_own, grad_group = fence(proj, out_own, out_grad)
+
+    out_own = gather_at(out_own, len(outer_axes), inner_axes[0])
     *saved, own_logits, query_moved, key_moved, product = leaf_forward(proj)
+    own_logits, out_own, grad_group = fence(own_logits, out_own, grad_group)
+
+    out_own = gather_at(out_own, len(outer_axes) + 1, inner_axes[1])
+    grad_group = gather_at(grad_group, 1, inner_axes[0])
     attended, log_total, *levels = run_merge_forward(
         proj, own_logits, query_moved, key_moved, product, label_column, label_all, scale
     )
     attended_low = attended.astype(low)
-
-    blocks = [w.reshape(rows, inner, units) for w in (w_gate, w_up, w_down.T)]
-    mlp_weight = jnp.concatenate(blocks, axis=2).transpose(1, 0, 2)
-    mlp_weight = lax.all_to_all(mlp_weight, INNER, 0, 0, tiled=True).reshape(inner * rows, 3 * units)
-    mlp_weight = lax.all_gather(mlp_weight, "outer", axis=0, tiled=True)
-    gate_up_weight, down_weight = mlp_weight[:, : 2 * units], mlp_weight[:, 2 * units :]
-    out_own = lax.all_gather(w_out.T, SEQ, axis=0, tiled=True)
-    out_other = other_head(out_own)
-    grad_group = lax.all_gather(out_grad, INNER, axis=0, tiled=True).reshape(-1, width)
-
-    heads_here = lax.all_to_all(attended_low.reshape(count, positions, LEAF), SEQ, 0, 0, tiled=True)
-    heads_here = heads_here[:heads].reshape(2, half_heads, positions, LEAF).transpose(0, 2, 1, 3)
-    heads_here = heads_here.reshape(2, positions, half_heads * LEAF)
-    branch = dot(lax.dynamic_index_in_dim(heads_here, half, 0, False), out_own, NT)
-    branch = branch + dot(lax.dynamic_index_in_dim(heads_here, 1 - half, 0, False), out_other, NT)
-    inputs = own_tokens.astype(jnp.float32)
+    attended_low, out_own, grad_group, first_weight, mlp_own = fence(attended_low, out_own, grad_group, first_weight, mlp_own)
+    out_own = out_own.reshape(width, half_heads * LEAF)
+
+    second_weight = gathered_outer(mlp_own[:, cut:])
+    grad_group = gather_at(grad_group, 2, inner_axes[1]).reshape(-1, width)
+    heads_here = lax.all_to_all(attended_low.reshape(count, positions, LEAF), steps, 0, 0, tiled=True)
+    heads_here = heads_here.reshape(2, slots, positions, LEAF)[:, :half_heads].transpose(0, 2, 1, 3)
+    heads_here = heads_here.reshape(2 * positions, half_heads * LEAF)
+    branch = dot(heads_here, out_own, NT).reshape(2, positions, width)
+    branch = pick(branch, 0, half) + swap(pick(branch, 0, 1 - half), "head")
+    inputs = pick(tokens, 0, half).astype(jnp.float32)
     middle = inputs + branch
     normed_two = normalize(middle)
     mlp_in = (normed_two * gain_mlp).astype(low)
-
-    mlp_group = lax.all_gather(mlp_in, GROUP, axis=0, tiled=True)
-    gate_up = dot(mlp_group, gate_up_weight)
-    gate, up = gate_up[:, :units], gate_up[:, units:]
-    sigmoid_gate = jax.nn.sigmoid(gate)
-    silu_gate = gate * sigmoid_gate
-    hidden = (silu_gate * up).astype(low)
-    hidden_grad = dot(grad_group, down_weight)
-    gate_rows = (hidden_grad * up * sigmoid_gate * (1.0 + gate * (1.0 - sigmoid_gate))).astype(low)
-    up_rows = (hidden_grad * silu_gate).astype(low)
-    rows_grad = jnp.concatenate([gate_rows, up_rows], axis=1)
-    mlp_in_part = dot(rows_grad, gate_up_weight, NT).astype(low)
-    mlp_in_grad = lax.psum_scatter(mlp_in_part, GROUP, scatter_dimension=0, tiled=True).astype(jnp.float32)
-    mlp_part = dot(hidden, down_weight, NT).astype(low)
-    mlp_branch = lax.psum_scatter(mlp_part, GROUP, scatter_dimension=0, tiled=True).astype(jnp.float32)
-    block_out = (middle + mlp_branch).astype(low)[None]
-    block_out = by_head(block_out, other_head(block_out))
-
-    mlp_grads = jnp.concatenate([dot(mlp_group, rows_grad, TN), dot(grad_group, hidden, TN)], axis=1).astype(low)
-    mlp_grads = lax.psum_scatter(mlp_grads, "outer", scatter_dimension=0, tiled=True)
-    mlp_grads = lax.all_to_all(mlp_grads.reshape(inner, rows, 3 * units), INNER, 0, 0, tiled=True).astype(jnp.float32)
-    gate_grad, up_grad, down_grad = (
-        mlp_grads[:, :, i * units : (i + 1) * units].transpose(1, 0, 2).reshape(rows, inner * units) for i in range(3)
-    )
-    down_grad = down_grad.T
-
+    mlp_group = copies(mlp_in, group).reshape(-1, width)
+    columns = heads_here.reshape(2 * positions, inner, -1).transpose(1, 0, 2)
+    columns = columns.reshape(2, 2, 2 * positions, -1)
+    mlp_group, second_weight, grad_group = fence(mlp_group, second_weight, grad_group)
+
+    rows_grad, hidden, mlp_in_part = mlp_of(mlp_group, grad_group, first_weight, second_weight)
+    mlp_in_grad = sums(mlp_in_part, group)
+    mlp_grads = mlp_grads_of(mlp_group, grad_group, rows_grad, hidden)
+    mlp_grads[0] = outer_sums(mlp_grads[0])
+    mlp_part = dot(hidden, second_weight[:, 2 * units - cut :], NT).astype(low)
+    columns = exchange_at(after(columns, mlp_grads[2]), 0, inner_axes[0])
+    mlp_in_grad, mlp_part, columns, *mlp_grads = fence(mlp_in_grad, mlp_part, columns, *mlp_grads)
+
+    mlp_grads[1] = outer_sums(mlp_grads[1])
+    mlp_grads[0] = to_owner(mlp_grads[0])
+    mlp_part = scattered(mlp_part.reshape(2, 2, 2, positions, width), ("head",)).astype(low)
     mlp_gain_part = jnp.sum(mlp_in_grad * normed_two, axis=0)
-    own_grad = lax.dynamic_index_in_dim(out_grad, half, 0, False).astype(jnp.float32)
+    own_grad = pick(out_grad, 0, half).astype(jnp.float32)
     middle_grad = own_grad + norm_back(mlp_in_grad * gain_mlp, normed_two, middle)
     branch_low = middle_grad.astype(low)
-    attended_grad = by_head(dot(branch_low, out_own).astype(low)[None], dot(branch_low, out_other).astype(low)[None])
+    branch_low = by_half(branch_low, swap(branch_low, "head"))
+    attended_grad = dot(branch_low.reshape(2 * positions, width), out_own).astype(low)
     attended_grad = attended_grad.reshape(2, positions, half_heads, LEAF).transpose(0, 2, 1, 3)
-    attended_grad = padded(attended_grad.reshape(heads, positions, LEAF), 0, count)
-    attended_grad = lax.all_to_all(attended_grad, SEQ, 0, 0, tiled=True).reshape(length, LEAF).astype(jnp.float32)
-    branch_all = lax.all_gather(branch_low, SEQ, axis=0, tiled=True)
-
+    attended_grad = padded(attended_grad, 1, slots).reshape(count, positions, LEAF)
+    attended_grad = lax.all_to_all(attended_grad, steps, 0, 0, tiled=True).reshape(length, LEAF).astype(jnp.float32)
+    branch_group = gather_at(gather_at(branch_low, 1, inner_axes[0]), 2, inner_axes[1]).reshape(-1, width)
+    columns = exchange_at(columns, 1, inner_axes[1]).reshape(inner, 2, positions, -1)
+    columns = columns.swapaxes(0, 1).reshape(-1, columns.shape[-1])
+    attended_grad, branch_group, columns, mlp_part, *mlp_grads = fence(attended_grad, branch_group, columns, mlp_part, *mlp_grads)
+
+    mlp_grads[2] = outer_sums(mlp_grads[2])
+    mlp_grads[1] = exchange_at(mlp_grads[1].reshape(2, 2, rows, -1), 0, inner_axes[0])
+    mlp_part = scattered(mlp_part.swapaxes(0, 1), inner_axes[1:]).astype(low)
+    out_weight_grad = dot(branch_group, columns, TN).astype(low).reshape(count, rows, -1)
+    attended_grad = after(attended_grad, out_weight_grad)
+    out_weight_grad = lax.all_to_all(out_weight_grad, steps, 0, 0, tiled=True)
     merged = run_merge_backward(
         proj, own_logits, query_moved, key_moved, product, levels, label_column, label_all, attended, log_total, attended_grad, scale
     )
+    mlp_part, mlp_grads[1], *merged = fence(mlp_part, mlp_grads[1], *merged)
+
+    mlp_grads[1] = exchange_at(mlp_grads[1], 1, inner_axes[1]).reshape(inner, rows, -1)
+    mlp_part = scattered(mlp_part, inner_axes[:1])
     proj_grad = leaf_backward(proj, saved, merged)
-
-    attn_in_part = dot(proj_grad, weight, NT)
-    attn_gain_part = jnp.sum(attn_in_part * normalize(all_inputs), axis=0)
-    attn_in_grad = lax.psum_scatter(attn_in_part.astype(low), SEQ, scatter_dimension=0, tiled=True).astype(jnp.float32)
-
-    weight_grad = dot(attn_in, proj_grad, TN)
-    out_weight = dot(branch_all, attended_low, TN)
-    bias_part = jnp.sum(proj_grad[:, 4 * LEAF :].astype(jnp.float32), axis=0)
-    span = 5 * LEAF
-    main = jnp.concatenate([weight_grad[:, : 4 * LEAF], out_weight], axis=1).reshape(count, rows, span)
-    beta_rows = padded(weight_grad[:, 4 * LEAF].reshape(count, 1, rows), 2, span)
-    gains = jnp.concatenate([attn_gain_part, mlp_gain_part]).reshape(-1, 4 * LEAF)
-    gain_rows = gains.shape[0]
-    small = jnp.concatenate([padded(gains, 1, span), padded(bias_part[None], 1, span)], axis=0)
-    small = jnp.broadcast_to(padded(small, 0, EXTRA - 1), (count, EXTRA - 1, span))
-    packed_grad = jnp.concatenate([main, beta_rows, small], axis=1).astype(low)
-    packed_grad = lax.all_to_all(packed_grad, SEQ, 0, 0, tiled=True)
-    gain_sums = jnp.sum(packed_grad[:, rows + 1 : rows + 1 + gain_rows].astype(jnp.float32), axis=0)
-    gain_sums = lax.reduce_precision(gain_sums, 8, 7)
-    by_half = packed_grad[:heads].reshape(2, half_heads, rows + EXTRA, span)
-    kept = lax.dynamic_index_in_dim(by_half, half, 0, False)
-    sent = lax.dynamic_index_in_dim(by_half, 1 - half, 0, False)
-    sent = sent.at[:, rows + 1 : rows + 1 + gain_rows].set(gain_sums.astype(low)[None])
-    came = other_head(sent)
-    sums = kept.astype(jnp.float32) + came.astype(jnp.float32)
-    gain_sums = gain_sums + came[0, rows + 1 : rows + 1 + gain_rows].astype(jnp.float32)
-    gain_sums = gain_sums[:, : 4 * LEAF].reshape(2, width)
-    grads = [
-        sums[:, :rows, i * LEAF : (i + 1) * LEAF].transpose(1, 0, 2).reshape(rows, half_heads * LEAF) for i in range(4)
-    ]
-    out_weight_grad = sums[:, :rows, 4 * LEAF :].transpose(0, 2, 1).reshape(half_heads * LEAF, rows)
-    beta_grad = sums[:, rows, :rows].T
-    bias_grad = sums[:, rows + 1 + gain_rows, 0]
-
-    tokens_grad = (middle_grad + norm_back(attn_in_grad * gain_attn, normalize(inputs), inputs))[None]
-    tokens_grad = by_head(tokens_grad, other_head(tokens_grad))
+    proj_grad, mlp_part, out_weight_grad, *mlp_grads = fence(proj_grad, mlp_part, out_weight_grad, *mlp_grads)
+
+    packed_grad, attn_gain_part = pair_grads_of(attn_in, proj_grad, weight, gain_attn, rows)
+    attn_in_part = dot(after(proj_grad, packed_grad), weight, NT)
+    packed_grad = lax.all_to_all(packed_grad, steps, 0, 0, tiled=True)
+    attn_in_part = attn_in_part.astype(low).reshape(2, *(2,) * (len(steps) - 1), positions, width)
+    for at in range(len(steps) - 1, 0, -1):
+        attn_in_part = scatter_at(attn_in_part, at, steps[at])
+        if at == len(outer_axes):
+            mlp_grads[2] = after(mlp_grads[2], attn_in_part)
+    attn_in_part = exchanged(attn_in_part, steps[:1])
+    attn_in_grad = scattered(attn_in_part, ("head",))
+
+    block_out = (middle + mlp_part).astype(low)
+    block_out = by_half(block_out, swap(block_out, "head"))
+    mlp_grads[2] = to_owner(mlp_grads[2])
+    mlp_grads = jnp.concatenate(mlp_grads, axis=2).astype(jnp.float32)
+    gate_grad, up_grad = (
+        mlp_grads[:, :, i * units : (i + 1) * units].transpose(1, 0, 2).reshape(rows, inner * units) for i in range(2)
+    )
+    down_grad = mlp_grads[:, :, 2 * units :].transpose(0, 2, 1).reshape(inner * units, rows)
+    out_weight_grad = jnp.sum(out_weight_grad.reshape(-1, inner, rows, out_weight_grad.shape[-1]).astype(jnp.float32), axis=0)
+    out_weight_grad = out_weight_grad.transpose(0, 2, 1).reshape(-1, rows)
+
+    gains = jnp.stack([attn_gain_part[0], mlp_gain_part])
+    gains = after(gains, packed_grad)
+    for axis in (*steps, "head"):
+        gains = gains + swap(gains, axis)
+    small = after(packed_grad[:, rows : rows + 2], gains)
+    small = jnp.sum(small.reshape(2, slots, 2, -1)[:, :half_heads].astype(jnp.float32), axis=0)
+    turn = rank % (GRAD_ROWS // rows) * rows
+    beta_grad = lax.dynamic_slice(small[:, 0], (0, turn), (half_heads, rows)).T
+    bias_grad = small[:, 1, 0]
+    total = packed_grad[:, :rows].reshape(2, slots, rows, -1)[:, :half_heads].astype(jnp.float32)
+    total = total[0] + total[1]
+    grads = [total[..., i * LEAF : (i + 1) * LEAF].transpose(1, 0, 2).reshape(rows, half_heads * LEAF) for i in range(4)]
+
+    tokens_grad = middle_grad + norm_back(attn_in_grad * gain_attn, normalize(inputs), inputs)
+    tokens_grad = by_half(tokens_grad, swap(tokens_grad, "head"))
     return (
-        block_out, tokens_grad, *grads, beta_grad, bias_grad, out_weight_grad, gate_grad, up_grad, down_grad, gain_sums[0], gain_sums[1]
+        block_out, tokens_grad, *grads, beta_grad, bias_grad, out_weight_grad, gate_grad, up_grad, down_grad, gains[0], gains[1]
     )
 
 
 def solution(mesh):
-    inner = (2, 2)
-    fine = Mesh(mesh.devices.reshape(-1, *inner, mesh.shape["head"]), (*SEQ, "head"))
-    split_rows, split_columns, by_position = P(SEQ, "head"), P("head", SEQ), P(None, SEQ, None)
+    depth = mesh.shape["seq"].bit_length() - 1
+    assert mesh.shape["seq"] == 2**depth and mesh.shape["head"] == 2
+    steps = tuple(f"s{i}" for i in range(depth))
+    fine = Mesh(mesh.devices.reshape(*(2,) * depth, 2), (*steps, "head"))
+    split_rows, split_columns, by_position = P(steps, "head"), P("head", steps), P(None, steps, None)
     placed = (
         (by_position,) + (split_rows,) * 5 + (P("head"), split_columns, split_rows, split_rows, split_columns)
-        + (P(), P(), P(None, SEQ), by_position)
+        + (P(), P(), P(None, steps), by_position)
     )
     returned = (
         (by_position, by_position) + (split_rows,) * 5 + (P("head"), split_columns, split_rows, split_rows, split_columns, P(), P())
     )
-    return jax.shard_map(local, mesh=fine, in_specs=placed, out_specs=returned, check_vma=False)
+    return jax.shard_map(functools.partial(local, steps), mesh=fine, in_specs=placed, out_specs=returned, check_vma=False)

time: 630 us -> 489 us (0.78)
  waiting for transfers between devices: 397 us -> 193 us
  starting transfers between devices: 32 us -> 88.1 us
  matrix products: 46.2 us -> 15.9 us
  Pallas kernels: 45.6 us -> 70.2 us
  blocking collectives: 18.5 us -> 0 us
  other arithmetic: 30.1 us -> 47.3 us
  local copies, waits for them, and re-layouts: 38.3 us -> 50.4 us
    reduce_scatter x4 -> x3, waiting for transfers between devices: 212 us -> 4.27 us  [outer_sums(): return lax.psum_scatter(value, outer_axes, scatter_dimension=0, tiled=True)]
    ppermute x6 -> x36, waiting for transfers between devices: 17.6 us -> 137 us  [swap(): return lax.ppermute(value, axis, [(0, 1), (1, 0)])]
    all_gather x6 -> x3, waiting for transfers between devices: 90.4 us -> 3.14 us  [the longest x2 3.14 us: gathered_outer(): return lax.all_gather(value, outer_axes, axis=0, tiled=True)]
    ppermute x6 -> x36, starting transfers between devices: 4.68 us -> 42.6 us  [swap(): return lax.ppermute(value, axis, [(0, 1), (1, 0)])]
    dot_general x14 -> x6, matrix products: 46.2 us -> 15.9 us  [dot(): lax.dot_general(a, b, (dims, ((), ())), preferred_element_type=jnp.float32)]
    all_to_all x5 -> x7, waiting for transfers between devices: 75.5 us -> 48.5 us  [the longest x1 14.6 us: copies(): lax.all_to_all(jnp.broadcast_to(value, (lax.axis_size(axes), *value.shape...]
    pallas_call x0 -> x3, Pallas kernels: none -> 25.3 us  [the longest x1 10.9 us: mlp_of(): pl.pallas_call(functools.partial(mlp_kernel, units, first.shape[1]), in_s...]
    another operation x0 -> x48, other arithmetic: none -> 20.8 us  [the longest x43 20.6 us: by_index(): jnp.stack([jnp.where(first, own, other), jnp.where(first, other, own)], a...]
  transfers between devices with their start and end apart: 21 -> 49, of which waited for: 16 -> 26; matrix products, arithmetic and copies ran while one was open for 15% -> 19% of each run, Pallas kernels for 7% -> 9%
where the time goes in v2:
time: 489 us; the launch traced here: 480 us
  waiting for transfers between devices  193 us (39%)
  starting transfers between devices  88.1 us (18%)
  Pallas kernels  70.2 us (14%)
  local copies, waits for them, and re-layouts  50.4 us (10%)
  other arithmetic  47.3 us (10%)
  matrix products  15.9 us (3%)
  between operations  15.6 us (3%)
    ppermute x36, waiting for transfers between devices, swap(): return lax.ppermute(value, axis, [(0, 1), (1, 0)])  137 us
    ppermute x36, starting transfers between devices, swap(): return lax.ppermute(value, axis, [(0, 1), (1, 0)])  42.6 us
    another operation x43, other arithmetic, by_index(): jnp.stack([jnp.where(first, own, other), jnp.where(first, other, own)], a...  20.6 us
    dot_general x6, matrix products, dot(): lax.dot_general(a, b, (dims, ((), ())), preferred_element_type=jnp.float32)  15.9 us
    all_to_all x1, waiting for transfers between devices, copies(): lax.all_to_all(jnp.broadcast_to(value, (lax.axis_size(axes), *value.shape...  14.6 us
    pallas_call x1, Pallas kernels, run_merge_backward(): pl.pallas_call(functools.partial(merge_backward_kernel, length, scale), g...  12.9 us
    all_to_all x1, waiting for transfers between devices, local(): lax.all_to_all(attended_low.reshape(count, positions, LEAF), steps, 0, 0,...  12.7 us
    pallas_call x1, Pallas kernels, leaf_forward(): pl.pallas_call(functools.partial(leaf_forward_kernel, leaves), grid=(leng...  11.3 us
  transfers between devices with their start and end apart: 49, of which 26 were waited for; matrix products, arithmetic and copies ran while one was open for 19% of the time, Pallas kernels for 9%

profile of v2, /device:TPU:21, one launch (start us, length us, event | category | flops | bytes accessed | tf_op | source)
XLA Modules:
  0.0 480.1 jit_solution(16717431795556217728)
XLA Ops:
  15.7 7.5 %collective-permute-done.2 = bf16[96,768]{1,0:T(8,128)(2,1)S(1)} collective-permute-done((bf16[96,768]{1,0:T(8,128)(2,1)S(1)}, bf16[96,768]{1,0:T(8,128)(2,1)S(1)}, u32[]{:S(2)}, u32[]{:S(2)}) %collective-permute-start.2) | collective-permute-done | bytes 147488 | tf_op jit(solution)/shard_map/ppermute | solution.py:499
  28.3 9.8 %all-to-all-start = ((bf16[16,112,512]{2,1,0:T(8,128)(2,1)}), bf16[16,112,512]{2,1,0:T(8,128)(2,1)}, u32[]{:S(2)}, u32[]{:S(2)}) async-start(bf16[16,112,512]{2,1,0:T(8,128)(2,1)} %bitcast.9), calls=%async_computation | async-start | bytes 3670016 | tf_op jit(solution)/shard_map/all_to_all | solution.py:713
  41.4 47.8 %collective-permute-done.4 = bf16[2,96,768]{2,1,0:T(8,128)(2,1)} collective-permute-done((bf16[2,96,768]{2,1,0:T(8,128)(2,1)S(1)}, bf16[2,96,768]{2,1,0:T(8,128)(2,1)}, u32[]{:S(2)}, u32[]{:S(2)}) %collective-permute-start.4) | collective-permute-done | bytes 294944 | tf_op jit(solution)/shard_map/ppermute | solution.py:499
  102.9 5.6 %convolution_add_fusion.q_ref.k_ref.h_ref.g_ref.v = f32[1024,640]{1,0:T(8,128)} fusion(bf16[1024,1536]{1,0:T(8,128)(2,1)S(1)} %fusion.1.in_ref, f32[640]{0:T(1024)S(1)} %pad.140, bf16[1536,1]{1,0:T(8,128)(2,1)S(1)} %reshape_squeeze.8, bf16[1536,512]{1,0:T(8,128)(2,1)} %bitcast.443), kind=kOutput, calls=%fused_computation.16 | convolution fusion | flops 2019819520 | bytes 7345664 | tf_op jit(solution)/shard_map/dot_general | solution.py:491
  109.5 11.3 %leaf_forward.1 = (f32[1024,128]{1,0:T(8,128)}, f32[1024,128]{1,0:T(8,128)}, f32[1024,128]{1,0:T(8,128)}, f32[1024,128]{1,0:T(8,128)}, f32[1024,128]{1,0:T(8,128...) custom-call(f32[1024,640]{1,0:T(8,128)} %convolution_add_fusion.q_re, ...), custom_call_target="tpu_custom_call" | custom-call | flops 1 | bytes 1 | tf_op jit(solution)/shard_map/leaf_forward/pallas_call | solution.py:358
  129.4 9.7 %merge_forward.1 = (f32[1024,128]{1,0:T(8,128)}, f32[1024,128]{1,0:T(8,128)}, f32[1024,128]{1,0:T(8,128)}, f32[1024,128]{1,0:T(8,128)}, f32[512,128]{1,0:T(8,128...) custom-call(f32[1024,128]{1,0:T(8,128)} %get-tuple-element.110.own, ...), custom_call_target="tpu_custom_call" | custom-call | flops 1 | bytes 1 | tf_op jit(solution)/shard_map/merge_forward/pallas_call | solution.py:430
  147.3 5.9 %all-to-all-start.1 = ((bf16[16,64,128]{2,1,0:T(8,128)(2,1)}), bf16[16,64,128]{2,1,0:T(8,128)(2,1)S(1)}, u32[]{:S(2)}, u32[]{:S(2)}) async-start(bf16[16,64,128]{2,1,0:T(8,128)(2,1)} %bitcast.51), calls=%async_computation.1 | async-start | bytes 524288 | tf_op jit(solution)/shard_map/all_to_all | solution.py:750
  153.2 12.7 %all-to-all-done.1 = bf16[16,64,128]{2,1,0:T(8,128)(2,1)S(1)} async-done(((bf16[16,64,128]{2,1,0:T(8,128)(2,1)}), bf16[16,64,128]{2,1,0:T(8,128)(2,1)S(1)}, u32[]{:S(2)}, u32[]{:S(2)}) %all-to-all-start.1) | async-done | bytes 262176 | tf_op jit(solution)/shard_map/all_to_all | solution.py:750
  169.7 7.2 %collective-permute-done.8 = f32[64,1536]{1,0:T(8,128)} collective-permute-done((f32[64,1536]{1,0:T(8,128)S(1)}, f32[64,1536]{1,0:T(8,128)}, u32[]{:S(2)}, u32[]{:S(2)}) %collective-permute-start.8) | collective-permute-done | bytes 393248 | tf_op jit(solution)/shard_map/ppermute | solution.py:499
  180.5 6.9 %all-to-all-start.2 = ((bf16[8,64,1536]{2,1,0:T(8,128)(2,1)}), bf16[8,64,1536]{2,1,0:T(8,128)(2,1)}, u32[]{:S(2)}, u32[]{:S(2)}) async-start(bf16[8,64,1536]{2,1,0:T(8,128)(2,1)} %broadcast_in_dim.19), calls=%async_computation.2 | async-start | bytes 3145728 | tf_op jit(solution)/shard_map/all_to_all | solution.py:547
  190.1 14.6 %all-to-all-done.2 = bf16[8,64,1536]{2,1,0:T(8,128)(2,1)} async-done(((bf16[8,64,1536]{2,1,0:T(8,128)(2,1)}), bf16[8,64,1536]{2,1,0:T(8,128)(2,1)}, u32[]{:S(2)}, u32[]{:S(2)}) %all-to-all-start.2) | async-done | bytes 1572896 | tf_op jit(solution)/shard_map/all_to_all | solution.py:547
  204.9 10.9 %mlp.1 = (bf16[512,1024]{1,0:T(8,128)(2,1)}, bf16[512,512]{1,0:T(8,128)(2,1)}, bf16[512,1536]{1,0:T(8,128)(2,1)}) custom-call(bf16[512,1536]{1,0:T(8,128)(2,1)} %bitcast.59.act_ref, bf16[512,1536]{1,0:T(8,128)(2,1)} %bitcast.440, bf16[1536,640]{1,0:T(8,128)(2,1)} %all-gather.6.cloned.1.call-done.first_w, bf16[1536,896]{1,0:T(8,128)(2,1)} %all-gather.8.cloned.1.call-done.second_w), custom_call_target="tpu_custom_call" | custom-call | flops 1 | bytes 1 | tf_op jit(solution)/shard_map/mlp/pallas_call | solution.py:586
  215.9 7.1 %mlp_grads.1 = (bf16[1536,384]{1,0:T(8,128)(2,1)}, bf16[1536,512]{1,0:T(8,128)(2,1)}, bf16[1536,640]{1,0:T(8,128)(2,1)}) custom-call(bf16[512,1536]{1,0:T(8,128)(2,1)} %bitcast.59.act_ref, bf16[512,1536]{1,0:T(8,128)(2,1)} %bitcast.441, bf16[512,1024]{1,0:T(8,128)(2,1)} %get-tuple-element.135.rows_ref, bf16[512,512]{1,0:T(8,128)(2,1)} %get-tuple-element.134.hidden_ref), custom_call_target="tpu_custom_call" | custom-call | flops 1 | bytes 1 | tf_op jit(solution)/shard_map/mlp_grads/pallas_call | solution.py:615
  223.0 8.0 %all-to-all-start.3 = ((bf16[8,64,1536]{2,1,0:T(8,128)(2,1)}), bf16[8,64,1536]{2,1,0:T(8,128)(2,1)}, u32[]{:S(2)}, u32[]{:S(2)}) async-start(bf16[8,64,1536]{2,1,0:T(8,128)(2,1)} %bitcast.455), calls=%async_computation.3 | async-start | bytes 3145728 | tf_op jit(solution)/shard_map/all_to_all | solution.py:552
  233.0 3.8 convolution_convert_fusion.1
  236.7 15.5 %collective-permute-done.10 = bf16[2,128,192]{1,2,0:T(8,128)(2,1)S(1)} collective-permute-done((bf16[2,128,192]{1,2,0:T(8,128)(2,1)S(1)}, bf16[2,128,192]{1,2,0:T(8,128)(2,1)S(1)}, u32[]{:S(2)}, u32[]{:S(2)}) %collective-permute-start.10) | collective-permute-done | bytes 98336 | tf_op jit(solution)/shard_map/ppermute | solution.py:499
  276.6 5.1 %all-to-all-start.4 = ((bf16[16,64,128]{2,1,0:T(8,128)(2,1)}), bf16[16,64,128]{2,1,0:T(8,128)(2,1)S(1)}, u32[]{:S(2)}, u32[]{:S(2)}) async-start(bf16[16,64,128]{2,1,0:T(8,128)(2,1)} %bitcast.74), calls=%async_computation.5 | async-start | bytes 524288 | tf_op jit(solution)/shard_map/all_to_all | solution.py:783
  286.8 11.0 %all-to-all-done.4 = bf16[16,64,128]{2,1,0:T(8,128)(2,1)S(1)} async-done(((bf16[16,64,128]{2,1,0:T(8,128)(2,1)}), bf16[16,64,128]{2,1,0:T(8,128)(2,1)S(1)}, u32[]{:S(2)}, u32[]{:S(2)}) %all-to-all-start.4) | async-done | bytes 262176 | tf_op jit(solution)/shard_map/all_to_all | solution.py:783
  313.9 4.8 all-to-all-start.5
  318.7 12.9 %merge_backward.1 = (f32[1024,128]{1,0:T(8,128)}, f32[1024,128]{1,0:T(8,128)}, f32[1024,128]{1,0:T(8,128)}, f32[1024,128]{1,0:T(8,128)}, f32[1024,128]{1,0:T(8,128)}) custom-call(f32[1024,128]{1,0:T(8,128)} %get-tuple-element.110.own, f32[1024,640]{1,0:T(8,128)} %convolution_add_fusion.q_ref.k_ref.h_ref.g_ref.v, f32[1024,128]{1,0:T(8,128)} %get-tuple-element.111.qm, ...), custom_call_target="tpu_custom_call" | custom-call | flops 1 | bytes 1 | tf_op jit(solution)/shard_map/merge_backward/pallas_call | solution.py:465
  335.6 11.1 %leaf_backward.1.grad_ref = bf16[1024,640]{1,0:T(8,128)(2,1)} custom-call(f32[1024,640]{1,0:T(8,128)} %convolution_add_fusion.q_ref.k_ref.h_ref.g_ref.v, f32[1024,640]{1,0:T(8,128)} %convolution_add_fusion.q_ref.k_ref.h_ref.g_ref.v, f32[1024,640]{1,0:T(8,128)} %convolution_add_fusion.q_ref.k_ref.h_ref.g_ref.v, ...), custom_call_target="tpu_custom_call" | custom-call | flops 1 | bytes 1 | tf_op jit(solution)/shard_map/leaf_backward/pallas_call | solution.py:375
  348.3 10.1 %all-to-all-done.5 = bf16[16,96,192]{1,2,0:T(8,128)(2,1)S(1)} async-done(((bf16[16,96,192]{1,2,0:T(8,128)(2,1)}), bf16[16,96,192]{1,2,0:T(8,128)(2,1)S(1)}, u32[]{:S(2)}, u32[]{:S(2)}) %all-to-all-start.5) | async-done | bytes 589856 | tf_op jit(solution)/shard_map/all_to_all | solution.py:794
  358.4 3.4 reduce-scatter.8.cloned.1.call-done
  361.9 7.2 %pair_grads.1 = (bf16[16,112,512]{2,1,0:T(8,128)(2,1)}, f32[1,1536]{1,0:T(1,128)}) custom-call(bf16[1024,1536]{1,0:T(8,128)(2,1)} %copy-done, bf16[1024,640]{1,0:T(8,128)(2,1)} %leaf_backward.1.grad_ref, bf16[1536,640]{1,0:T(8,128)(2,1)} %fusion.4.weight_ref, f32[1,1536]{1,0:T(1,128)} %broadcast_in_dim.20.gain_ref), custom_call_target="tpu_custom_call" | custom-call | flops 1 | bytes 1 | tf_op jit(solution)/shard_map/pair_grads/pallas_call | solution.py:648
  379.0 4.6 all-to-all-start.6
  383.7 19.2 %collective-permute-done.24 = bf16[2,2,64,1536]{3,2,1,0:T(8,128)(2,1)} collective-permute-done((bf16[2,2,64,1536]{3,2,1,0:T(8,128)(2,1)S(1)}, bf16[2,2,64,1536]{3,2,1,0:T(8,128)(2,1)}, u32[]{:S(2)}, u32[]{:S(2)}) %collective-permute-start.24) | collective-permute-done | bytes 786464 | tf_op jit(solution)/shard_map/ppermute | solution.py:499
  411.4 9.2 %collective-permute-done.34 = bf16[2,96,640]{2,1,0:T(8,128)(2,1)} collective-permute-done((bf16[2,96,640]{2,1,0:T(8,128)(2,1)}, bf16[2,96,640]{2,1,0:T(8,128)(2,1)}, u32[]{:S(2)}, u32[]{:S(2)}) %collective-permute-start.34) | collective-permute-done | bytes 245792 | tf_op jit(solution)/shard_map/ppermute | solution.py:499
  423.0 4.4 collective-permute-done.25
  428.8 7.9 %collective-permute-done.26 = bf16[64,1536]{1,0:T(8,128)(2,1)S(1)} collective-permute-done((bf16[64,1536]{1,0:T(8,128)(2,1)S(1)}, bf16[64,1536]{1,0:T(8,128)(2,1)S(1)}, u32[]{:S(2)}, u32[]{:S(2)}) %collective-permute-start.26) | collective-permute-done | bytes 196640 | tf_op jit(solution)/shard_map/ppermute | solution.py:499
  437.6 4.5 collective-permute-done.27
  451.7 5.1 %collective-permute-start.30 = (f32[2,1536]{1,0:T(2,128)S(1)}, f32[2,1536]{1,0:T(2,128)S(1)}, u32[]{:S(2)}, u32[]{:S(2)}) collective-permute-start(f32[2,1536]{1,0:T(2,128)S(1)} %add.262), channel_id=1, source_target_pairs={{0,8},{8,0},{1,9},{9,1},{2,10},{10,2},{3,11},{11,3},{4,12},{12,4},... | collective-permute-start | bytes 36872 | tf_op jit(solution)/shard_map/ppermute | solution.py:499
  460.8 4.8 %collective-permute-start.32 = (f32[2,1536]{1,0:T(2,128)S(1)}, f32[2,1536]{1,0:T(2,128)S(1)}, u32[]{:S(2)}, u32[]{:S(2)}) collective-permute-start(f32[2,1536]{1,0:T(2,128)S(1)} %add.264), channel_id=1, source_target_pairs={{0,2},{2,0},{1,3},{3,1},{4,6},{6,4},{5,7},{7,5},{8,10},{10,8},{9,1... | collective-permute-start | bytes 36872 | tf_op jit(solution)/shard_map/ppermute | solution.py:499
  (367 shorter events, 154.7 us)
Async XLA Ops:
  7.2 85.2 %all-gather.4.cloned.1.call-start = ((), (), s32[]{:S(2)}) async-start(), calls=%async_computation.10 | async-start | bytes 3538944 | tf_op jit(solution)/shard_map/all_gather | solution.py:714
  8.9 14.5 %collective-permute-start = (bf16[64,1536]{1,0:T(8,128)(2,1)}, bf16[64,1536]{1,0:T(8,128)(2,1)}, u32[]{:S(2)}, u32[]{:S(2)}) collective-permute-start(bf16[64,1536]{1,0:T(8,128)(2,1)} %dynamic-slice_bitcast_fusion.12), channel_id=1, source_target_pairs={{0,16},{16,0},{1,17},{17,1},{2,18},{18,2},{3,19},{19,3},{4,20},{20... | collective-permute-start | bytes 589832 | tf_op jit(solution)/shard_map/ppermute | solution.py:499
  11.5 14.0 %collective-permute-start.1 = (bf16[2,96,1536]{2,1,0:T(8,128)(2,1)S(1)}, bf16[2,96,1536]{2,1,0:T(8,128)(2,1)}, u32[]{:S(2)}, u32[]{:S(2)}) collective-permute-start(bf16[2,96,1536]{2,1,0:T(8,128)(2,1)S(1)} %dynamic-slice_bitcast_fusion.3), channel_id=1, source_target_pairs={{0,4},{4,0},{1,5},{5,1},{2,6},{6,2},{3,7},{7,3},{8,12},{12,8},{9,1... | collective-permute-start | bytes 1769480 | tf_op jit(solution)/shard_map/ppermute | solution.py:499
  28.3 67.7 %all-to-all-start = ((bf16[16,112,512]{2,1,0:T(8,128)(2,1)}), bf16[16,112,512]{2,1,0:T(8,128)(2,1)}, u32[]{:S(2)}, u32[]{:S(2)}) async-start(bf16[16,112,512]{2,1,0:T(8,128)(2,1)} %bitcast.9), calls=%async_computation | async-start | bytes 3670016 | tf_op jit(solution)/shard_map/all_to_all | solution.py:713
  38.1 107.1 %all-gather.6.cloned.1.call-start = ((), (), s32[]{:S(2)}) async-start(), calls=%async_computation.11 | async-start | bytes 2457600 | tf_op jit(solution)/shard_map/all_gather | solution.py:688
  38.2 51.0 %collective-permute-start.4 = (bf16[2,96,768]{2,1,0:T(8,128)(2,1)S(1)}, bf16[2,96,768]{2,1,0:T(8,128)(2,1)}, u32[]{:S(2)}, u32[]{:S(2)}) collective-permute-start(bf16[2,96,768]{2,1,0:T(8,128)(2,1)S(1)} %pad_maximum_fusion.17), channel_id=1, source_target_pairs={{0,8},{8,0},{1,9},{9,1},{2,10},{10,2},{3,11},{11,3},{4,12},{12,4},... | collective-permute-start | bytes 884744 | tf_op jit(solution)/shard_map/ppermute | solution.py:499
  39.5 51.6 %collective-permute-start.3 = (bf16[2,96,1536]{2,1,0:T(8,128)(2,1)S(1)}, bf16[2,96,1536]{2,1,0:T(8,128)(2,1)S(1)}, u32[]{:S(2)}, u32[]{:S(2)}) collective-permute-start(bf16[2,96,1536]{2,1,0:T(8,128)(2,1)S(1)} %dynamic-slice_bitcast_fusion.2), channel_id=1, source_target_pairs={{0,2},{2,0},{1,3},{3,1},{4,6},{6,4},{5,7},{7,5},{8,10},{10,8},{9,1... | collective-permute-start | bytes 1769480 | tf_op jit(solution)/shard_map/ppermute | solution.py:499
  102.6 102.3 %all-gather.8.cloned.1.call-start = ((), (), s32[]{:S(2)}) async-start(), calls=%async_computation.12 | async-start | bytes 3440640 | tf_op jit(solution)/shard_map/all_gather | solution.py:688
  108.5 14.0 %collective-permute-start.5 = (bf16[2,2,96,768]{3,2,1,0:T(8,128)(2,1)S(1)}, bf16[2,2,96,768]{3,2,1,0:T(8,128)(2,1)S(1)}, u32[]{:S(2)}, u32[]{:S(2)}) collective-permute-start(bf16[2,2,96,768]{3,2,1,0:T(8,128)(2,1)S(1)} %copy-done.15), channel_id=1, source_target_pairs={{0,4},{4,0},{1,5},{5,1},{2,6},{6,2},{3,7},{7,3},{8,12},{12,8},{9,1... | collective-permute-start | bytes 1769480 | tf_op jit(solution)/shard_map/ppermute | solution.py:499
  122.7 19.2 %collective-permute-start.6 = (bf16[2,2,2,96,768]{4,3,2,1,0:T(8,128)(2,1)S(1)}, bf16[2,2,2,96,768]{4,3,2,1,0:T(8,128)(2,1)S(1)}, u32[]{:S(2)}, u32[]{:S(2)}) collective-permute-start(bf16[2,2,2,96,768]{4,3,2,1,0:T(8,128)(2,1)S(1)} %pad_maximum_fusion.6), channel_id=1, source_target_pairs={{0,2},{2,0},{1,3},{3,1},{4,6},{6,4},{5,7},{7,5},{8,10},{10,8},{9,1... | collective-permute-start | bytes 3538952 | tf_op jit(solution)/shard_map/ppermute | solution.py:499
  124.6 16.3 %collective-permute-start.7 = (bf16[2,64,1536]{2,1,0:T(8,128)(2,1)S(1)}, bf16[2,64,1536]{2,1,0:T(8,128)(2,1)S(1)}, u32[]{:S(2)}, u32[]{:S(2)}) collective-permute-start(bf16[2,64,1536]{2,1,0:T(8,128)(2,1)S(1)} %copy-done.18), channel_id=1, source_target_pairs={{0,4},{4,0},{1,5},{5,1},{2,6},{6,2},{3,7},{7,3},{8,12},{12,8},{9,1... | collective-permute-start | bytes 1179656 | tf_op jit(solution)/shard_map/ppermute | solution.py:499
  147.3 18.6 %all-to-all-start.1 = ((bf16[16,64,128]{2,1,0:T(8,128)(2,1)}), bf16[16,64,128]{2,1,0:T(8,128)(2,1)S(1)}, u32[]{:S(2)}, u32[]{:S(2)}) async-start(bf16[16,64,128]{2,1,0:T(8,128)(2,1)} %bitcast.51), calls=%async_computation.1 | async-start | bytes 524288 | tf_op jit(solution)/shard_map/all_to_all | solution.py:750
  167.9 19.5 %collective-permute-start.9 = (bf16[2,2,64,1536]{3,2,1,0:T(8,128)(2,1)}, bf16[2,2,64,1536]{3,2,1,0:T(8,128)(2,1)}, u32[]{:S(2)}, u32[]{:S(2)}) collective-permute-start(bf16[2,2,64,1536]{3,2,1,0:T(8,128)(2,1)} %pad_maximum_fusion.7), channel_id=1, source_target_pairs={{0,2},{2,0},{1,3},{3,1},{4,6},{6,4},{5,7},{7,5},{8,10},{10,8},{9,1... | collective-permute-start | bytes 2359304 | tf_op jit(solution)/shard_map/ppermute | solution.py:499
  180.5 24.2 %all-to-all-start.2 = ((bf16[8,64,1536]{2,1,0:T(8,128)(2,1)}), bf16[8,64,1536]{2,1,0:T(8,128)(2,1)}, u32[]{:S(2)}, u32[]{:S(2)}) async-start(bf16[8,64,1536]{2,1,0:T(8,128)(2,1)} %broadcast_in_dim.19), calls=%async_computation.2 | async-start | bytes 3145728 | tf_op jit(solution)/shard_map/all_to_all | solution.py:547
  187.4 67.2 %reduce-scatter.4.cloned.1.call-start = ((), (), s32[]{:S(2)}) async-start(), calls=%async_computation.13 | async-start | bytes 1474560 | tf_op jit(solution)/shard_map/reduce_scatter | solution.py:694
  223.0 29.9 %all-to-all-start.3 = ((bf16[8,64,1536]{2,1,0:T(8,128)(2,1)}), bf16[8,64,1536]{2,1,0:T(8,128)(2,1)}, u32[]{:S(2)}, u32[]{:S(2)}) async-start(bf16[8,64,1536]{2,1,0:T(8,128)(2,1)} %bitcast.455), calls=%async_computation.3 | async-start | bytes 3145728 | tf_op jit(solution)/shard_map/all_to_all | solution.py:552
  231.0 72.1 %reduce-scatter.6.cloned.1.call-start = ((), (), s32[]{:S(2)}) async-start(), calls=%async_computation.14 | async-start | bytes 1966080 | tf_op jit(solution)/shard_map/reduce_scatter | solution.py:694
  231.7 20.5 %collective-permute-start.10 = (bf16[2,128,192]{1,2,0:T(8,128)(2,1)S(1)}, bf16[2,128,192]{1,2,0:T(8,128)(2,1)S(1)}, u32[]{:S(2)}, u32[]{:S(2)}) collective-permute-start(bf16[2,128,192]{1,2,0:T(8,128)(2,1)S(1)} %dynamic-slice_bitcast_fusion.15), channel_id=1, source_target_pairs={{0,4},{4,0},{1,5},{5,1},{2,6},{6,2},{3,7},{7,3},{8,12},{12,8},{9,1... | collective-permute-start | bytes 294920 | tf_op jit(solution)/shard_map/ppermute | solution.py:499
  257.8 14.2 %collective-permute-start.11 = (bf16[64,1536]{1,0:T(8,128)(2,1)}, bf16[64,1536]{1,0:T(8,128)(2,1)}, u32[]{:S(2)}, u32[]{:S(2)}) collective-permute-start(bf16[64,1536]{1,0:T(8,128)(2,1)} %fusion.65), channel_id=1, source_target_pairs={{0,1},{1,0},{2,3},{3,2},{4,5},{5,4},{6,7},{7,6},{8,9},{9,8},{10,11... | collective-permute-start | bytes 589832 | tf_op jit(solution)/shard_map/ppermute | solution.py:499
  261.8 36.9 %collective-permute-start.15 = (bf16[2,2,64,1536]{3,2,0,1:T(8,128)(2,1)}, bf16[2,2,64,1536]{3,2,0,1:T(8,128)(2,1)}, u32[]{:S(2)}, u32[]{:S(2)}) collective-permute-start(bf16[2,2,64,1536]{3,2,0,1:T(8,128)(2,1)} %bitcast.432), channel_id=1, source_target_pairs={{0,1},{1,0},{2,3},{3,2},{4,5},{5,4},{6,7},{7,6},{8,9},{9,8},{10,11... | collective-permute-start | bytes 2359304 | tf_op jit(solution)/shard_map/ppermute | solution.py:499
  276.6 21.2 %all-to-all-start.4 = ((bf16[16,64,128]{2,1,0:T(8,128)(2,1)}), bf16[16,64,128]{2,1,0:T(8,128)(2,1)S(1)}, u32[]{:S(2)}, u32[]{:S(2)}) async-start(bf16[16,64,128]{2,1,0:T(8,128)(2,1)} %bitcast.74), calls=%async_computation.5 | async-start | bytes 524288 | tf_op jit(solution)/shard_map/all_to_all | solution.py:783
  281.7 80.2 %reduce-scatter.8.cloned.1.call-start = ((), (), s32[]{:S(2)}) async-start(), calls=%async_computation.15 | async-start | bytes 2457600 | tf_op jit(solution)/shard_map/reduce_scatter | solution.py:694
  285.1 15.7 %collective-permute-start.13 = (bf16[2,2,64,1536]{3,2,1,0:T(8,128)(2,1)S(1)}, bf16[2,2,64,1536]{3,2,1,0:T(8,128)(2,1)}, u32[]{:S(2)}, u32[]{:S(2)}) collective-permute-start(bf16[2,2,64,1536]{3,2,1,0:T(8,128)(2,1)S(1)} %pad_maximum_fusion.8), channel_id=1, source_target_pairs={{0,2},{2,0},{1,3},{3,1},{4,6},{6,4},{5,7},{7,5},{8,10},{10,8},{9,1... | collective-permute-start | bytes 2359304 | tf_op jit(solution)/shard_map/ppermute | solution.py:499
  307.1 25.5 %collective-permute-start.18 = (bf16[2,64,1536]{2,1,0:T(8,128)(2,1)}, bf16[2,64,1536]{2,1,0:T(8,128)(2,1)}, u32[]{:S(2)}, u32[]{:S(2)}) collective-permute-start(bf16[2,64,1536]{2,1,0:T(8,128)(2,1)} %dynamic-slice_bitcast_fusion.5), channel_id=1, source_target_pairs={{0,2},{2,0},{1,3},{3,1},{4,6},{6,4},{5,7},{7,5},{8,10},{10,8},{9,1... | collective-permute-start | bytes 1179656 | tf_op jit(solution)/shard_map/ppermute | solution.py:499
  308.4 23.1 %collective-permute-start.19 = (bf16[2,96,512]{2,1,0:T(8,128)(2,1)}, bf16[2,96,512]{2,1,0:T(8,128)(2,1)}, u32[]{:S(2)}, u32[]{:S(2)}) collective-permute-start(bf16[2,96,512]{2,1,0:T(8,128)(2,1)} %dynamic-slice_bitcast_fusion.11), channel_id=1, source_target_pairs={{0,4},{4,0},{1,5},{5,1},{2,6},{6,2},{3,7},{7,3},{8,12},{12,8},{9,1... | collective-permute-start | bytes 589832 | tf_op jit(solution)/shard_map/ppermute | solution.py:499
  313.9 44.6 %all-to-all-start.5 = ((bf16[16,96,192]{1,2,0:T(8,128)(2,1)}), bf16[16,96,192]{1,2,0:T(8,128)(2,1)S(1)}, u32[]{:S(2)}, u32[]{:S(2)}) async-start(bf16[16,96,192]{1,2,0:T(8,128)(2,1)} %copy.194), calls=%async_computation.7 | async-start | bytes 1572864 | tf_op jit(solution)/shard_map/all_to_all | solution.py:794
  334.3 13.2 %collective-permute-start.20 = (bf16[64,1536]{1,0:T(8,128)(2,1)S(1)}, bf16[64,1536]{1,0:T(8,128)(2,1)S(1)}, u32[]{:S(2)}, u32[]{:S(2)}) collective-permute-start(bf16[64,1536]{1,0:T(8,128)(2,1)S(1)} %dynamic-slice_bitcast_fusion.10), channel_id=1, source_target_pairs={{0,4},{4,0},{1,5},{5,1},{2,6},{6,2},{3,7},{7,3},{8,12},{12,8},{9,1... | collective-permute-start | bytes 589832 | tf_op jit(solution)/shard_map/ppermute | solution.py:499
  377.7 25.2 %collective-permute-start.24 = (bf16[2,2,64,1536]{3,2,1,0:T(8,128)(2,1)S(1)}, bf16[2,2,64,1536]{3,2,1,0:T(8,128)(2,1)}, u32[]{:S(2)}, u32[]{:S(2)}) collective-permute-start(bf16[2,2,64,1536]{3,2,1,0:T(8,128)(2,1)S(1)} %dynamic-slice_bitcast_fusion.1), channel_id=1, source_target_pairs={{0,4},{4,0},{1,5},{5,1},{2,6},{6,2},{3,7},{7,3},{8,12},{12,8},{9,1... | collective-permute-start | bytes 2359304 | tf_op jit(solution)/shard_map/ppermute | solution.py:499
  379.0 68.5 %all-to-all-start.6 = ((bf16[16,112,512]{2,1,0:T(8,128)(2,1)}), bf16[16,112,512]{2,1,0:T(8,128)(2,1)S(1)}, u32[]{:S(2)}, u32[]{:S(2)}) async-start(bf16[16,112,512]{2,1,0:T(8,128)(2,1)} %get-tuple-element.174), calls=%async_computation.9 | async-start | bytes 3670016 | tf_op jit(solution)/shard_map/all_to_all | solution.py:807
  405.2 15.4 %collective-permute-start.34 = (bf16[2,96,640]{2,1,0:T(8,128)(2,1)}, bf16[2,96,640]{2,1,0:T(8,128)(2,1)}, u32[]{:S(2)}, u32[]{:S(2)}) collective-permute-start(bf16[2,96,640]{2,1,0:T(8,128)(2,1)} %dynamic-slice_bitcast_fusion.7), channel_id=1, source_target_pairs={{0,4},{4,0},{1,5},{5,1},{2,6},{6,2},{3,7},{7,3},{8,12},{12,8},{9,1... | collective-permute-start | bytes 737288 | tf_op jit(solution)/shard_map/ppermute | solution.py:499
  408.3 19.1 %collective-permute-start.25 = (bf16[2,64,1536]{2,1,0:T(8,128)(2,1)}, bf16[2,64,1536]{2,1,0:T(8,128)(2,1)}, u32[]{:S(2)}, u32[]{:S(2)}) collective-permute-start(bf16[2,64,1536]{2,1,0:T(8,128)(2,1)} %dynamic-slice_bitcast_fusion.4), channel_id=1, source_target_pairs={{0,8},{8,0},{1,9},{9,1},{2,10},{10,2},{3,11},{11,3},{4,12},{12,4},... | collective-permute-start | bytes 1179656 | tf_op jit(solution)/shard_map/ppermute | solution.py:499
  446.4 25.6 %collective-permute-start.28 = (f32[64,1536]{1,0:T(8,128)S(1)}, f32[64,1536]{1,0:T(8,128)S(1)}, u32[]{:S(2)}, u32[]{:S(2)}) collective-permute-start(f32[64,1536]{1,0:T(8,128)S(1)} %get-tuple-element.237), channel_id=1, source_target_pairs={{0,1},{1,0},{2,3},{3,2},{4,5},{5,4},{6,7},{7,6},{8,9},{9,8},{10,11... | collective-permute-start | bytes 1179656 | tf_op jit(solution)/shard_map/ppermute | solution.py:499
  (72 other events, 429.7 us)
Sparse Core Ops, SparseCore 0:
  28.5 58.3 all-gather.3
  102.8 42.4 all-gather.5
  147.4 57.4 all-gather.7
  223.1 29.0 reduce-scatter.3
  264.1 38.9 reduce-scatter.5
  305.3 56.5 reduce-scatter.7

commit v3 on v2

--- a/solution.py
+++ b/solution.py
@@ -157,7 +157,7 @@
     return found
 
 
-def merge_forward(length, scale, own, v, qm, km, p, lab_col, lab_row, attended, lse, levels, m_ref, l_ref, o_ref):
+def merge_forward(length, scale, own, v, qm, km, p, lab_col, lab_row, attended, attended_low, lse, levels, m_ref, l_ref, o_ref):
     mm = dot_parts
     row, col = leaf_masks()
     for start in range(0, length, LEAF):
@@ -200,7 +200,9 @@
         if not last:
             qm, km, p = qm_next, km_next, p_next
     total = l_ref[...]
-    attended[...] = o_ref[...] / total
+    result = o_ref[...] / total
+    attended[...] = result
+    attended_low[...] = result.astype(jnp.bfloat16)
     lse[...] = jnp.broadcast_to(m_ref[...] + jnp.log(total), (length, LEAF))
 
 
@@ -298,7 +300,7 @@
             p = whole_dot("nde,nef->ndf", p_b, p_a).reshape(-1, LEAF)
             levels += [qm, km] + ([p] if 4 * h < length else [])
     top, total, out = state
-    return [out / total, jnp.broadcast_to(top + jnp.log(total), (length, LEAF))] + levels
+    return [out / total, (out / total).astype(jnp.bfloat16), jnp.broadcast_to(top + jnp.log(total), (length, LEAF))] + levels
 
 
 def long_backward(length, scale, own, v, levels, label, attended, lse, dout):
@@ -414,10 +416,10 @@
     return pl.BlockSpec(shape, lambda i: (0, 0))
 
 
-def merge_forward_kernel(length, scale, own, v, qm, km, p, lab_col, lab_row, attended, lse, *rest):
+def merge_forward_kernel(length, scale, own, v, qm, km, p, lab_col, lab_row, attended, attended_low, lse, *rest):
     flat, (m_ref, l_ref, o_ref) = rest[:-3], rest[-3:]
     merge_forward(
-        length, scale, own, v, qm, km, p, lab_col, lab_row, attended, lse, level_groups(length, flat), m_ref, l_ref, o_ref
+        length, scale, own, v, qm, km, p, lab_col, lab_row, attended, attended_low, lse, level_groups(length, flat), m_ref, l_ref, o_ref
     )
 
 
@@ -426,7 +428,7 @@
     extra = level_shapes(length)
     if length > MERGE_LIMIT:
         return long_forward(length, scale, own, proj[:, 2 * LEAF : 3 * LEAF], qm, km, p, lab_row)
-    outs = [matrix(length), matrix(length)] + extra
+    outs = [matrix(length), matrix(length, LEAF, jnp.bfloat16), matrix(length)] + extra
     return pl.pallas_call(
         functools.partial(merge_forward_kernel, length, scale),
         grid=(1,),
@@ -562,66 +564,54 @@
     return lax.optimization_barrier(values)
 
 
-def mlp_kernel(units, cut, act_ref, grad_ref, first_w, second_w, rows_out, hidden_out, part_out):
-    act = act_ref[...]
-    rest = 2 * units - cut
-    first = raw_dot(act, first_w[...], NN)
-    second = raw_dot(act, second_w[:, :rest], NN)
-    gate = first[:, :units]
-    up = jnp.concatenate([first[:, units:], second], axis=1)
-    hidden_grad = raw_dot(grad_ref[...], second_w[:, rest:], NN)
+def mlp_kernel(units, act_ref, grad_ref, weight_ref, rows_out, hidden_out, part_out):
+    both = raw_dot(act_ref[...], weight_ref[:, : 2 * units], NN)
+    hidden_grad = raw_dot(grad_ref[...], weight_ref[:, 2 * units :], NN)
+    gate, up = both[:, :units], both[:, units:]
     sigmoid_gate = jax.nn.sigmoid(gate)
     silu_gate = gate * sigmoid_gate
     hidden_out[...] = (silu_gate * up).astype(jnp.bfloat16)
     rows_out[:, :units] = (hidden_grad * up * sigmoid_gate * (1.0 + gate * (1.0 - sigmoid_gate))).astype(jnp.bfloat16)
     rows_out[:, units:] = (hidden_grad * silu_gate).astype(jnp.bfloat16)
-    part = raw_dot(rows_out[:, :cut], first_w[...], NT) + raw_dot(rows_out[:, cut:], second_w[:, :rest], NT)
-    part_out[...] = part.astype(jnp.bfloat16)
-
-
-def mlp_of(act, grad, first, second):
+    part_out[...] = raw_dot(rows_out[...], weight_ref[:, : 2 * units], NT).astype(jnp.bfloat16)
+
+
+def mlp_of(act, grad, weight):
     tokens, width = act.shape
-    units = (first.shape[1] + second.shape[1]) // 3
+    units = weight.shape[1] // 3
     outs = [matrix(tokens, 2 * units, jnp.bfloat16), matrix(tokens, units, jnp.bfloat16), matrix(tokens, width, jnp.bfloat16)]
     return pl.pallas_call(
-        functools.partial(mlp_kernel, units, first.shape[1]),
-        in_specs=[whole_spec()] * 4,
+        functools.partial(mlp_kernel, units),
+        in_specs=[whole_spec()] * 3,
         out_specs=[whole_spec()] * 3,
         out_shape=outs,
         compiler_params=settings(),
         cost_estimate=cost(1, 1),
         name="mlp",
-    )(act, grad, first, second)
-
-
-def mlp_grads_kernel(cuts, act_ref, grad_ref, rows_ref, hidden_ref, first_out, second_out, third_out):
-    both = raw_dot(act_ref[...], rows_ref[...], TN).astype(jnp.bfloat16)
-    down = raw_dot(grad_ref[...], hidden_ref[...], TN).astype(jnp.bfloat16)
-    first_out[...] = both[:, : cuts[0]]
-    second_out[...] = both[:, cuts[0] : cuts[1]]
-    third_out[:, : both.shape[1] - cuts[1]] = both[:, cuts[1] :]
-    third_out[:, both.shape[1] - cuts[1] :] = down
+    )(act, grad, weight)
+
+
+def mlp_grads_kernel(act_ref, grad_ref, rows_ref, hidden_ref, out):
+    wide = rows_ref.shape[1]
+    out[:, :wide] = raw_dot(act_ref[...], rows_ref[...], TN).astype(jnp.bfloat16)
+    out[:, wide:] = raw_dot(grad_ref[...], hidden_ref[...], TN).astype(jnp.bfloat16)
 
 
 def mlp_grads_of(act, grad, rows, hidden):
     tokens, width = act.shape
     units = hidden.shape[1]
-    cuts = (3 * units // 4, 15 * units // 8) if units % (8 * LEAF) == 0 else (3 * units // 4, 7 * units // 4)
-    if units % (4 * LEAF):
-        cuts = (units, 2 * units)
-    widths = (cuts[0], cuts[1] - cuts[0], 3 * units - cuts[1])
     step = 2 * LEAF
     column = pl.BlockSpec((tokens, step), lambda i: (0, i))
-    return list(pl.pallas_call(
-        functools.partial(mlp_grads_kernel, cuts),
+    return pl.pallas_call(
+        mlp_grads_kernel,
         grid=(width // step,),
         in_specs=[column, column, plain_spec(rows.shape), plain_spec(hidden.shape)],
-        out_specs=[pl.BlockSpec((step, w), lambda i: (i, 0)) for w in widths],
-        out_shape=[matrix(width, w, jnp.bfloat16) for w in widths],
+        out_specs=pl.BlockSpec((step, 3 * units), lambda i: (i, 0)),
+        out_shape=matrix(width, 3 * units, jnp.bfloat16),
         compiler_params=settings(),
         cost_estimate=cost(1, 1),
         name="mlp_grads",
-    )(act, grad, rows, hidden))
+    )(act, grad, rows, hidden)
 
 
 GRAD_ROWS = 3 * LEAF
@@ -660,7 +650,7 @@
             jax.ShapeDtypeStruct((1, width), jnp.float32),
         ],
         compiler_params=settings(),
-        cost_estimate=cost(1, 1),
+        cost_estimate=cost(12 * 10**9, 36 * 10**6),
         name="pair_grads",
     )(attn_in, proj_grad, weight, gain.reshape(1, width))
 
@@ -703,55 +693,51 @@
     label_row = jnp.broadcast_to(padded(segment_ids.astype(low).reshape(1, 1, -1), 2, 4 * LEAF), (half_heads, 1, 4 * LEAF))
     packed = padded(padded(jnp.concatenate([packed, beta_row, label_row], axis=1), 1, rows + EXTRA), 0, slots)
     packed = jnp.broadcast_to(packed[None], (2, *packed.shape)).reshape(count, rows + EXTRA, 4 * LEAF)
-    all_tokens = exchanged(tokens, steps[:1])
+    both_inputs = tokens.astype(jnp.float32)
+    attn_in = exchanged((normalize(both_inputs) * gain_attn).astype(low), steps[:1])
+    attn_in = lax.all_gather(attn_in, steps[1:], axis=1, tiled=True).reshape(length, width)
     blocks = [slice(i * units, (i + 1) * units) for i in range(inner)]
     mlp_own = jnp.stack([jnp.concatenate([w_gate[:, i], w_up[:, i], w_down[i].T], axis=1) for i in blocks])
     mlp_own = exchanged(mlp_own.reshape(2, 2, rows, 3 * units), inner_axes[:1])
-    out_own = gathered(w_out.T, steps[:1])
-    packed, all_tokens, mlp_own, out_own = fence(packed, all_tokens, mlp_own, out_own)
+    out_own = gathered(w_out.T, outer_axes)
+
+    packed, mlp_own, out_own = fence(packed, mlp_own, out_own)
 
     packed = lax.all_to_all(packed, steps, 0, 0, tiled=True)
-    all_tokens = lax.all_gather(all_tokens, steps[1:], axis=1, tiled=True).reshape(length, width)
-    all_inputs = all_tokens.astype(jnp.float32)
-    attn_in = (normalize(all_inputs) * gain_attn).astype(low)
     mlp_own = exchange_at(mlp_own, 1, inner_axes[1]).reshape(depth, 3 * units)
-    for at in range(1, len(outer_axes)):
-        out_own = by_index(out_own, swap(out_own, steps[at]), steps[at], at)
-    packed, attn_in, mlp_own, out_own = fence(packed, attn_in, mlp_own, out_own)
-
     weight = packed[:, :rows].reshape(width, 4 * LEAF)
     beta_column = padded(packed[:, rows, :rows].reshape(width, 1), 1, LEAF)
     weight = jnp.concatenate([weight, beta_column], axis=1)
     label_all = pick(packed[:, rows + 1, : 2 * positions].reshape(count, 2, positions), 1, micro)
     label_all = label_all.reshape(1, length).astype(jnp.float32)
     label_column = jnp.broadcast_to(label_all.reshape(length, 1), (length, LEAF))
+    weight, label_all, label_column, attn_in, mlp_own, out_own = fence(
+        weight, label_all, label_column, attn_in, mlp_own, out_own
+    )
+
     bias_row = padded(lax.dynamic_slice(padded(beta_bias, 0, slots), (rank % slots,), (1,)), 0, LEAF)
     bias_row = jnp.concatenate([jnp.zeros(4 * LEAF, jnp.float32), bias_row])
-    cut = 5 * units // 4
-    first_weight = gathered_outer(mlp_own[:, :cut])
     proj = dot(attn_in, weight) + bias_row
-    proj, out_own, grad_group = fence(proj, out_own, out_grad)
+    mlp_weight = gathered_outer(mlp_own)
+    proj, out_own = fence(proj, out_own)
 
     out_own = gather_at(out_own, len(outer_axes), inner_axes[0])
     *saved, own_logits, query_moved, key_moved, product = leaf_forward(proj)
-    own_logits, out_own, grad_group = fence(own_logits, out_own, grad_group)
+    own_logits, out_own = fence(own_logits, out_own)
 
     out_own = gather_at(out_own, len(outer_axes) + 1, inner_axes[1])
-    grad_group = gather_at(grad_group, 1, inner_axes[0])
-    attended, log_total, *levels = run_merge_forward(
+    attended, attended_low, log_total, *levels = run_merge_forward(
         proj, own_logits, query_moved, key_moved, product, label_column, label_all, scale
     )
-    attended_low = attended.astype(low)
-    attended_low, out_own, grad_group, first_weight, mlp_own = fence(attended_low, out_own, grad_group, first_weight, mlp_own)
+    attended_low, out_own = fence(attended_low, out_own)
     out_own = out_own.reshape(width, half_heads * LEAF)
 
-    second_weight = gathered_outer(mlp_own[:, cut:])
-    grad_group = gather_at(grad_group, 2, inner_axes[1]).reshape(-1, width)
+    grad_group = gather_at(gather_at(after(out_grad, attended_low), 1, inner_axes[0]), 2, inner_axes[1]).reshape(-1, width)
     heads_here = lax.all_to_all(attended_low.reshape(count, positions, LEAF), steps, 0, 0, tiled=True)
     heads_here = heads_here.reshape(2, slots, positions, LEAF)[:, :half_heads].transpose(0, 2, 1, 3)
     heads_here = heads_here.reshape(2 * positions, half_heads * LEAF)
     branch = dot(heads_here, out_own, NT).reshape(2, positions, width)
-    branch = pick(branch, 0, half) + swap(pick(branch, 0, 1 - half), "head")
+    branch = pick(branch, 0, half) + swap(pick(branch, 0, 1 - half).astype(low), "head").astype(jnp.float32)
     inputs = pick(tokens, 0, half).astype(jnp.float32)
     middle = inputs + branch
     normed_two = normalize(middle)
@@ -759,19 +745,16 @@
     mlp_group = copies(mlp_in, group).reshape(-1, width)
     columns = heads_here.reshape(2 * positions, inner, -1).transpose(1, 0, 2)
     columns = columns.reshape(2, 2, 2 * positions, -1)
-    mlp_group, second_weight, grad_group = fence(mlp_group, second_weight, grad_group)
-
-    rows_grad, hidden, mlp_in_part = mlp_of(mlp_group, grad_group, first_weight, second_weight)
+    mlp_group, mlp_weight, grad_group = fence(mlp_group, mlp_weight, grad_group)
+
+    rows_grad, hidden, mlp_in_part = mlp_of(mlp_group, grad_group, mlp_weight)
     mlp_in_grad = sums(mlp_in_part, group)
     mlp_grads = mlp_grads_of(mlp_group, grad_group, rows_grad, hidden)
-    mlp_grads[0] = outer_sums(mlp_grads[0])
-    mlp_part = dot(hidden, second_weight[:, 2 * units - cut :], NT).astype(low)
-    columns = exchange_at(after(columns, mlp_grads[2]), 0, inner_axes[0])
-    mlp_in_grad, mlp_part, columns, *mlp_grads = fence(mlp_in_grad, mlp_part, columns, *mlp_grads)
-
-    mlp_grads[1] = outer_sums(mlp_grads[1])
-    mlp_grads[0] = to_owner(mlp_grads[0])
-    mlp_part = scattered(mlp_part.reshape(2, 2, 2, positions, width), ("head",)).astype(low)
+    mlp_sums = outer_sums(mlp_grads)
+    mlp_part = dot(hidden, mlp_weight[:, 2 * units :], NT).astype(low)
+    columns = exchange_at(after(columns, mlp_grads), 0, inner_axes[0])
+    mlp_in_grad, mlp_part, columns, mlp_grads = fence(mlp_in_grad, mlp_part, columns, mlp_grads)
+
     mlp_gain_part = jnp.sum(mlp_in_grad * normed_two, axis=0)
     own_grad = pick(out_grad, 0, half).astype(jnp.float32)
     middle_grad = own_grad + norm_back(mlp_in_grad * gain_mlp, normed_two, middle)
@@ -781,52 +764,62 @@
     attended_grad = attended_grad.reshape(2, positions, half_heads, LEAF).transpose(0, 2, 1, 3)
     attended_grad = padded(attended_grad, 1, slots).reshape(count, positions, LEAF)
     attended_grad = lax.all_to_all(attended_grad, steps, 0, 0, tiled=True).reshape(length, LEAF).astype(jnp.float32)
-    branch_group = gather_at(gather_at(branch_low, 1, inner_axes[0]), 2, inner_axes[1]).reshape(-1, width)
-    columns = exchange_at(columns, 1, inner_axes[1]).reshape(inner, 2, positions, -1)
-    columns = columns.swapaxes(0, 1).reshape(-1, columns.shape[-1])
-    attended_grad, branch_group, columns, mlp_part, *mlp_grads = fence(attended_grad, branch_group, columns, mlp_part, *mlp_grads)
-
-    mlp_grads[2] = outer_sums(mlp_grads[2])
-    mlp_grads[1] = exchange_at(mlp_grads[1].reshape(2, 2, rows, -1), 0, inner_axes[0])
-    mlp_part = scattered(mlp_part.swapaxes(0, 1), inner_axes[1:]).astype(low)
-    out_weight_grad = dot(branch_group, columns, TN).astype(low).reshape(count, rows, -1)
-    attended_grad = after(attended_grad, out_weight_grad)
-    out_weight_grad = lax.all_to_all(out_weight_grad, steps, 0, 0, tiled=True)
+    attended_grad, branch_low, mlp_part = fence(attended_grad, branch_low, mlp_part)
+
+    mlp_part = scatter_at(mlp_part.reshape(2, 2, 2, positions, width), 0, "head")
     merged = run_merge_backward(
         proj, own_logits, query_moved, key_moved, product, levels, label_column, label_all, attended, log_total, attended_grad, scale
     )
-    mlp_part, mlp_grads[1], *merged = fence(mlp_part, mlp_grads[1], *merged)
-
-    mlp_grads[1] = exchange_at(mlp_grads[1], 1, inner_axes[1]).reshape(inner, rows, -1)
-    mlp_part = scattered(mlp_part, inner_axes[:1])
+    branch_group = gather_at(branch_low, 1, inner_axes[0])
+    mlp_part, mlp_sums, branch_group, *merged = fence(mlp_part, mlp_sums, branch_group, *merged)
+
+    mlp_part = scatter_at(mlp_part, 1, inner_axes[1])
+    mlp_sums = exchange_at(mlp_sums.reshape(2, 2, rows, 3 * units), 0, inner_axes[0])
+    middle_both = by_half(middle_grad, swap(middle_grad, "head"))
     proj_grad = leaf_backward(proj, saved, merged)
-    proj_grad, mlp_part, out_weight_grad, *mlp_grads = fence(proj_grad, mlp_part, out_weight_grad, *mlp_grads)
-
+    branch_group = gather_at(branch_group, 2, inner_axes[1]).reshape(-1, width)
+    proj_grad, mlp_part, middle_both, mlp_sums, branch_group = fence(proj_grad, mlp_part, middle_both, mlp_sums, branch_group)
+
+    attn_in_part = dot(proj_grad, weight, NT).astype(low).reshape(*(2,) * len(steps), positions, width)
     packed_grad, attn_gain_part = pair_grads_of(attn_in, proj_grad, weight, gain_attn, rows)
-    attn_in_part = dot(after(proj_grad, packed_grad), weight, NT)
+    attn_in_part = scatter_at(attn_in_part, len(steps) - 1, steps[-1])
+    mlp_grads = exchange_at(mlp_sums, 1, inner_axes[1]).reshape(inner, rows, 3 * units)
+    mlp_part = scatter_at(mlp_part, 0, inner_axes[0])
+    columns = exchange_at(columns, 1, inner_axes[1]).reshape(inner, 2, positions, -1)
+    packed_grad, attn_gain_part, attn_in_part, mlp_grads, mlp_part, columns = fence(
+        packed_grad, attn_gain_part, attn_in_part, mlp_grads, mlp_part, columns
+    )
+
     packed_grad = lax.all_to_all(packed_grad, steps, 0, 0, tiled=True)
-    attn_in_part = attn_in_part.astype(low).reshape(2, *(2,) * (len(steps) - 1), positions, width)
-    for at in range(len(steps) - 1, 0, -1):
-        attn_in_part = scatter_at(attn_in_part, at, steps[at])
-        if at == len(outer_axes):
-            mlp_grads[2] = after(mlp_grads[2], attn_in_part)
-    attn_in_part = exchanged(attn_in_part, steps[:1])
-    attn_in_grad = scattered(attn_in_part, ("head",))
+    attn_in_part = scatter_at(attn_in_part, 0, "head")
+    for at in range(len(steps) - 2, 0, -1):
+        attn_in_part = scatter_at(attn_in_part, at - 1, steps[at])
+    gains = jnp.stack([attn_gain_part[0], mlp_gain_part])
+    for axis in (*inner_axes, "head"):
+        gains = gains + swap(gains, axis)
+    columns = columns.swapaxes(0, 1).reshape(-1, columns.shape[-1])
+    out_weight_grad = dot(branch_group, columns, TN).astype(low).reshape(count, rows, -1)
+    mlp_grads = mlp_grads.astype(jnp.float32)
+    gate_grad, up_grad = (
+        mlp_grads[:, :, i * units : (i + 1) * units].transpose(1, 0, 2).reshape(rows, inner * units) for i in range(2)
+    )
+    down_grad = mlp_grads[:, :, 2 * units :].transpose(0, 2, 1).reshape(inner * units, rows)
+    packed_grad, attn_in_part, mlp_part, gains, out_weight_grad, gate_grad, up_grad, down_grad = fence(
+        packed_grad, attn_in_part, mlp_part, gains, out_weight_grad, gate_grad, up_grad, down_grad
+    )
+
+    plane = (steps[0], "head")
+    same = lax.ppermute(attn_in_part, plane, [(0, 0), (1, 2), (2, 1), (3, 3)])
+    opposite = lax.ppermute(attn_in_part, plane, [(0, 1), (1, 3), (2, 0), (3, 2)])
+    attn_in_grad = by_half(same, opposite).astype(jnp.float32)
 
     block_out = (middle + mlp_part).astype(low)
     block_out = by_half(block_out, swap(block_out, "head"))
-    mlp_grads[2] = to_owner(mlp_grads[2])
-    mlp_grads = jnp.concatenate(mlp_grads, axis=2).astype(jnp.float32)
-    gate_grad, up_grad = (
-        mlp_grads[:, :, i * units : (i + 1) * units].transpose(1, 0, 2).reshape(rows, inner * units) for i in range(2)
-    )
-    down_grad = mlp_grads[:, :, 2 * units :].transpose(0, 2, 1).reshape(inner * units, rows)
-    out_weight_grad = jnp.sum(out_weight_grad.reshape(-1, inner, rows, out_weight_grad.shape[-1]).astype(jnp.float32), axis=0)
+    out_weight_grad = lax.all_to_all(out_weight_grad, steps, 0, 0, tiled=True).astype(jnp.float32)
+    out_weight_grad = jnp.sum(out_weight_grad.reshape(-1, inner, rows, out_weight_grad.shape[-1]), axis=0)
     out_weight_grad = out_weight_grad.transpose(0, 2, 1).reshape(-1, rows)
 
-    gains = jnp.stack([attn_gain_part[0], mlp_gain_part])
-    gains = after(gains, packed_grad)
-    for axis in (*steps, "head"):
+    for axis in outer_axes:
         gains = gains + swap(gains, axis)
     small = after(packed_grad[:, rows : rows + 2], gains)
     small = jnp.sum(small.reshape(2, slots, 2, -1)[:, :half_heads].astype(jnp.float32), axis=0)
@@ -837,8 +830,8 @@
     total = total[0] + total[1]
     grads = [total[..., i * LEAF : (i + 1) * LEAF].transpose(1, 0, 2).reshape(rows, half_heads * LEAF) for i in range(4)]
 
-    tokens_grad = middle_grad + norm_back(attn_in_grad * gain_attn, normalize(inputs), inputs)
-    tokens_grad = by_half(tokens_grad, swap(tokens_grad, "head"))
+    attn_in_grad = after(attn_in_grad, *grads)
+    tokens_grad = middle_both + norm_back(attn_in_grad * gain_attn, normalize(both_inputs), both_inputs)
     return (
         block_out, tokens_grad, *grads, beta_grad, bias_grad, out_weight_grad, gate_grad, up_grad, down_grad, gains[0], gains[1]
     )

time: 489 us -> 435 us (0.89)
  waiting for transfers between devices: 193 us -> 156 us
  other arithmetic: 47.3 us -> 39.4 us
  local copies, waits for them, and re-layouts: 50.4 us -> 44.5 us
    ppermute x36 -> x31, waiting for transfers between devices: 137 us -> 70.1 us  [swap(): return lax.ppermute(value, axis, [(0, 1), (1, 0)])]
    all_to_all x1, waiting for transfers between devices: 0.01 us -> 35.8 us  [local(): packed = lax.all_to_all(packed, steps, 0, 0, tiled=True)]
    all_to_all x1, waiting for transfers between devices: 10.1 us -> 3.65 us  [local(): lax.all_to_all(out_weight_grad, steps, 0, 0, tiled=True).astype(jnp.float32)]
    all_to_all x1, waiting for transfers between devices: 12.7 us -> 7.19 us  [local(): lax.all_to_all(attended_low.reshape(count, positions, LEAF), steps, 0, 0,...]
    all_to_all x1, starting transfers between devices: 4.78 us -> 9.87 us  [local(): lax.all_to_all(out_weight_grad, steps, 0, 0, tiled=True).astype(jnp.float32)]
    ppermute x36 -> x31, starting transfers between devices: 42.6 us -> 39.1 us  [swap(): return lax.ppermute(value, axis, [(0, 1), (1, 0)])]
    another operation x43 -> x37, other arithmetic: 20.6 us -> 19.6 us  [by_index(): jnp.stack([jnp.where(first, own, other), jnp.where(first, other, own)], a...]
  transfers between devices with their start and end apart: 49 -> 43, of which waited for: 26 -> 20; matrix products, arithmetic and copies ran while one was open for 19% -> 21% of each run, Pallas kernels for 9% -> 12%
where the time goes in v3:
time: 435 us; the launch traced here: 428 us
  waiting for transfers between devices  156 us (36%)
  starting transfers between devices  88.3 us (20%)
  Pallas kernels  68.9 us (16%)
  local copies, waits for them, and re-layouts  44.5 us (10%)
  other arithmetic  39.4 us (9%)
  matrix products  16 us (4%)
  between operations  15 us (3%)
    ppermute x31, waiting for transfers between devices, swap(): return lax.ppermute(value, axis, [(0, 1), (1, 0)])  70.1 us
    ppermute x31, starting transfers between devices, swap(): return lax.ppermute(value, axis, [(0, 1), (1, 0)])  39.1 us
    all_to_all x1, waiting for transfers between devices, local(): packed = lax.all_to_all(packed, steps, 0, 0, tiled=True)  35.8 us
    another operation x37, other arithmetic, by_index(): jnp.stack([jnp.where(first, own, other), jnp.where(first, other, own)], a...  19.6 us
    dot_general x6, matrix products, dot(): lax.dot_general(a, b, (dims, ((), ())), preferred_element_type=jnp.float32)  16 us
    all_to_all x1, waiting for transfers between devices, local(): lax.all_to_all(attended_grad, steps, 0, 0, tiled=True).reshape(length, LEAF)  14.5 us
    all_to_all x1, waiting for transfers between devices, copies(): lax.all_to_all(jnp.broadcast_to(value, (lax.axis_size(axes), *value.shape...  14.3 us
    pallas_call x1, Pallas kernels, run_merge_backward(): pl.pallas_call(functools.partial(merge_backward_kernel, length, scale), g...  12.9 us
  transfers between devices with their start and end apart: 43, of which 20 were waited for; matrix products, arithmetic and copies ran while one was open for 21% of the time, Pallas kernels for 12%

profile of v3, /device:TPU:21, one launch (start us, length us, event | category | flops | bytes accessed | tf_op | source)
XLA Modules:
  0.0 427.9 jit_solution(12497365387753570801)
XLA Ops:
  17.2 6.7 %collective-permute-start.2 = (bf16[2,96,768]{2,1,0:T(8,128)(2,1)S(1)}, bf16[2,96,768]{2,1,0:T(8,128)(2,1)}, u32[]{:S(2)}, u32[]{:S(2)}) collective-permute-start(bf16[2,96,768]{2,1,0:T(8,128)(2,1)S(1)} %pad_maximum_fusion.16), channel_id=1, source_target_pairs={{0,8},{8,0},{1,9},{9,1},{2,10},{10,2},{3,11},{11,3},{4,12},{12,4},... | collective-permute-start | bytes 884744 | tf_op jit(solution)/shard_map/ppermute | solution.py:501
  35.5 7.6 %all-to-all-start = ((bf16[16,112,512]{2,1,0:T(8,128)(2,1)}), bf16[16,112,512]{2,1,0:T(8,128)(2,1)S(1)}, u32[]{:S(2)}, u32[]{:S(2)}) async-start(bf16[16,112,512]{2,1,0:T(8,128)(2,1)} %bitcast.9), calls=%async_computation | async-start | bytes 3670016 | tf_op jit(solution)/shard_map/all_to_all | solution.py:706
  48.8 35.8 %all-to-all-done = bf16[16,112,512]{2,1,0:T(8,128)(2,1)S(1)} async-done(((bf16[16,112,512]{2,1,0:T(8,128)(2,1)}), bf16[16,112,512]{2,1,0:T(8,128)(2,1)S(1)}, u32[]{:S(2)}, u32[]{:S(2)}) %all-to-all-start) | async-done | bytes 1835040 | tf_op jit(solution)/shard_map/all_to_all | solution.py:706
  89.0 6.0 %convolution_add_fusion.q_ref.k_ref.h_ref.g_ref.v = f32[1024,640]{1,0:T(8,128)} fusion(bf16[1024,1536]{1,0:T(8,128)(2,1)} %bitcast.390, bf16[1536,640]{1,0:T(8,128)(2,1)S(1)} %fusion.2.weight_ref, f32[640]{0:T(1024)S(1)} %pad.129), kind=kOutput, calls=%fused_computation.12 | convolution fusion | flops 2013921280 | bytes 7735808 | tf_op jit(solution)/shard_map/dot_general | solution.py:493
  95.1 11.5 %leaf_forward.1 = (f32[1024,128]{1,0:T(8,128)}, f32[1024,128]{1,0:T(8,128)}, f32[1024,128]{1,0:T(8,128)}, f32[1024,128]{1,0:T(8,128)}, f32[1024,128]{1,0:T(8,128...) custom-call(f32[1024,640]{1,0:T(8,128)} %convolution_add_fusion.q_re, ...), custom_call_target="tpu_custom_call" | custom-call | flops 1 | bytes 1 | tf_op jit(solution)/shard_map/leaf_forward/pallas_call | solution.py:360
  111.1 9.9 %merge_forward.1 = (f32[1024,128]{1,0:T(8,128)}, bf16[1024,128]{1,0:T(8,128)(2,1)}, f32[1024,128]{1,0:T(8,128)}, f32[1024,128]{1,0:T(8,128)}, f32[1024,128]{1,0:...) custom-call(f32[1024,128]{1,0:T(8,128)} %get-tuple-element.107.own, ...), custom_call_target="tpu_custom_call" | custom-call | flops 1 | bytes 1 | tf_op jit(solution)/shard_map/merge_forward/pallas_call | solution.py:432
  122.1 5.6 %all-to-all-start.1 = ((bf16[16,64,128]{2,1,0:T(8,128)(2,1)}), bf16[16,64,128]{2,1,0:T(8,128)(2,1)}, u32[]{:S(2)}, u32[]{:S(2)}) async-start(bf16[16,64,128]{2,1,0:T(8,128)(2,1)} %bitcast.46), calls=%async_computation.1 | async-start | bytes 524288 | tf_op jit(solution)/shard_map/all_to_all | solution.py:736
  127.7 5.5 %collective-permute-done.8 = bf16[2,64,1536]{2,1,0:T(8,128)(2,1)} collective-permute-done((bf16[2,64,1536]{2,1,0:T(8,128)(2,1)S(1)}, bf16[2,64,1536]{2,1,0:T(8,128)(2,1)}, u32[]{:S(2)}, u32[]{:S(2)}) %collective-permute-start.8) | collective-permute-done | bytes 393248 | tf_op jit(solution)/shard_map/ppermute | solution.py:501
  134.3 7.2 %all-to-all-done.1 = bf16[16,64,128]{2,1,0:T(8,128)(2,1)} async-done(((bf16[16,64,128]{2,1,0:T(8,128)(2,1)}), bf16[16,64,128]{2,1,0:T(8,128)(2,1)}, u32[]{:S(2)}, u32[]{:S(2)}) %all-to-all-start.1) | async-done | bytes 262176 | tf_op jit(solution)/shard_map/all_to_all | solution.py:736
  151.1 6.7 %all-to-all-start.2 = ((bf16[8,64,1536]{2,1,0:T(8,128)(2,1)}), bf16[8,64,1536]{2,1,0:T(8,128)(2,1)}, u32[]{:S(2)}, u32[]{:S(2)}) async-start(bf16[8,64,1536]{2,1,0:T(8,128)(2,1)} %broadcast_in_dim.17), calls=%async_computation.2 | async-start | bytes 3145728 | tf_op jit(solution)/shard_map/all_to_all | solution.py:549
  160.8 14.3 %all-to-all-done.2 = bf16[8,64,1536]{2,1,0:T(8,128)(2,1)} async-done(((bf16[8,64,1536]{2,1,0:T(8,128)(2,1)}), bf16[8,64,1536]{2,1,0:T(8,128)(2,1)}, u32[]{:S(2)}, u32[]{:S(2)}) %all-to-all-start.2) | async-done | bytes 1572896 | tf_op jit(solution)/shard_map/all_to_all | solution.py:549
  175.0 5.9 %all-gather.5.cloned.1.call-done.weight_ref = bf16[1536,1536]{1,0:T(8,128)(2,1)} async-done(((bf16[384,1536]{1,0:T(8,128)(2,1)}), bf16[1536,1536]{1,0:T(8,128)(2,1)}) %all-gather.5.cloned.1.call-update) | async-done | bytes 4718608 | tf_op jit(solution)/shard_map/all_gather | solution.py:678
  181.0 8.9 %mlp.1 = (bf16[512,1024]{1,0:T(8,128)(2,1)}, bf16[512,512]{1,0:T(8,128)(2,1)}, bf16[512,1536]{1,0:T(8,128)(2,1)}) custom-call(bf16[512,1536]{1,0:T(8,128)(2,1)} %bitcast.54.act_ref, bf16[512,1536]{1,0:T(8,128)(2,1)} %bitcast.349, bf16[1536,1536]{1,0:T(8,128)(2,1)} %all-gather.5.cloned.1.call-done.weight_ref), custom_call_target="tpu_custom_call" | custom-call | flops 1 | bytes 1 | tf_op jit(solution)/shard_map/mlp/pallas_call | solution.py:583
  189.9 7.6 %mlp_grads.1 = bf16[1536,1536]{1,0:T(8,128)(2,1)} custom-call(bf16[512,1536]{1,0:T(8,128)(2,1)} %bitcast.54.act_ref, bf16[512,1536]{1,0:T(8,128)(2,1)} %bitcast.350, bf16[512,1024]{1,0:T(8,128)(2,1)} %get-tuple-element.131.rows_ref, bf16[512,512]{1,0:T(8,128)(2,1)} %get-tuple-element.130.hidden_ref), custom_call_target="tpu_custom_call" | custom-call | flops 1 | bytes 1 | tf_op jit(solution)/shard_map/mlp_grads/pallas_call | solution.py:605
  197.5 5.1 %all-to-all-start.3 = ((bf16[8,64,1536]{2,1,0:T(8,128)(2,1)}), bf16[8,64,1536]{2,1,0:T(8,128)(2,1)}, u32[]{:S(2)}, u32[]{:S(2)}) async-start(bf16[8,64,1536]{2,1,0:T(8,128)(2,1)} %bitcast.362), calls=%async_computation.3 | async-start | bytes 3145728 | tf_op jit(solution)/shard_map/all_to_all | solution.py:554
  207.1 3.7 convolution_convert_fusion.1
  210.8 13.0 %collective-permute-done.10 = bf16[2,128,192]{1,2,0:T(8,128)(2,1)S(1)} collective-permute-done((bf16[2,128,192]{1,2,0:T(8,128)(2,1)S(1)}, bf16[2,128,192]{1,2,0:T(8,128)(2,1)S(1)}, u32[]{:S(2)}, u32[]{:S(2)}) %collective-permute-start.10) | collective-permute-done | bytes 98336 | tf_op jit(solution)/shard_map/ppermute | solution.py:501
  228.2 5.7 %collective-permute-done.11 = bf16[64,1536]{1,0:T(8,128)(2,1)S(1)} collective-permute-done((bf16[64,1536]{1,0:T(8,128)(2,1)}, bf16[64,1536]{1,0:T(8,128)(2,1)S(1)}, u32[]{:S(2)}, u32[]{:S(2)}) %collective-permute-start.11) | collective-permute-done | bytes 196640 | tf_op jit(solution)/shard_map/ppermute | solution.py:501
  238.1 8.5 %all-to-all-start.4 = ((bf16[16,64,128]{2,1,0:T(8,128)(2,1)}), bf16[16,64,128]{2,1,0:T(8,128)(2,1)S(1)}, u32[]{:S(2)}, u32[]{:S(2)}) async-start(bf16[16,64,128]{2,1,0:T(8,128)(2,1)} %bitcast.71), calls=%async_computation.4 | async-start | bytes 524288 | tf_op jit(solution)/shard_map/all_to_all | solution.py:766
  249.0 14.5 %all-to-all-done.4 = bf16[16,64,128]{2,1,0:T(8,128)(2,1)S(1)} async-done(((bf16[16,64,128]{2,1,0:T(8,128)(2,1)}), bf16[16,64,128]{2,1,0:T(8,128)(2,1)S(1)}, u32[]{:S(2)}, u32[]{:S(2)}) %all-to-all-start.4) | async-done | bytes 262176 | tf_op jit(solution)/shard_map/all_to_all | solution.py:766
  268.2 12.9 %merge_backward.1 = (f32[1024,128]{1,0:T(8,128)}, f32[1024,128]{1,0:T(8,128)}, f32[1024,128]{1,0:T(8,128)}, f32[1024,128]{1,0:T(8,128)}, f32[1024,128]{1,0:T(8,128)}) custom-call(f32[1024,128]{1,0:T(8,128)} %get-tuple-element.107.own, f32[1024,640]{1,0:T(8,128)} %convolution_add_fusion.q_ref.k_ref.h_ref.g_ref.v, f32[1024,128]{1,0:T(8,128)} %get-tuple-element.108.qm, ...), custom_call_target="tpu_custom_call" | custom-call | flops 1 | bytes 1 | tf_op jit(solution)/shard_map/merge_backward/pallas_call | solution.py:467
  285.1 4.1 reduce-scatter.2.cloned.1.call-done
  293.5 11.1 %leaf_backward.1.grad_ref = bf16[1024,640]{1,0:T(8,128)(2,1)} custom-call(f32[1024,640]{1,0:T(8,128)} %convolution_add_fusion.q_ref.k_ref.h_ref.g_ref.v, f32[1024,640]{1,0:T(8,128)} %convolution_add_fusion.q_ref.k_ref.h_ref.g_ref.v, f32[1024,640]{1,0:T(8,128)} %convolution_add_fusion.q_ref.k_ref.h_ref.g_ref.v, ...), custom_call_target="tpu_custom_call" | custom-call | flops 1 | bytes 1 | tf_op jit(solution)/shard_map/leaf_backward/pallas_call | solution.py:377
  313.7 7.1 %pair_grads.1 = (bf16[16,112,512]{2,1,0:T(8,128)(2,1)}, f32[1,1536]{1,0:T(1,128)}) custom-call(bf16[1024,1536]{1,0:T(8,128)(2,1)} %bitcast.391, bf16[1024,640]{1,0:T(8,128)(2,1)} %leaf_backward.1.grad_ref, bf16[1536,640]{1,0:T(8,128)(2,1)} %copy-done.9, f32[1,1536]{1,0:T(1,128)} %reshape.240.gain_ref), custom_call_target="tpu_custom_call" | custom-call | flops 12000000000 | bytes 36000000 | tf_op jit(solution)/shard_map/pair_grads/pallas_call | solution.py:638
  327.7 4.6 %all-to-all-start.5 = ((bf16[16,112,512]{2,1,0:T(8,128)(2,1)}), bf16[16,112,512]{2,1,0:T(8,128)(2,1)S(1)}, u32[]{:S(2)}, u32[]{:S(2)}) async-start(bf16[16,112,512]{2,1,0:T(8,128)(2,1)} %get-tuple-element.164), calls=%async_computation.6 | async-start | bytes 3670016 | tf_op jit(solution)/shard_map/all_to_all | solution.py:793
  337.0 5.2 %collective-permute-done.25 = f32[2,1536]{1,0:T(2,128)S(1)} collective-permute-done((f32[2,1536]{1,0:T(2,128)S(1)}, f32[2,1536]{1,0:T(2,128)S(1)}, u32[]{:S(2)}, u32[]{:S(2)}) %collective-permute-start.25) | collective-permute-done | bytes 12320 | tf_op jit(solution)/shard_map/ppermute | solution.py:501
  343.1 9.4 %collective-permute-done.22 = bf16[2,2,64,1536]{3,2,0,1:T(8,128)(2,1)S(1)} collective-permute-done((bf16[2,2,64,1536]{3,2,0,1:T(8,128)(2,1)S(1)}, bf16[2,2,64,1536]{3,2,0,1:T(8,128)(2,1)S(1)}, u32[]{:S(2)}, u32[]{:S(2)}) %collective-permute-start.22) | collective-permute-done | bytes 786464 | tf_op jit(solution)/shard_map/ppermute | solution.py:501
  354.4 15.1 %collective-permute-done.23 = bf16[2,64,1536]{2,1,0:T(8,128)(2,1)S(1)} collective-permute-done((bf16[2,64,1536]{2,1,0:T(8,128)(2,1)S(1)}, bf16[2,64,1536]{2,1,0:T(8,128)(2,1)S(1)}, u32[]{:S(2)}, u32[]{:S(2)}) %collective-permute-start.23) | collective-permute-done | bytes 393248 | tf_op jit(solution)/shard_map/ppermute | solution.py:501
  381.1 3.9 collective-permute-start.31
  387.0 9.9 %all-to-all-start.6 = ((bf16[16,96,192]{1,2,0:T(8,128)(2,1)}), bf16[16,96,192]{1,2,0:T(8,128)(2,1)S(1)}, u32[]{:S(2)}, u32[]{:S(2)}) async-start(bf16[16,96,192]{1,2,0:T(8,128)(2,1)} %copy.143), calls=%async_computation.7 | async-start | bytes 1572864 | tf_op jit(solution)/shard_map/all_to_all | solution.py:818
  397.9 8.6 %collective-permute-start.32 = (f32[2,1536]{1,0:T(2,128)S(1)}, f32[2,1536]{1,0:T(2,128)S(1)}, u32[]{:S(2)}, u32[]{:S(2)}) collective-permute-start(f32[2,1536]{1,0:T(2,128)S(1)} %add.230), channel_id=1, source_target_pairs={{0,8},{8,0},{1,9},{9,1},{2,10},{10,2},{3,11},{11,3},{4,12},{12,4},... | collective-permute-start | bytes 36872 | tf_op jit(solution)/shard_map/ppermute | solution.py:501
  416.2 3.7 all-to-all-done.6
  (307 shorter events, 127.5 us)
Async XLA Ops:
  7.2 80.6 %all-gather.3.cloned.1.call-start = ((), (), s32[]{:S(2)}) async-start(), calls=%async_computation.8 | async-start | bytes 3538944 | tf_op jit(solution)/shard_map/all_gather | solution.py:698
  9.8 14.2 %collective-permute-start.3 = (bf16[64,1536]{1,0:T(8,128)(2,1)S(1)}, bf16[64,1536]{1,0:T(8,128)(2,1)}, u32[]{:S(2)}, u32[]{:S(2)}) collective-permute-start(bf16[64,1536]{1,0:T(8,128)(2,1)S(1)} %dynamic-slice_bitcast_fusion.9), channel_id=1, source_target_pairs={{0,16},{16,0},{1,17},{17,1},{2,18},{18,2},{3,19},{19,3},{4,20},{20... | collective-permute-start | bytes 589832 | tf_op jit(solution)/shard_map/ppermute | solution.py:501
  12.7 20.1 %collective-permute-start = (bf16[2,96,1536]{2,1,0:T(8,128)(2,1)S(1)}, bf16[2,96,1536]{2,1,0:T(8,128)(2,1)}, u32[]{:S(2)}, u32[]{:S(2)}) collective-permute-start(bf16[2,96,1536]{2,1,0:T(8,128)(2,1)S(1)} %dynamic-slice_bitcast_fusion.4), channel_id=1, source_target_pairs={{0,4},{4,0},{1,5},{5,1},{2,6},{6,2},{3,7},{7,3},{8,12},{12,8},{9,1... | collective-permute-start | bytes 1769480 | tf_op jit(solution)/shard_map/ppermute | solution.py:501
  17.2 13.7 %collective-permute-start.2 = (bf16[2,96,768]{2,1,0:T(8,128)(2,1)S(1)}, bf16[2,96,768]{2,1,0:T(8,128)(2,1)}, u32[]{:S(2)}, u32[]{:S(2)}) collective-permute-start(bf16[2,96,768]{2,1,0:T(8,128)(2,1)S(1)} %pad_maximum_fusion.16), channel_id=1, source_target_pairs={{0,8},{8,0},{1,9},{9,1},{2,10},{10,2},{3,11},{11,3},{4,12},{12,4},... | collective-permute-start | bytes 884744 | tf_op jit(solution)/shard_map/ppermute | solution.py:501
  35.5 49.1 %all-to-all-start = ((bf16[16,112,512]{2,1,0:T(8,128)(2,1)}), bf16[16,112,512]{2,1,0:T(8,128)(2,1)S(1)}, u32[]{:S(2)}, u32[]{:S(2)}) async-start(bf16[16,112,512]{2,1,0:T(8,128)(2,1)} %bitcast.9), calls=%async_computation | async-start | bytes 3670016 | tf_op jit(solution)/shard_map/all_to_all | solution.py:706
  43.1 137.9 %all-gather.5.cloned.1.call-start = ((), (), s32[]{:S(2)}) async-start(), calls=%async_computation.9 | async-start | bytes 5898240 | tf_op jit(solution)/shard_map/all_gather | solution.py:678
  95.1 14.1 %collective-permute-start.5 = (bf16[2,2,96,768]{3,2,1,0:T(8,128)(2,1)S(1)}, bf16[2,2,96,768]{3,2,1,0:T(8,128)(2,1)S(1)}, u32[]{:S(2)}, u32[]{:S(2)}) collective-permute-start(bf16[2,2,96,768]{3,2,1,0:T(8,128)(2,1)S(1)} %copy-done.8), channel_id=1, source_target_pairs={{0,4},{4,0},{1,5},{5,1},{2,6},{6,2},{3,7},{7,3},{8,12},{12,8},{9,1... | collective-permute-start | bytes 1769480 | tf_op jit(solution)/shard_map/ppermute | solution.py:501
  122.1 19.4 %all-to-all-start.1 = ((bf16[16,64,128]{2,1,0:T(8,128)(2,1)}), bf16[16,64,128]{2,1,0:T(8,128)(2,1)}, u32[]{:S(2)}, u32[]{:S(2)}) async-start(bf16[16,64,128]{2,1,0:T(8,128)(2,1)} %bitcast.46), calls=%async_computation.1 | async-start | bytes 524288 | tf_op jit(solution)/shard_map/all_to_all | solution.py:736
  145.7 12.3 %collective-permute-start.9 = (bf16[2,2,64,1536]{3,2,0,1:T(8,128)(2,1)}, bf16[2,2,64,1536]{3,2,0,1:T(8,128)(2,1)}, u32[]{:S(2)}, u32[]{:S(2)}) collective-permute-start(bf16[2,2,64,1536]{3,2,0,1:T(8,128)(2,1)} %pad_maximum_fusion.9), channel_id=1, source_target_pairs={{0,2},{2,0},{1,3},{3,1},{4,6},{6,4},{5,7},{7,5},{8,10},{10,8},{9,1... | collective-permute-start | bytes 2359304 | tf_op jit(solution)/shard_map/ppermute | solution.py:501
  151.1 23.9 %all-to-all-start.2 = ((bf16[8,64,1536]{2,1,0:T(8,128)(2,1)}), bf16[8,64,1536]{2,1,0:T(8,128)(2,1)}, u32[]{:S(2)}, u32[]{:S(2)}) async-start(bf16[8,64,1536]{2,1,0:T(8,128)(2,1)} %broadcast_in_dim.17), calls=%async_computation.2 | async-start | bytes 3145728 | tf_op jit(solution)/shard_map/all_to_all | solution.py:549
  157.7 131.5 %reduce-scatter.2.cloned.1.call-start = ((), (), s32[]{:S(2)}) async-start(), calls=%async_computation.10 | async-start | bytes 5898240 | tf_op jit(solution)/shard_map/reduce_scatter | solution.py:684
  197.5 27.1 %all-to-all-start.3 = ((bf16[8,64,1536]{2,1,0:T(8,128)(2,1)}), bf16[8,64,1536]{2,1,0:T(8,128)(2,1)}, u32[]{:S(2)}, u32[]{:S(2)}) async-start(bf16[8,64,1536]{2,1,0:T(8,128)(2,1)} %bitcast.362), calls=%async_computation.3 | async-start | bytes 3145728 | tf_op jit(solution)/shard_map/all_to_all | solution.py:554
  205.8 18.0 %collective-permute-start.10 = (bf16[2,128,192]{1,2,0:T(8,128)(2,1)S(1)}, bf16[2,128,192]{1,2,0:T(8,128)(2,1)S(1)}, u32[]{:S(2)}, u32[]{:S(2)}) collective-permute-start(bf16[2,128,192]{1,2,0:T(8,128)(2,1)S(1)} %dynamic-slice_bitcast_fusion.11), channel_id=1, source_target_pairs={{0,4},{4,0},{1,5},{5,1},{2,6},{6,2},{3,7},{7,3},{8,12},{12,8},{9,1... | collective-permute-start | bytes 294920 | tf_op jit(solution)/shard_map/ppermute | solution.py:501
  238.1 25.4 %all-to-all-start.4 = ((bf16[16,64,128]{2,1,0:T(8,128)(2,1)}), bf16[16,64,128]{2,1,0:T(8,128)(2,1)S(1)}, u32[]{:S(2)}, u32[]{:S(2)}) async-start(bf16[16,64,128]{2,1,0:T(8,128)(2,1)} %bitcast.71), calls=%async_computation.4 | async-start | bytes 524288 | tf_op jit(solution)/shard_map/all_to_all | solution.py:766
  247.7 18.5 %collective-permute-start.15 = (f32[64,1536]{1,0:T(8,128)S(1)}, f32[64,1536]{1,0:T(8,128)}, u32[]{:S(2)}, u32[]{:S(2)}) collective-permute-start(f32[64,1536]{1,0:T(8,128)S(1)} %copy-done.11), channel_id=1, source_target_pairs={{0,1},{1,0},{2,3},{3,2},{4,5},{5,4},{6,7},{7,6},{8,9},{9,8},{10,11... | collective-permute-start | bytes 1179656 | tf_op jit(solution)/shard_map/ppermute | solution.py:501
  264.4 16.7 %collective-permute-start.13 = (bf16[2,64,1536]{2,1,0:T(8,128)(2,1)S(1)}, bf16[2,64,1536]{2,1,0:T(8,128)(2,1)S(1)}, u32[]{:S(2)}, u32[]{:S(2)}) collective-permute-start(bf16[2,64,1536]{2,1,0:T(8,128)(2,1)S(1)} %pad_maximum_fusion.14), channel_id=1, source_target_pairs={{0,4},{4,0},{1,5},{5,1},{2,6},{6,2},{3,7},{7,3},{8,12},{12,8},{9,1... | collective-permute-start | bytes 1179656 | tf_op jit(solution)/shard_map/ppermute | solution.py:501
  266.0 18.9 %collective-permute-start.12 = (bf16[2,2,64,1536]{3,2,0,1:T(8,128)(2,1)S(1)}, bf16[2,2,64,1536]{3,2,0,1:T(8,128)(2,1)S(1)}, u32[]{:S(2)}, u32[]{:S(2)}) collective-permute-start(bf16[2,2,64,1536]{3,2,0,1:T(8,128)(2,1)S(1)} %bitcast.378), channel_id=1, source_target_pairs={{0,1},{1,0},{2,3},{3,2},{4,5},{5,4},{6,7},{7,6},{8,9},{9,8},{10,11... | collective-permute-start | bytes 2359304 | tf_op jit(solution)/shard_map/ppermute | solution.py:501
  289.2 15.4 %collective-permute-start.14 = (bf16[2,64,1536]{2,1,0:T(8,128)(2,1)S(1)}, bf16[2,64,1536]{2,1,0:T(8,128)(2,1)S(1)}, u32[]{:S(2)}, u32[]{:S(2)}) collective-permute-start(bf16[2,64,1536]{2,1,0:T(8,128)(2,1)S(1)} %dynamic-slice_bitcast_fusion.6), channel_id=1, source_target_pairs={{0,2},{2,0},{1,3},{3,1},{4,6},{6,4},{5,7},{7,5},{8,10},{10,8},{9,1... | collective-permute-start | bytes 1179656 | tf_op jit(solution)/shard_map/ppermute | solution.py:501
  291.0 15.0 %collective-permute-start.16 = (bf16[2,96,1536]{2,1,0:T(8,128)(2,1)S(1)}, bf16[2,96,1536]{2,1,0:T(8,128)(2,1)S(1)}, u32[]{:S(2)}, u32[]{:S(2)}) collective-permute-start(bf16[2,96,1536]{2,1,0:T(8,128)(2,1)S(1)} %dynamic-slice_bitcast_fusion.2), channel_id=1, source_target_pairs={{0,4},{4,0},{1,5},{5,1},{2,6},{6,2},{3,7},{7,3},{8,12},{12,8},{9,1... | collective-permute-start | bytes 1769480 | tf_op jit(solution)/shard_map/ppermute | solution.py:501
  293.2 13.0 %collective-permute-start.17 = (bf16[2,2,64,1536]{3,2,0,1:T(8,128)(2,1)S(1)}, bf16[2,2,64,1536]{3,2,0,1:T(8,128)(2,1)S(1)}, u32[]{:S(2)}, u32[]{:S(2)}) collective-permute-start(bf16[2,2,64,1536]{3,2,0,1:T(8,128)(2,1)S(1)} %pad_maximum_fusion.10), channel_id=1, source_target_pairs={{0,2},{2,0},{1,3},{3,1},{4,6},{6,4},{5,7},{7,5},{8,10},{10,8},{9,1... | collective-permute-start | bytes 2359304 | tf_op jit(solution)/shard_map/ppermute | solution.py:501
  307.8 13.0 %collective-permute-start.20 = (bf16[64,1536]{1,0:T(8,128)(2,1)S(1)}, bf16[64,1536]{1,0:T(8,128)(2,1)}, u32[]{:S(2)}, u32[]{:S(2)}) collective-permute-start(bf16[64,1536]{1,0:T(8,128)(2,1)S(1)} %dynamic-slice_bitcast_fusion.8), channel_id=1, source_target_pairs={{0,4},{4,0},{1,5},{5,1},{2,6},{6,2},{3,7},{7,3},{8,12},{12,8},{9,1... | collective-permute-start | bytes 589832 | tf_op jit(solution)/shard_map/ppermute | solution.py:501
  309.1 13.3 %collective-permute-start.19 = (bf16[2,96,1536]{2,1,0:T(8,128)(2,1)S(1)}, bf16[2,96,1536]{2,1,0:T(8,128)(2,1)}, u32[]{:S(2)}, u32[]{:S(2)}) collective-permute-start(bf16[2,96,1536]{2,1,0:T(8,128)(2,1)S(1)} %dynamic-slice_bitcast_fusion.1), channel_id=1, source_target_pairs={{0,2},{2,0},{1,3},{3,1},{4,6},{6,4},{5,7},{7,5},{8,10},{10,8},{9,1... | collective-permute-start | bytes 1769480 | tf_op jit(solution)/shard_map/ppermute | solution.py:501
  327.7 52.2 %all-to-all-start.5 = ((bf16[16,112,512]{2,1,0:T(8,128)(2,1)}), bf16[16,112,512]{2,1,0:T(8,128)(2,1)S(1)}, u32[]{:S(2)}, u32[]{:S(2)}) async-start(bf16[16,112,512]{2,1,0:T(8,128)(2,1)} %get-tuple-element.164), calls=%async_computation.6 | async-start | bytes 3670016 | tf_op jit(solution)/shard_map/all_to_all | solution.py:793
  333.7 18.8 %collective-permute-start.22 = (bf16[2,2,64,1536]{3,2,0,1:T(8,128)(2,1)S(1)}, bf16[2,2,64,1536]{3,2,0,1:T(8,128)(2,1)S(1)}, u32[]{:S(2)}, u32[]{:S(2)}) collective-permute-start(bf16[2,2,64,1536]{3,2,0,1:T(8,128)(2,1)S(1)} %dynamic-slice_bitcast_fusion), channel_id=1, source_target_pairs={{0,1},{1,0},{2,3},{3,2},{4,5},{5,4},{6,7},{7,6},{8,9},{9,8},{10,11... | collective-permute-start | bytes 2359304 | tf_op jit(solution)/shard_map/ppermute | solution.py:501
  352.8 16.7 %collective-permute-start.23 = (bf16[2,64,1536]{2,1,0:T(8,128)(2,1)S(1)}, bf16[2,64,1536]{2,1,0:T(8,128)(2,1)S(1)}, u32[]{:S(2)}, u32[]{:S(2)}) collective-permute-start(bf16[2,64,1536]{2,1,0:T(8,128)(2,1)S(1)} %dynamic-slice_bitcast_fusion.5), channel_id=1, source_target_pairs={{0,4},{4,0},{1,5},{5,1},{2,6},{6,2},{3,7},{7,3},{8,12},{12,8},{9,1... | collective-permute-start | bytes 1179656 | tf_op jit(solution)/shard_map/ppermute | solution.py:501
  354.0 24.8 %collective-permute-start.27 = (f32[2,1536]{1,0:T(2,128)S(1)}, f32[2,1536]{1,0:T(2,128)S(1)}, u32[]{:S(2)}, u32[]{:S(2)}) collective-permute-start(f32[2,1536]{1,0:T(2,128)S(1)} %fusion.70), channel_id=1, source_target_pairs={{0,1},{1,0},{2,3},{3,2},{4,5},{5,4},{6,7},{7,6},{8,9},{9,8},{10,11... | collective-permute-start | bytes 36872 | tf_op jit(solution)/shard_map/ppermute | solution.py:501
  380.1 33.7 %collective-permute-start.30 = (bf16[64,1536]{1,0:T(8,128)(2,1)S(1)}, bf16[64,1536]{1,0:T(8,128)(2,1)S(1)}, u32[]{:S(2)}, u32[]{:S(2)}) collective-permute-start(bf16[64,1536]{1,0:T(8,128)(2,1)S(1)} %fusion.30), channel_id=1, source_target_pairs={{0,1},{1,17},{16,0},{17,16},{2,3},{3,19},{18,2},{19,18},{4,5},{5,2... | collective-permute-start | bytes 589832 | tf_op jit(solution)/shard_map/ppermute | solution.py:813
  380.4 33.4 %collective-permute-start.29 = (bf16[64,1536]{1,0:T(8,128)(2,1)S(1)}, bf16[64,1536]{1,0:T(8,128)(2,1)S(1)}, u32[]{:S(2)}, u32[]{:S(2)}) collective-permute-start(bf16[64,1536]{1,0:T(8,128)(2,1)S(1)} %fusion.30), channel_id=1, source_target_pairs={{0,0},{1,16},{16,1},{17,17},{2,2},{3,18},{18,3},{19,19},{4,4},{5,2... | collective-permute-start | bytes 589832 | tf_op jit(solution)/shard_map/ppermute | solution.py:812
  381.1 16.8 %collective-permute-start.31 = (f32[2,1536]{1,0:T(2,128)S(1)}, f32[2,1536]{1,0:T(2,128)S(1)}, u32[]{:S(2)}, u32[]{:S(2)}) collective-permute-start(f32[2,1536]{1,0:T(2,128)S(1)} %add.225), channel_id=1, source_target_pairs={{0,16},{16,0},{1,17},{17,1},{2,18},{18,2},{3,19},{19,3},{4,20},{20... | collective-permute-start | bytes 36872 | tf_op jit(solution)/shard_map/ppermute | solution.py:501
  385.1 28.8 %collective-permute-start.28 = (bf16[64,1536]{1,0:T(8,128)(2,1)S(1)}, bf16[64,1536]{1,0:T(8,128)(2,1)S(1)}, u32[]{:S(2)}, u32[]{:S(2)}) collective-permute-start(bf16[64,1536]{1,0:T(8,128)(2,1)S(1)} %add_convert_fusion), channel_id=1, source_target_pairs={{0,1},{1,0},{2,3},{3,2},{4,5},{5,4},{6,7},{7,6},{8,9},{9,8},{10,11... | collective-permute-start | bytes 589832 | tf_op jit(solution)/shard_map/ppermute | solution.py:501
  387.0 32.9 %all-to-all-start.6 = ((bf16[16,96,192]{1,2,0:T(8,128)(2,1)}), bf16[16,96,192]{1,2,0:T(8,128)(2,1)S(1)}, u32[]{:S(2)}, u32[]{:S(2)}) async-start(bf16[16,96,192]{1,2,0:T(8,128)(2,1)} %copy.143), calls=%async_computation.7 | async-start | bytes 1572864 | tf_op jit(solution)/shard_map/all_to_all | solution.py:818
  397.9 13.8 %collective-permute-start.32 = (f32[2,1536]{1,0:T(2,128)S(1)}, f32[2,1536]{1,0:T(2,128)S(1)}, u32[]{:S(2)}, u32[]{:S(2)}) collective-permute-start(f32[2,1536]{1,0:T(2,128)S(1)} %add.230), channel_id=1, source_target_pairs={{0,8},{8,0},{1,9},{9,1},{2,10},{10,2},{3,11},{11,3},{4,12},{12,4},... | collective-permute-start | bytes 36872 | tf_op jit(solution)/shard_map/ppermute | solution.py:501
  (50 other events, 305.4 us)
Sparse Core Ops, SparseCore 0:
  25.9 38.6 all-gather.2
  89.1 91.7 all-gather.4
  197.6 91.5 reduce-scatter.1

commit v4 on v3

--- a/solution.py
+++ b/solution.py
@@ -347,14 +347,14 @@
     return pltpu.CompilerParams(vmem_limit_bytes=56 * 1024 * 1024)
 
 
-def leaf_group(length):
+def leaf_group(length, most):
     leaves = length // LEAF
-    return 4 if leaves % 4 == 0 else 1
+    return next(g for g in (most, 4, 2, 1) if leaves % g == 0)
 
 
 def leaf_forward(proj):
     length = proj.shape[0]
-    leaves = leaf_group(length)
+    leaves = leaf_group(length, 8)
     rows = leaves * LEAF
     column = lambda j: pl.BlockSpec((rows, LEAF), lambda i, j=j: (i, j))
     return pl.pallas_call(
@@ -371,7 +371,7 @@
 
 def leaf_backward(proj, saved, grads):
     length = proj.shape[0]
-    leaves = leaf_group(length)
+    leaves = leaf_group(length, 4)
     rows = leaves * LEAF
     column = lambda j: pl.BlockSpec((rows, LEAF), lambda i, j=j: (i, j))
     return pl.pallas_call(
@@ -600,7 +600,7 @@
 def mlp_grads_of(act, grad, rows, hidden):
     tokens, width = act.shape
     units = hidden.shape[1]
-    step = 2 * LEAF
+    step = width // 2
     column = pl.BlockSpec((tokens, step), lambda i: (0, i))
     return pl.pallas_call(
         mlp_grads_kernel,
@@ -830,7 +830,7 @@
     total = total[0] + total[1]
     grads = [total[..., i * LEAF : (i + 1) * LEAF].transpose(1, 0, 2).reshape(rows, half_heads * LEAF) for i in range(4)]
 
-    attn_in_grad = after(attn_in_grad, *grads)
+    attn_in_grad, *grads = fence(attn_in_grad, *grads)
     tokens_grad = middle_both + norm_back(attn_in_grad * gain_attn, normalize(both_inputs), both_inputs)
     return (
         block_out, tokens_grad, *grads, beta_grad, bias_grad, out_weight_grad, gate_grad, up_grad, down_grad, gains[0], gains[1]

time: 435 us -> 431 us (level)
  no operation moved by 1% of the time
where the time goes in v4:
time: 431 us; the launch traced here: 427 us
  waiting for transfers between devices  157 us (36%)
  starting transfers between devices  88.4 us (21%)
  Pallas kernels  66.5 us (15%)
  local copies, waits for them, and re-layouts  44.5 us (10%)
  other arithmetic  39.4 us (9%)
  matrix products  16 us (4%)
  between operations  15.3 us (4%)
    ppermute x31, waiting for transfers between devices, swap(): return lax.ppermute(value, axis, [(0, 1), (1, 0)])  71.3 us
    ppermute x31, starting transfers between devices, swap(): return lax.ppermute(value, axis, [(0, 1), (1, 0)])  39.1 us
    all_to_all x1, waiting for transfers between devices, local(): packed = lax.all_to_all(packed, steps, 0, 0, tiled=True)  35.4 us
    another operation x37, other arithmetic, by_index(): jnp.stack([jnp.where(first, own, other), jnp.where(first, other, own)], a...  19.6 us
    dot_general x6, matrix products, dot(): lax.dot_general(a, b, (dims, ((), ())), preferred_element_type=jnp.float32)  16 us
    all_to_all x1, waiting for transfers between devices, local(): lax.all_to_all(attended_grad, steps, 0, 0, tiled=True).reshape(length, LEAF)  14.7 us
    all_to_all x1, waiting for transfers between devices, copies(): lax.all_to_all(jnp.broadcast_to(value, (lax.axis_size(axes), *value.shape...  14.5 us
    pallas_call x1, Pallas kernels, run_merge_backward(): pl.pallas_call(functools.partial(merge_backward_kernel, length, scale), g...  12.9 us
  transfers between devices with their start and end apart: 43, of which 20 were waited for; matrix products, arithmetic and copies ran while one was open for 21% of the time, Pallas kernels for 12%

profile of v4, /device:TPU:21, one launch (start us, length us, event | category | flops | bytes accessed | tf_op | source)
XLA Modules:
  0.0 426.8 jit_solution(4986964236232705992)
XLA Ops:
  17.2 6.7 %collective-permute-start.2 = (bf16[2,96,768]{2,1,0:T(8,128)(2,1)S(1)}, bf16[2,96,768]{2,1,0:T(8,128)(2,1)}, u32[]{:S(2)}, u32[]{:S(2)}) collective-permute-start(bf16[2,96,768]{2,1,0:T(8,128)(2,1)S(1)} %pad_maximum_fusion.16), channel_id=1, source_target_pairs={{0,8},{8,0},{1,9},{9,1},{2,10},{10,2},{3,11},{11,3},{4,12},{12,4},... | collective-permute-start | bytes 884744 | tf_op jit(solution)/shard_map/ppermute | solution.py:501
  35.5 7.6 %all-to-all-start = ((bf16[16,112,512]{2,1,0:T(8,128)(2,1)}), bf16[16,112,512]{2,1,0:T(8,128)(2,1)S(1)}, u32[]{:S(2)}, u32[]{:S(2)}) async-start(bf16[16,112,512]{2,1,0:T(8,128)(2,1)} %bitcast.9), calls=%async_computation | async-start | bytes 3670016 | tf_op jit(solution)/shard_map/all_to_all | solution.py:706
  49.2 35.4 %all-to-all-done = bf16[16,112,512]{2,1,0:T(8,128)(2,1)S(1)} async-done(((bf16[16,112,512]{2,1,0:T(8,128)(2,1)}), bf16[16,112,512]{2,1,0:T(8,128)(2,1)S(1)}, u32[]{:S(2)}, u32[]{:S(2)}) %all-to-all-start) | async-done | bytes 1835040 | tf_op jit(solution)/shard_map/all_to_all | solution.py:706
  89.0 6.0 %convolution_add_fusion.q_ref.k_ref.h_ref.g_ref.v = f32[1024,640]{1,0:T(8,128)} fusion(bf16[1024,1536]{1,0:T(8,128)(2,1)} %bitcast.390, bf16[1536,640]{1,0:T(8,128)(2,1)S(1)} %fusion.2.weight_ref, f32[640]{0:T(1024)S(1)} %pad.129), kind=kOutput, calls=%fused_computation.12 | convolution fusion | flops 2013921280 | bytes 7735808 | tf_op jit(solution)/shard_map/dot_general | solution.py:493
  95.1 10.2 %leaf_forward.1 = (f32[1024,128]{1,0:T(8,128)}, f32[1024,128]{1,0:T(8,128)}, f32[1024,128]{1,0:T(8,128)}, f32[1024,128]{1,0:T(8,128)}, f32[1024,128]{1,0:T(8,128...) custom-call(f32[1024,640]{1,0:T(8,128)} %convolution_add_fusion.q_re, ...), custom_call_target="tpu_custom_call" | custom-call | flops 1 | bytes 1 | tf_op jit(solution)/shard_map/leaf_forward/pallas_call | solution.py:360
  105.3 3.9 collective-permute-done.5
  111.1 10.0 %merge_forward.1 = (f32[1024,128]{1,0:T(8,128)}, bf16[1024,128]{1,0:T(8,128)(2,1)}, f32[1024,128]{1,0:T(8,128)}, f32[1024,128]{1,0:T(8,128)}, f32[1024,128]{1,0:...) custom-call(f32[1024,128]{1,0:T(8,128)} %get-tuple-element.111.own, ...), custom_call_target="tpu_custom_call" | custom-call | flops 1 | bytes 1 | tf_op jit(solution)/shard_map/merge_forward/pallas_call | solution.py:432
  122.3 5.6 %all-to-all-start.1 = ((bf16[16,64,128]{2,1,0:T(8,128)(2,1)}), bf16[16,64,128]{2,1,0:T(8,128)(2,1)}, u32[]{:S(2)}, u32[]{:S(2)}) async-start(bf16[16,64,128]{2,1,0:T(8,128)(2,1)} %bitcast.46), calls=%async_computation.1 | async-start | bytes 524288 | tf_op jit(solution)/shard_map/all_to_all | solution.py:736
  127.9 5.6 %collective-permute-done.8 = bf16[2,64,1536]{2,1,0:T(8,128)(2,1)} collective-permute-done((bf16[2,64,1536]{2,1,0:T(8,128)(2,1)S(1)}, bf16[2,64,1536]{2,1,0:T(8,128)(2,1)}, u32[]{:S(2)}, u32[]{:S(2)}) %collective-permute-start.8) | collective-permute-done | bytes 393248 | tf_op jit(solution)/shard_map/ppermute | solution.py:501
  134.5 7.2 %all-to-all-done.1 = bf16[16,64,128]{2,1,0:T(8,128)(2,1)} async-done(((bf16[16,64,128]{2,1,0:T(8,128)(2,1)}), bf16[16,64,128]{2,1,0:T(8,128)(2,1)}, u32[]{:S(2)}, u32[]{:S(2)}) %all-to-all-start.1) | async-done | bytes 262176 | tf_op jit(solution)/shard_map/all_to_all | solution.py:736
  151.3 6.7 %all-to-all-start.2 = ((bf16[8,64,1536]{2,1,0:T(8,128)(2,1)}), bf16[8,64,1536]{2,1,0:T(8,128)(2,1)}, u32[]{:S(2)}, u32[]{:S(2)}) async-start(bf16[8,64,1536]{2,1,0:T(8,128)(2,1)} %broadcast_in_dim.17), calls=%async_computation.2 | async-start | bytes 3145728 | tf_op jit(solution)/shard_map/all_to_all | solution.py:549
  160.7 14.5 %all-to-all-done.2 = bf16[8,64,1536]{2,1,0:T(8,128)(2,1)} async-done(((bf16[8,64,1536]{2,1,0:T(8,128)(2,1)}), bf16[8,64,1536]{2,1,0:T(8,128)(2,1)}, u32[]{:S(2)}, u32[]{:S(2)}) %all-to-all-start.2) | async-done | bytes 1572896 | tf_op jit(solution)/shard_map/all_to_all | solution.py:549
  175.2 5.8 %all-gather.5.cloned.1.call-done.weight_ref = bf16[1536,1536]{1,0:T(8,128)(2,1)} async-done(((bf16[384,1536]{1,0:T(8,128)(2,1)}), bf16[1536,1536]{1,0:T(8,128)(2,1)}) %all-gather.5.cloned.1.call-update) | async-done | bytes 4718608 | tf_op jit(solution)/shard_map/all_gather | solution.py:678
  181.0 8.9 %mlp.1 = (bf16[512,1024]{1,0:T(8,128)(2,1)}, bf16[512,512]{1,0:T(8,128)(2,1)}, bf16[512,1536]{1,0:T(8,128)(2,1)}) custom-call(bf16[512,1536]{1,0:T(8,128)(2,1)} %bitcast.54.act_ref, bf16[512,1536]{1,0:T(8,128)(2,1)} %bitcast.349, bf16[1536,1536]{1,0:T(8,128)(2,1)} %all-gather.5.cloned.1.call-done.weight_ref), custom_call_target="tpu_custom_call" | custom-call | flops 1 | bytes 1 | tf_op jit(solution)/shard_map/mlp/pallas_call | solution.py:583
  189.9 6.2 %mlp_grads.1 = bf16[1536,1536]{1,0:T(8,128)(2,1)} custom-call(bf16[512,1536]{1,0:T(8,128)(2,1)} %bitcast.54.act_ref, bf16[512,1536]{1,0:T(8,128)(2,1)} %bitcast.350, bf16[512,1024]{1,0:T(8,128)(2,1)} %get-tuple-element.135.rows_ref, bf16[512,512]{1,0:T(8,128)(2,1)} %get-tuple-element.134.hidden_ref), custom_call_target="tpu_custom_call" | custom-call | flops 1 | bytes 1 | tf_op jit(solution)/shard_map/mlp_grads/pallas_call | solution.py:605
  196.1 5.1 %all-to-all-start.3 = ((bf16[8,64,1536]{2,1,0:T(8,128)(2,1)}), bf16[8,64,1536]{2,1,0:T(8,128)(2,1)}, u32[]{:S(2)}, u32[]{:S(2)}) async-start(bf16[8,64,1536]{2,1,0:T(8,128)(2,1)} %bitcast.362), calls=%async_computation.3 | async-start | bytes 3145728 | tf_op jit(solution)/shard_map/all_to_all | solution.py:554
  205.7 3.7 convolution_convert_fusion.1
  209.4 13.0 %collective-permute-done.10 = bf16[2,128,192]{1,2,0:T(8,128)(2,1)S(1)} collective-permute-done((bf16[2,128,192]{1,2,0:T(8,128)(2,1)S(1)}, bf16[2,128,192]{1,2,0:T(8,128)(2,1)S(1)}, u32[]{:S(2)}, u32[]{:S(2)}) %collective-permute-start.10) | collective-permute-done | bytes 98336 | tf_op jit(solution)/shard_map/ppermute | solution.py:501
  226.9 5.7 %collective-permute-done.11 = bf16[64,1536]{1,0:T(8,128)(2,1)S(1)} collective-permute-done((bf16[64,1536]{1,0:T(8,128)(2,1)}, bf16[64,1536]{1,0:T(8,128)(2,1)S(1)}, u32[]{:S(2)}, u32[]{:S(2)}) %collective-permute-start.11) | collective-permute-done | bytes 196640 | tf_op jit(solution)/shard_map/ppermute | solution.py:501
  236.8 8.3 %all-to-all-start.4 = ((bf16[16,64,128]{2,1,0:T(8,128)(2,1)}), bf16[16,64,128]{2,1,0:T(8,128)(2,1)S(1)}, u32[]{:S(2)}, u32[]{:S(2)}) async-start(bf16[16,64,128]{2,1,0:T(8,128)(2,1)} %bitcast.71), calls=%async_computation.4 | async-start | bytes 524288 | tf_op jit(solution)/shard_map/all_to_all | solution.py:766
  247.4 14.7 %all-to-all-done.4 = bf16[16,64,128]{2,1,0:T(8,128)(2,1)S(1)} async-done(((bf16[16,64,128]{2,1,0:T(8,128)(2,1)}), bf16[16,64,128]{2,1,0:T(8,128)(2,1)S(1)}, u32[]{:S(2)}, u32[]{:S(2)}) %all-to-all-start.4) | async-done | bytes 262176 | tf_op jit(solution)/shard_map/all_to_all | solution.py:766
  266.8 12.9 %merge_backward.1 = (f32[1024,128]{1,0:T(8,128)}, f32[1024,128]{1,0:T(8,128)}, f32[1024,128]{1,0:T(8,128)}, f32[1024,128]{1,0:T(8,128)}, f32[1024,128]{1,0:T(8,128)}) custom-call(f32[1024,128]{1,0:T(8,128)} %get-tuple-element.111.own, f32[1024,640]{1,0:T(8,128)} %convolution_add_fusion.q_ref.k_ref.h_ref.g_ref.v, f32[1024,128]{1,0:T(8,128)} %get-tuple-element.112.qm, ...), custom_call_target="tpu_custom_call" | custom-call | flops 1 | bytes 1 | tf_op jit(solution)/shard_map/merge_backward/pallas_call | solution.py:467
  283.7 4.1 reduce-scatter.2.cloned.1.call-done
  292.1 11.2 %leaf_backward.1.grad_ref = bf16[1024,640]{1,0:T(8,128)(2,1)} custom-call(f32[1024,640]{1,0:T(8,128)} %convolution_add_fusion.q_ref.k_ref.h_ref.g_ref.v, f32[1024,640]{1,0:T(8,128)} %convolution_add_fusion.q_ref.k_ref.h_ref.g_ref.v, f32[1024,640]{1,0:T(8,128)} %convolution_add_fusion.q_ref.k_ref.h_ref.g_ref.v, ...), custom_call_target="tpu_custom_call" | custom-call | flops 1 | bytes 1 | tf_op jit(solution)/shard_map/leaf_backward/pallas_call | solution.py:377
  312.3 7.1 %pair_grads.1 = (bf16[16,112,512]{2,1,0:T(8,128)(2,1)}, f32[1,1536]{1,0:T(1,128)}) custom-call(bf16[1024,1536]{1,0:T(8,128)(2,1)} %bitcast.391, bf16[1024,640]{1,0:T(8,128)(2,1)} %leaf_backward.1.grad_ref, bf16[1536,640]{1,0:T(8,128)(2,1)} %copy-done.9, f32[1,1536]{1,0:T(1,128)} %reshape.240.gain_ref), custom_call_target="tpu_custom_call" | custom-call | flops 12000000000 | bytes 36000000 | tf_op jit(solution)/shard_map/pair_grads/pallas_call | solution.py:638
  326.3 4.6 %all-to-all-start.5 = ((bf16[16,112,512]{2,1,0:T(8,128)(2,1)}), bf16[16,112,512]{2,1,0:T(8,128)(2,1)S(1)}, u32[]{:S(2)}, u32[]{:S(2)}) async-start(bf16[16,112,512]{2,1,0:T(8,128)(2,1)} %get-tuple-element.168), calls=%async_computation.6 | async-start | bytes 3670016 | tf_op jit(solution)/shard_map/all_to_all | solution.py:793
  335.6 5.2 %collective-permute-done.25 = f32[2,1536]{1,0:T(2,128)S(1)} collective-permute-done((f32[2,1536]{1,0:T(2,128)S(1)}, f32[2,1536]{1,0:T(2,128)S(1)}, u32[]{:S(2)}, u32[]{:S(2)}) %collective-permute-start.25) | collective-permute-done | bytes 12320 | tf_op jit(solution)/shard_map/ppermute | solution.py:501
  341.7 9.4 %collective-permute-done.22 = bf16[2,2,64,1536]{3,2,0,1:T(8,128)(2,1)S(1)} collective-permute-done((bf16[2,2,64,1536]{3,2,0,1:T(8,128)(2,1)S(1)}, bf16[2,2,64,1536]{3,2,0,1:T(8,128)(2,1)S(1)}, u32[]{:S(2)}, u32[]{:S(2)}) %collective-permute-start.22) | collective-permute-done | bytes 786464 | tf_op jit(solution)/shard_map/ppermute | solution.py:501
  353.0 15.1 %collective-permute-done.23 = bf16[2,64,1536]{2,1,0:T(8,128)(2,1)S(1)} collective-permute-done((bf16[2,64,1536]{2,1,0:T(8,128)(2,1)S(1)}, bf16[2,64,1536]{2,1,0:T(8,128)(2,1)S(1)}, u32[]{:S(2)}, u32[]{:S(2)}) %collective-permute-start.23) | collective-permute-done | bytes 393248 | tf_op jit(solution)/shard_map/ppermute | solution.py:501
  379.7 3.9 collective-permute-start.31
  385.6 9.9 %all-to-all-start.6 = ((bf16[16,96,192]{1,2,0:T(8,128)(2,1)}), bf16[16,96,192]{1,2,0:T(8,128)(2,1)S(1)}, u32[]{:S(2)}, u32[]{:S(2)}) async-start(bf16[16,96,192]{1,2,0:T(8,128)(2,1)} %copy.143), calls=%async_computation.7 | async-start | bytes 1572864 | tf_op jit(solution)/shard_map/all_to_all | solution.py:818
  396.5 8.6 %collective-permute-start.32 = (f32[2,1536]{1,0:T(2,128)S(1)}, f32[2,1536]{1,0:T(2,128)S(1)}, u32[]{:S(2)}, u32[]{:S(2)}) collective-permute-start(f32[2,1536]{1,0:T(2,128)S(1)} %add.230), channel_id=1, source_target_pairs={{0,8},{8,0},{1,9},{9,1},{2,10},{10,2},{3,11},{11,3},{4,12},{12,4},... | collective-permute-start | bytes 36872 | tf_op jit(solution)/shard_map/ppermute | solution.py:501
  (307 shorter events, 128.7 us)
Async XLA Ops:
  7.2 80.6 %all-gather.3.cloned.1.call-start = ((), (), s32[]{:S(2)}) async-start(), calls=%async_computation.8 | async-start | bytes 3538944 | tf_op jit(solution)/shard_map/all_gather | solution.py:698
  9.8 14.2 %collective-permute-start.3 = (bf16[64,1536]{1,0:T(8,128)(2,1)S(1)}, bf16[64,1536]{1,0:T(8,128)(2,1)}, u32[]{:S(2)}, u32[]{:S(2)}) collective-permute-start(bf16[64,1536]{1,0:T(8,128)(2,1)S(1)} %dynamic-slice_bitcast_fusion.9), channel_id=1, source_target_pairs={{0,16},{16,0},{1,17},{17,1},{2,18},{18,2},{3,19},{19,3},{4,20},{20... | collective-permute-start | bytes 589832 | tf_op jit(solution)/shard_map/ppermute | solution.py:501
  12.7 20.1 %collective-permute-start = (bf16[2,96,1536]{2,1,0:T(8,128)(2,1)S(1)}, bf16[2,96,1536]{2,1,0:T(8,128)(2,1)}, u32[]{:S(2)}, u32[]{:S(2)}) collective-permute-start(bf16[2,96,1536]{2,1,0:T(8,128)(2,1)S(1)} %dynamic-slice_bitcast_fusion.4), channel_id=1, source_target_pairs={{0,4},{4,0},{1,5},{5,1},{2,6},{6,2},{3,7},{7,3},{8,12},{12,8},{9,1... | collective-permute-start | bytes 1769480 | tf_op jit(solution)/shard_map/ppermute | solution.py:501
  17.2 13.7 %collective-permute-start.2 = (bf16[2,96,768]{2,1,0:T(8,128)(2,1)S(1)}, bf16[2,96,768]{2,1,0:T(8,128)(2,1)}, u32[]{:S(2)}, u32[]{:S(2)}) collective-permute-start(bf16[2,96,768]{2,1,0:T(8,128)(2,1)S(1)} %pad_maximum_fusion.16), channel_id=1, source_target_pairs={{0,8},{8,0},{1,9},{9,1},{2,10},{10,2},{3,11},{11,3},{4,12},{12,4},... | collective-permute-start | bytes 884744 | tf_op jit(solution)/shard_map/ppermute | solution.py:501
  35.5 49.1 %all-to-all-start = ((bf16[16,112,512]{2,1,0:T(8,128)(2,1)}), bf16[16,112,512]{2,1,0:T(8,128)(2,1)S(1)}, u32[]{:S(2)}, u32[]{:S(2)}) async-start(bf16[16,112,512]{2,1,0:T(8,128)(2,1)} %bitcast.9), calls=%async_computation | async-start | bytes 3670016 | tf_op jit(solution)/shard_map/all_to_all | solution.py:706
  43.1 137.9 %all-gather.5.cloned.1.call-start = ((), (), s32[]{:S(2)}) async-start(), calls=%async_computation.9 | async-start | bytes 5898240 | tf_op jit(solution)/shard_map/all_gather | solution.py:678
  95.1 14.1 %collective-permute-start.5 = (bf16[2,2,96,768]{3,2,1,0:T(8,128)(2,1)S(1)}, bf16[2,2,96,768]{3,2,1,0:T(8,128)(2,1)S(1)}, u32[]{:S(2)}, u32[]{:S(2)}) collective-permute-start(bf16[2,2,96,768]{3,2,1,0:T(8,128)(2,1)S(1)} %copy-done.8), channel_id=1, source_target_pairs={{0,4},{4,0},{1,5},{5,1},{2,6},{6,2},{3,7},{7,3},{8,12},{12,8},{9,1... | collective-permute-start | bytes 1769480 | tf_op jit(solution)/shard_map/ppermute | solution.py:501
  122.3 19.4 %all-to-all-start.1 = ((bf16[16,64,128]{2,1,0:T(8,128)(2,1)}), bf16[16,64,128]{2,1,0:T(8,128)(2,1)}, u32[]{:S(2)}, u32[]{:S(2)}) async-start(bf16[16,64,128]{2,1,0:T(8,128)(2,1)} %bitcast.46), calls=%async_computation.1 | async-start | bytes 524288 | tf_op jit(solution)/shard_map/all_to_all | solution.py:736
  145.9 12.1 %collective-permute-start.9 = (bf16[2,2,64,1536]{3,2,0,1:T(8,128)(2,1)}, bf16[2,2,64,1536]{3,2,0,1:T(8,128)(2,1)}, u32[]{:S(2)}, u32[]{:S(2)}) collective-permute-start(bf16[2,2,64,1536]{3,2,0,1:T(8,128)(2,1)} %pad_maximum_fusion.9), channel_id=1, source_target_pairs={{0,2},{2,0},{1,3},{3,1},{4,6},{6,4},{5,7},{7,5},{8,10},{10,8},{9,1... | collective-permute-start | bytes 2359304 | tf_op jit(solution)/shard_map/ppermute | solution.py:501
  151.3 23.9 %all-to-all-start.2 = ((bf16[8,64,1536]{2,1,0:T(8,128)(2,1)}), bf16[8,64,1536]{2,1,0:T(8,128)(2,1)}, u32[]{:S(2)}, u32[]{:S(2)}) async-start(bf16[8,64,1536]{2,1,0:T(8,128)(2,1)} %broadcast_in_dim.17), calls=%async_computation.2 | async-start | bytes 3145728 | tf_op jit(solution)/shard_map/all_to_all | solution.py:549
  157.9 129.9 %reduce-scatter.2.cloned.1.call-start = ((), (), s32[]{:S(2)}) async-start(), calls=%async_computation.10 | async-start | bytes 5898240 | tf_op jit(solution)/shard_map/reduce_scatter | solution.py:684
  196.1 27.1 %all-to-all-start.3 = ((bf16[8,64,1536]{2,1,0:T(8,128)(2,1)}), bf16[8,64,1536]{2,1,0:T(8,128)(2,1)}, u32[]{:S(2)}, u32[]{:S(2)}) async-start(bf16[8,64,1536]{2,1,0:T(8,128)(2,1)} %bitcast.362), calls=%async_computation.3 | async-start | bytes 3145728 | tf_op jit(solution)/shard_map/all_to_all | solution.py:554
  204.4 18.0 %collective-permute-start.10 = (bf16[2,128,192]{1,2,0:T(8,128)(2,1)S(1)}, bf16[2,128,192]{1,2,0:T(8,128)(2,1)S(1)}, u32[]{:S(2)}, u32[]{:S(2)}) collective-permute-start(bf16[2,128,192]{1,2,0:T(8,128)(2,1)S(1)} %dynamic-slice_bitcast_fusion.11), channel_id=1, source_target_pairs={{0,4},{4,0},{1,5},{5,1},{2,6},{6,2},{3,7},{7,3},{8,12},{12,8},{9,1... | collective-permute-start | bytes 294920 | tf_op jit(solution)/shard_map/ppermute | solution.py:501
  236.8 25.4 %all-to-all-start.4 = ((bf16[16,64,128]{2,1,0:T(8,128)(2,1)}), bf16[16,64,128]{2,1,0:T(8,128)(2,1)S(1)}, u32[]{:S(2)}, u32[]{:S(2)}) async-start(bf16[16,64,128]{2,1,0:T(8,128)(2,1)} %bitcast.71), calls=%async_computation.4 | async-start | bytes 524288 | tf_op jit(solution)/shard_map/all_to_all | solution.py:766
  246.2 18.7 %collective-permute-start.15 = (f32[64,1536]{1,0:T(8,128)S(1)}, f32[64,1536]{1,0:T(8,128)}, u32[]{:S(2)}, u32[]{:S(2)}) collective-permute-start(f32[64,1536]{1,0:T(8,128)S(1)} %copy-done.11), channel_id=1, source_target_pairs={{0,1},{1,0},{2,3},{3,2},{4,5},{5,4},{6,7},{7,6},{8,9},{9,8},{10,11... | collective-permute-start | bytes 1179656 | tf_op jit(solution)/shard_map/ppermute | solution.py:501
  263.0 16.8 %collective-permute-start.13 = (bf16[2,64,1536]{2,1,0:T(8,128)(2,1)S(1)}, bf16[2,64,1536]{2,1,0:T(8,128)(2,1)S(1)}, u32[]{:S(2)}, u32[]{:S(2)}) collective-permute-start(bf16[2,64,1536]{2,1,0:T(8,128)(2,1)S(1)} %pad_maximum_fusion.14), channel_id=1, source_target_pairs={{0,4},{4,0},{1,5},{5,1},{2,6},{6,2},{3,7},{7,3},{8,12},{12,8},{9,1... | collective-permute-start | bytes 1179656 | tf_op jit(solution)/shard_map/ppermute | solution.py:501
  264.5 18.9 %collective-permute-start.12 = (bf16[2,2,64,1536]{3,2,0,1:T(8,128)(2,1)S(1)}, bf16[2,2,64,1536]{3,2,0,1:T(8,128)(2,1)S(1)}, u32[]{:S(2)}, u32[]{:S(2)}) collective-permute-start(bf16[2,2,64,1536]{3,2,0,1:T(8,128)(2,1)S(1)} %bitcast.378), channel_id=1, source_target_pairs={{0,1},{1,0},{2,3},{3,2},{4,5},{5,4},{6,7},{7,6},{8,9},{9,8},{10,11... | collective-permute-start | bytes 2359304 | tf_op jit(solution)/shard_map/ppermute | solution.py:501
  287.8 15.5 %collective-permute-start.14 = (bf16[2,64,1536]{2,1,0:T(8,128)(2,1)S(1)}, bf16[2,64,1536]{2,1,0:T(8,128)(2,1)S(1)}, u32[]{:S(2)}, u32[]{:S(2)}) collective-permute-start(bf16[2,64,1536]{2,1,0:T(8,128)(2,1)S(1)} %dynamic-slice_bitcast_fusion.6), channel_id=1, source_target_pairs={{0,2},{2,0},{1,3},{3,1},{4,6},{6,4},{5,7},{7,5},{8,10},{10,8},{9,1... | collective-permute-start | bytes 1179656 | tf_op jit(solution)/shard_map/ppermute | solution.py:501
  289.6 15.0 %collective-permute-start.16 = (bf16[2,96,1536]{2,1,0:T(8,128)(2,1)S(1)}, bf16[2,96,1536]{2,1,0:T(8,128)(2,1)S(1)}, u32[]{:S(2)}, u32[]{:S(2)}) collective-permute-start(bf16[2,96,1536]{2,1,0:T(8,128)(2,1)S(1)} %dynamic-slice_bitcast_fusion.2), channel_id=1, source_target_pairs={{0,4},{4,0},{1,5},{5,1},{2,6},{6,2},{3,7},{7,3},{8,12},{12,8},{9,1... | collective-permute-start | bytes 1769480 | tf_op jit(solution)/shard_map/ppermute | solution.py:501
  291.8 13.0 %collective-permute-start.17 = (bf16[2,2,64,1536]{3,2,0,1:T(8,128)(2,1)S(1)}, bf16[2,2,64,1536]{3,2,0,1:T(8,128)(2,1)S(1)}, u32[]{:S(2)}, u32[]{:S(2)}) collective-permute-start(bf16[2,2,64,1536]{3,2,0,1:T(8,128)(2,1)S(1)} %pad_maximum_fusion.10), channel_id=1, source_target_pairs={{0,2},{2,0},{1,3},{3,1},{4,6},{6,4},{5,7},{7,5},{8,10},{10,8},{9,1... | collective-permute-start | bytes 2359304 | tf_op jit(solution)/shard_map/ppermute | solution.py:501
  306.4 12.9 %collective-permute-start.20 = (bf16[64,1536]{1,0:T(8,128)(2,1)S(1)}, bf16[64,1536]{1,0:T(8,128)(2,1)}, u32[]{:S(2)}, u32[]{:S(2)}) collective-permute-start(bf16[64,1536]{1,0:T(8,128)(2,1)S(1)} %dynamic-slice_bitcast_fusion.8), channel_id=1, source_target_pairs={{0,4},{4,0},{1,5},{5,1},{2,6},{6,2},{3,7},{7,3},{8,12},{12,8},{9,1... | collective-permute-start | bytes 589832 | tf_op jit(solution)/shard_map/ppermute | solution.py:501
  307.7 13.3 %collective-permute-start.19 = (bf16[2,96,1536]{2,1,0:T(8,128)(2,1)S(1)}, bf16[2,96,1536]{2,1,0:T(8,128)(2,1)}, u32[]{:S(2)}, u32[]{:S(2)}) collective-permute-start(bf16[2,96,1536]{2,1,0:T(8,128)(2,1)S(1)} %dynamic-slice_bitcast_fusion.1), channel_id=1, source_target_pairs={{0,2},{2,0},{1,3},{3,1},{4,6},{6,4},{5,7},{7,5},{8,10},{10,8},{9,1... | collective-permute-start | bytes 1769480 | tf_op jit(solution)/shard_map/ppermute | solution.py:501
  326.3 52.2 %all-to-all-start.5 = ((bf16[16,112,512]{2,1,0:T(8,128)(2,1)}), bf16[16,112,512]{2,1,0:T(8,128)(2,1)S(1)}, u32[]{:S(2)}, u32[]{:S(2)}) async-start(bf16[16,112,512]{2,1,0:T(8,128)(2,1)} %get-tuple-element.168), calls=%async_computation.6 | async-start | bytes 3670016 | tf_op jit(solution)/shard_map/all_to_all | solution.py:793
  332.3 18.8 %collective-permute-start.22 = (bf16[2,2,64,1536]{3,2,0,1:T(8,128)(2,1)S(1)}, bf16[2,2,64,1536]{3,2,0,1:T(8,128)(2,1)S(1)}, u32[]{:S(2)}, u32[]{:S(2)}) collective-permute-start(bf16[2,2,64,1536]{3,2,0,1:T(8,128)(2,1)S(1)} %dynamic-slice_bitcast_fusion), channel_id=1, source_target_pairs={{0,1},{1,0},{2,3},{3,2},{4,5},{5,4},{6,7},{7,6},{8,9},{9,8},{10,11... | collective-permute-start | bytes 2359304 | tf_op jit(solution)/shard_map/ppermute | solution.py:501
  351.4 16.7 %collective-permute-start.23 = (bf16[2,64,1536]{2,1,0:T(8,128)(2,1)S(1)}, bf16[2,64,1536]{2,1,0:T(8,128)(2,1)S(1)}, u32[]{:S(2)}, u32[]{:S(2)}) collective-permute-start(bf16[2,64,1536]{2,1,0:T(8,128)(2,1)S(1)} %dynamic-slice_bitcast_fusion.5), channel_id=1, source_target_pairs={{0,4},{4,0},{1,5},{5,1},{2,6},{6,2},{3,7},{7,3},{8,12},{12,8},{9,1... | collective-permute-start | bytes 1179656 | tf_op jit(solution)/shard_map/ppermute | solution.py:501
  352.6 24.8 %collective-permute-start.27 = (f32[2,1536]{1,0:T(2,128)S(1)}, f32[2,1536]{1,0:T(2,128)S(1)}, u32[]{:S(2)}, u32[]{:S(2)}) collective-permute-start(f32[2,1536]{1,0:T(2,128)S(1)} %fusion.70), channel_id=1, source_target_pairs={{0,1},{1,0},{2,3},{3,2},{4,5},{5,4},{6,7},{7,6},{8,9},{9,8},{10,11... | collective-permute-start | bytes 36872 | tf_op jit(solution)/shard_map/ppermute | solution.py:501
  378.7 33.7 %collective-permute-start.30 = (bf16[64,1536]{1,0:T(8,128)(2,1)S(1)}, bf16[64,1536]{1,0:T(8,128)(2,1)S(1)}, u32[]{:S(2)}, u32[]{:S(2)}) collective-permute-start(bf16[64,1536]{1,0:T(8,128)(2,1)S(1)} %fusion.30), channel_id=1, source_target_pairs={{0,1},{1,17},{16,0},{17,16},{2,3},{3,19},{18,2},{19,18},{4,5},{5,2... | collective-permute-start | bytes 589832 | tf_op jit(solution)/shard_map/ppermute | solution.py:813
  379.0 33.4 %collective-permute-start.29 = (bf16[64,1536]{1,0:T(8,128)(2,1)S(1)}, bf16[64,1536]{1,0:T(8,128)(2,1)S(1)}, u32[]{:S(2)}, u32[]{:S(2)}) collective-permute-start(bf16[64,1536]{1,0:T(8,128)(2,1)S(1)} %fusion.30), channel_id=1, source_target_pairs={{0,0},{1,16},{16,1},{17,17},{2,2},{3,18},{18,3},{19,19},{4,4},{5,2... | collective-permute-start | bytes 589832 | tf_op jit(solution)/shard_map/ppermute | solution.py:812
  379.7 16.8 %collective-permute-start.31 = (f32[2,1536]{1,0:T(2,128)S(1)}, f32[2,1536]{1,0:T(2,128)S(1)}, u32[]{:S(2)}, u32[]{:S(2)}) collective-permute-start(f32[2,1536]{1,0:T(2,128)S(1)} %add.225), channel_id=1, source_target_pairs={{0,16},{16,0},{1,17},{17,1},{2,18},{18,2},{3,19},{19,3},{4,20},{20... | collective-permute-start | bytes 36872 | tf_op jit(solution)/shard_map/ppermute | solution.py:501
  383.7 28.8 %collective-permute-start.28 = (bf16[64,1536]{1,0:T(8,128)(2,1)S(1)}, bf16[64,1536]{1,0:T(8,128)(2,1)S(1)}, u32[]{:S(2)}, u32[]{:S(2)}) collective-permute-start(bf16[64,1536]{1,0:T(8,128)(2,1)S(1)} %add_convert_fusion), channel_id=1, source_target_pairs={{0,1},{1,0},{2,3},{3,2},{4,5},{5,4},{6,7},{7,6},{8,9},{9,8},{10,11... | collective-permute-start | bytes 589832 | tf_op jit(solution)/shard_map/ppermute | solution.py:501
  385.6 32.9 %all-to-all-start.6 = ((bf16[16,96,192]{1,2,0:T(8,128)(2,1)}), bf16[16,96,192]{1,2,0:T(8,128)(2,1)S(1)}, u32[]{:S(2)}, u32[]{:S(2)}) async-start(bf16[16,96,192]{1,2,0:T(8,128)(2,1)} %copy.143), calls=%async_computation.7 | async-start | bytes 1572864 | tf_op jit(solution)/shard_map/all_to_all | solution.py:818
  396.5 13.8 %collective-permute-start.32 = (f32[2,1536]{1,0:T(2,128)S(1)}, f32[2,1536]{1,0:T(2,128)S(1)}, u32[]{:S(2)}, u32[]{:S(2)}) collective-permute-start(f32[2,1536]{1,0:T(2,128)S(1)} %add.230), channel_id=1, source_target_pairs={{0,8},{8,0},{1,9},{9,1},{2,10},{10,2},{3,11},{11,3},{4,12},{12,4},... | collective-permute-start | bytes 36872 | tf_op jit(solution)/shard_map/ppermute | solution.py:501
  (50 other events, 305.2 us)
Sparse Core Ops, SparseCore 0:
  25.9 38.6 all-gather.2
  89.1 91.7 all-gather.4
  196.2 91.5 reduce-scatter.1
